TPU v7x, 32 devices: a whole 2x2x4 slice. The times are simulated.
32 devices in a mesh: dp: 8 (over z, y), seq: 4 (over x, core).
Axes of the slice: x: 2, y: 2, z: 4, core: 2. Of those that a mesh axis runs over, the one named last changes fastest.
Arguments:
- tokens: bfloat16 [32, 256, 768], P('dp', 'seq'), may hold values from -6 to 6
- pad_mask: int32 [32, 256], P('dp'), may hold values from 0 to 1, as said below
- counts: int32 [8], P('dp'), may hold values from 2 to 4, as said below
- attn_gain: bfloat16 [768], P('dp'), may hold values from 0.5 to 1.5
- attn_shift: bfloat16 [768], P('dp'), may hold values from -4 to 4
- qkv_weight: bfloat16 [768, 2304], P('dp'), may hold values from -0.21875 to 0.21875
- mix_weight: bfloat16 [768, 768], P('dp'), may hold values from -1.75 to 1.75
- mix_bias: bfloat16 [768], P('dp'), may hold values from -4 to 4
- moe_gain: bfloat16 [768], P('dp'), may hold values from 0.5 to 1.5
- moe_shift: bfloat16 [768], P('dp'), may hold values from -4 to 4
- router: bfloat16 [768, 32], P('dp'), may hold values from -0.109375 to 0.109375
- expert_in: bfloat16 [32, 768, 3072], P(('dp', 'seq')), may hold values from -2.5 to 2.5
- hidden_bias: bfloat16 [32, 3072], P(('dp', 'seq')), may hold values from -1.5 to 1.5
- expert_out: bfloat16 [32, 3072, 768], P(('dp', 'seq')), may hold values from -1.75 to 1.75
- output_bias: bfloat16 [32, 768], P(('dp', 'seq')), may hold values from -6 to 6
- cotangent: bfloat16 [32, 256, 768], P('dp', 'seq'), may hold values from -6 to 6
Outputs:
- block_out: bfloat16 [32, 256, 768], P('dp', 'seq')
- input_grad: bfloat16 [32, 256, 768], P('dp', 'seq')
- grad_attn_gain: float32 [768], P('dp')
- grad_attn_shift: float32 [768], P('dp')
- grad_qkv_weight: float32 [768, 2304], P('dp')
- grad_mix_weight: float32 [768, 768], P('dp')
- grad_mix_bias: float32 [768], P('dp')
- grad_moe_gain: float32 [768], P('dp')
- grad_moe_shift: float32 [768], P('dp')
- grad_router: float32 [768, 32], P('dp')
- grad_expert_in: float32 [32, 768, 3072], P(('dp', 'seq'))
- grad_hidden_bias: float32 [32, 3072], P(('dp', 'seq'))
- grad_expert_out: float32 [32, 3072, 768], P(('dp', 'seq'))
- grad_output_bias: float32 [32, 768], P(('dp', 'seq'))
Inputs may be any that keep to these rules, and one draw needn't show every extreme that they name: `pad_mask`: each image's mask is 1 on its first tokens, between 193 and 197 of them, and 0 after. Index d of dp holds counts[d] live images in its first image slots; its other slots are padding; some index is full.
All inputs are finite; a program needn't handle non-finite values.
Results may differ from a plain program's by a relative error of at most 0.018.
Values may be sent and summed in bfloat16 or wider, within the bound.
No kernel may reach another device: no remote copies, remote signals or barrier semaphores. Data moves between devices by JAX's collectives and lax.ppermute only.
A program may use at most 128 MiB of HBM per device.

v0:
```python
import math

import jax
import jax.numpy as jnp
from jax import lax
from jax.sharding import PartitionSpec as P

HEADS = 12
HEAD_DIM = 64


eps_norm = 1e-06


def joined(part, axis, combine):
    gathered = jax.tree.map(lambda a: lax.all_gather(a, axis), part)

    def take(source):
        return jax.tree.map(lambda a: lax.dynamic_index_in_dim(a, source, 0, False), gathered)

    return lax.fori_loop(
        1, lax.axis_size(axis), lambda source, state: combine(state, take(source)), take(0)
    )


def normalize(values, gain_row, shift_row):
    center = values - jnp.mean(values, axis=-1, keepdims=True)
    spread = jnp.mean(center * center, axis=-1, keepdims=True)
    inv_root = lax.rsqrt(spread + eps_norm)
    unit_rows = center * inv_root
    return (unit_rows * gain_row + shift_row, unit_rows, inv_root)


def normalize_back(grad_rows, unit_rows, inv_root, gain_row):
    scaled = grad_rows * gain_row
    inner_sum = scaled - jnp.mean(scaled, axis=-1, keepdims=True)
    inner_sum = inner_sum - unit_rows * jnp.mean(scaled * unit_rows, axis=-1, keepdims=True)
    return inner_sum * inv_root


def gelu_value(pre_act):
    return 0.5 * pre_act * (1.0 + lax.erf(pre_act * 2.0 ** (-0.5)))


def gelu_slope(pre_act):
    return 0.5 * (1.0 + lax.erf(pre_act * 2.0 ** (-0.5))) + pre_act * jnp.exp(
        -0.5 * pre_act * pre_act
    ) * (2.0 * math.pi) ** (-0.5)


def join_stats(first, second):
    peak = jnp.maximum(first[0], second[0])
    return (peak, first[1] * jnp.exp(first[0] - peak) + second[1] * jnp.exp(second[0] - peak))


def to_owners(partial_value):
    images, experts, features = partial_value.shape
    dp_lanes = lax.axis_size("dp")
    groups = lax.axis_size("seq")
    arrived = lax.all_to_all(partial_value, ("dp", "seq"), split_axis=1, concat_axis=0, tiled=True)
    summed = jnp.sum(arrived.reshape(dp_lanes, groups, images, features), axis=1)
    owned = summed.astype(jnp.bfloat16).reshape(dp_lanes * images, features)
    return owned


def from_owners(values, images):
    dp_lanes = lax.axis_size("dp")
    groups = lax.axis_size("seq")
    features = values.shape[1]
    copies = jnp.broadcast_to(
        values.reshape(dp_lanes, 1, images, 1, features), (dp_lanes, groups, images, 1, features)
    )
    arrived = lax.all_to_all(
        copies.reshape(dp_lanes * groups, images, 1, features),
        ("dp", "seq"),
        split_axis=0,
        concat_axis=2,
        tiled=True,
    )
    return arrived.reshape(images, dp_lanes * groups, features)


def forward(
    tokens, valid_rows, key_valid, weights, expert_in, hidden_bias, expert_out, output_bias
):
    gathered = (
        lax.all_gather(weights[0], "dp", axis=0, tiled=True),
        lax.all_gather(weights[1], "dp", axis=0, tiled=True),
        lax.all_gather(weights[2], "dp", axis=0, tiled=True),
        lax.all_gather(weights[3], "dp", axis=0, tiled=True),
        lax.all_gather(weights[4], "dp", axis=0, tiled=True),
        lax.all_gather(weights[5], "dp", axis=0, tiled=True),
        lax.all_gather(weights[6], "dp", axis=0, tiled=True),
        lax.all_gather(weights[7], "dp", axis=0, tiled=True),
    )
    attn_gain, attn_shift, qkv_weight, mix_weight, mix_bias, moe_gain, moe_shift, router = gathered
    images, shard_len, features = tokens.shape
    groups = lax.axis_size("seq")
    heads_here = HEADS // groups
    full_len = shard_len * groups
    experts = router.shape[1]
    scaling = HEAD_DIM ** (-0.5)
    resid_in = tokens.astype(jnp.float32)
    normed, unit_one, root_one = normalize(
        resid_in, attn_gain.astype(jnp.float32), attn_shift.astype(jnp.float32)
    )
    normed_low = normed.astype(jnp.bfloat16)
    project = jnp.dot(
        normed_low.reshape(-1, features), qkv_weight, preferred_element_type=jnp.float32
    ).astype(jnp.bfloat16)
    project = project.reshape(images, shard_len, 3, groups, heads_here * HEAD_DIM)
    by_head = lax.all_to_all(project, "seq", split_axis=3, concat_axis=1, tiled=True)
    by_head = by_head.reshape(images, full_len, 3, heads_here, HEAD_DIM)
    queries = by_head[:, :, 0]
    key_rows = by_head[:, :, 1]
    values = by_head[:, :, 2]
    scores = (
        jnp.einsum("iqhd,ikhd->ihqk", queries, key_rows, preferred_element_type=jnp.float32)
        * scaling
    )
    scores = jnp.where(key_valid[:, None, None, :] > 0, scores, -1000000000.0)
    peak = jnp.max(scores, axis=-1, keepdims=True)
    log_total = peak + jnp.log(jnp.sum(jnp.exp(scores - peak), axis=-1, keepdims=True))
    attn_probs = jnp.exp(scores - log_total)
    attended = jnp.einsum(
        "ihqk,ikhd->iqhd",
        attn_probs.astype(jnp.bfloat16),
        values,
        preferred_element_type=jnp.float32,
    )
    attended = attended.astype(jnp.bfloat16).reshape(images, full_len, heads_here * HEAD_DIM)
    merged = lax.all_to_all(attended, "seq", split_axis=1, concat_axis=2, tiled=True)
    attn_part = jnp.dot(
        merged.reshape(-1, features), mix_weight, preferred_element_type=jnp.float32
    )
    resid = resid_in + attn_part.reshape(images, shard_len, features) + mix_bias.astype(jnp.float32)
    mixed, unit_two, root_two = normalize(
        resid, moe_gain.astype(jnp.float32), moe_shift.astype(jnp.float32)
    )
    mixed_low = mixed.astype(jnp.bfloat16)
    logits = jnp.dot(mixed_low.reshape(-1, features), router, preferred_element_type=jnp.float32)
    logits = logits.reshape(images, shard_len, experts)
    masked = jnp.where(valid_rows[:, :, None] > 0, logits, -1000000000.0)
    local_peak = jnp.max(masked, axis=1)
    local_total = jnp.sum(jnp.exp(masked - local_peak[:, None, :]), axis=1)
    whole_peak, whole_total = joined((local_peak, local_total), "seq", join_stats)
    dispatch = jnp.exp(masked - whole_peak[:, None, :]) / whole_total[:, None, :]
    dispatch_low = dispatch.astype(jnp.bfloat16)
    partial_value = jnp.einsum(
        "ite,itd->ied", dispatch_low, mixed_low, preferred_element_type=jnp.float32
    )
    slot_in = to_owners(partial_value)
    pre_act = jnp.dot(slot_in, expert_in[0], preferred_element_type=jnp.float32) + hidden_bias[
        0
    ].astype(jnp.float32)
    hidden = gelu_value(pre_act).astype(jnp.bfloat16)
    slot_out = jnp.dot(hidden, expert_out[0], preferred_element_type=jnp.float32) + output_bias[
        0
    ].astype(jnp.float32)
    returned = from_owners(slot_out.astype(jnp.bfloat16), images)
    combine = jax.nn.softmax(logits, axis=-1)
    combine_low = combine.astype(jnp.bfloat16)
    moe_out = jnp.einsum("ite,ied->itd", combine_low, returned, preferred_element_type=jnp.float32)
    block_out = (resid + moe_out) * valid_rows[:, :, None]
    saved = (
        gathered,
        normed_low,
        unit_one,
        root_one,
        queries,
        key_rows,
        values,
        log_total,
        merged,
        unit_two,
        root_two,
        mixed_low,
        dispatch,
        dispatch_low,
        combine,
        combine_low,
        returned,
        slot_in,
        pre_act,
        hidden,
    )
    return (block_out, saved)


def body(
    tokens,
    pad_mask,
    counts,
    attn_gain,
    attn_shift,
    qkv_weight,
    mix_weight,
    mix_bias,
    moe_gain,
    moe_shift,
    router,
    expert_in,
    hidden_bias,
    expert_out,
    output_bias,
    cotangent,
):
    images, shard_len, features = tokens.shape
    groups = lax.axis_size("seq")
    heads_here = HEADS // groups
    full_len = shard_len * groups
    scaling = HEAD_DIM ** (-0.5)
    live_images = (jnp.arange(images, dtype=jnp.int32) < counts[0]).astype(jnp.float32)
    key_valid = pad_mask.astype(jnp.float32) * live_images[:, None]
    valid_rows = lax.dynamic_slice_in_dim(
        key_valid, lax.axis_index("seq") * shard_len, shard_len, 1
    )
    weights = (attn_gain, attn_shift, qkv_weight, mix_weight, mix_bias, moe_gain, moe_shift, router)
    block_out, saved = forward(
        tokens, valid_rows, key_valid, weights, expert_in, hidden_bias, expert_out, output_bias
    )
    repeat_out, saved = forward(
        tokens, valid_rows, key_valid, weights, expert_in, hidden_bias, expert_out, output_bias
    )
    (
        gathered,
        normed_low,
        unit_one,
        root_one,
        queries,
        key_rows,
        values,
        log_total,
        merged,
        unit_two,
        root_two,
        mixed_low,
        dispatch,
        dispatch_low,
        combine,
        combine_low,
        returned,
        slot_in,
        pre_act,
        hidden,
    ) = saved
    (
        full_gain_one,
        full_shift_one,
        full_qkv,
        full_mix,
        full_bias,
        full_gain_two,
        full_shift_two,
        full_router,
    ) = gathered
    experts = full_router.shape[1]
    grad_block = cotangent.astype(jnp.float32) * valid_rows[:, :, None]
    grad_combine = jnp.einsum(
        "itd,ied->ite", grad_block, returned, preferred_element_type=jnp.float32
    )
    slot_grad_part = jnp.einsum(
        "ite,itd->ied", combine_low, grad_block, preferred_element_type=jnp.float32
    )
    grad_logits = combine * (grad_combine - jnp.sum(combine * grad_combine, axis=-1, keepdims=True))
    grad_slot_out = to_owners(slot_grad_part)
    grad_output_bias = jnp.sum(grad_slot_out.astype(jnp.float32), axis=0)[None]
    grad_expert_out = jnp.dot(hidden.T, grad_slot_out, preferred_element_type=jnp.float32)[None]
    grad_hidden = jnp.dot(grad_slot_out, expert_out[0].T, preferred_element_type=jnp.float32)
    grad_pre = (grad_hidden * gelu_slope(pre_act)).astype(jnp.bfloat16)
    grad_hidden_bias = jnp.sum(grad_pre.astype(jnp.float32), axis=0)[None]
    grad_expert_in = jnp.dot(slot_in.T, grad_pre, preferred_element_type=jnp.float32)[None]
    grad_slot_in = jnp.dot(grad_pre, expert_in[0].T, preferred_element_type=jnp.float32).astype(
        jnp.bfloat16
    )
    grad_slots = from_owners(grad_slot_in, images)
    grad_dispatch = jnp.einsum(
        "itd,ied->ite", mixed_low, grad_slots, preferred_element_type=jnp.float32
    )
    grad_mixed = jnp.einsum(
        "ite,ied->itd", dispatch_low, grad_slots, preferred_element_type=jnp.float32
    )
    local_inner = jnp.sum(dispatch * grad_dispatch, axis=1)
    whole_inner = lax.psum(local_inner, "seq")
    grad_logits = grad_logits + dispatch * (grad_dispatch - whole_inner[:, None, :])
    logits_low = grad_logits.astype(jnp.bfloat16)
    grad_router = jnp.dot(
        mixed_low.reshape(-1, features).T,
        logits_low.reshape(-1, experts),
        preferred_element_type=jnp.float32,
    )
    grad_mixed = grad_mixed + jnp.einsum(
        "ite,de->itd", logits_low, full_router, preferred_element_type=jnp.float32
    )
    grad_moe_gain = jnp.sum(grad_mixed * unit_two, axis=(0, 1))
    grad_moe_shift = jnp.sum(grad_mixed, axis=(0, 1))
    grad_resid = grad_block + normalize_back(
        grad_mixed, unit_two, root_two, full_gain_two.astype(jnp.float32)
    )
    grad_mix_bias = jnp.sum(grad_resid, axis=(0, 1))
    grad_mix_weight = jnp.dot(
        merged.reshape(-1, features).T,
        grad_resid.reshape(-1, features),
        preferred_element_type=jnp.float32,
    )
    grad_merged = jnp.einsum(
        "itd,ed->ite", grad_resid, full_mix, preferred_element_type=jnp.float32
    ).astype(jnp.bfloat16)
    grad_heads = lax.all_to_all(grad_merged, "seq", split_axis=2, concat_axis=1, tiled=True)
    grad_heads = grad_heads.reshape(images, full_len, heads_here, HEAD_DIM)
    scores = (
        jnp.einsum("iqhd,ikhd->ihqk", queries, key_rows, preferred_element_type=jnp.float32)
        * scaling
    )
    scores = jnp.where(key_valid[:, None, None, :] > 0, scores, -1000000000.0)
    attn_probs = jnp.exp(scores - log_total)
    grad_probs = jnp.einsum(
        "iqhd,ikhd->ihqk", grad_heads, values, preferred_element_type=jnp.float32
    )
    inner_sum = jnp.sum(attn_probs * grad_probs, axis=-1, keepdims=True)
    grad_scores = (attn_probs * (grad_probs - inner_sum)).astype(jnp.bfloat16)
    grad_queries = (
        jnp.einsum("ihqk,ikhd->iqhd", grad_scores, key_rows, preferred_element_type=jnp.float32)
        * scaling
    )
    grad_keys = (
        jnp.einsum("ihqk,iqhd->ikhd", grad_scores, queries, preferred_element_type=jnp.float32)
        * scaling
    )
    grad_values = jnp.einsum(
        "ihqk,iqhd->ikhd",
        attn_probs.astype(jnp.bfloat16),
        grad_heads,
        preferred_element_type=jnp.float32,
    )
    grad_project = jnp.stack([grad_queries, grad_keys, grad_values], axis=2).astype(jnp.bfloat16)
    grad_project = grad_project.reshape(images, full_len, 3, 1, heads_here * HEAD_DIM)
    token_side = lax.all_to_all(
        grad_project, "seq", split_axis=1, concat_axis=3, tiled=True
    ).reshape(-1, 3 * features)
    grad_qkv_weight = jnp.dot(
        normed_low.reshape(-1, features).T, token_side, preferred_element_type=jnp.float32
    )
    grad_normed = jnp.dot(token_side, full_qkv.T, preferred_element_type=jnp.float32).reshape(
        images, shard_len, features
    )
    grad_attn_gain = jnp.sum(grad_normed * unit_one, axis=(0, 1))
    grad_attn_shift = jnp.sum(grad_normed, axis=(0, 1))
    input_grad = grad_resid + normalize_back(
        grad_normed, unit_one, root_one, full_gain_one.astype(jnp.float32)
    )
    weight_grads = (
        grad_attn_gain,
        grad_attn_shift,
        grad_qkv_weight,
        grad_mix_weight,
        grad_mix_bias,
        grad_moe_gain,
        grad_moe_shift,
        grad_router,
    )
    shares = (
        lax.psum_scatter(weight_grads[0], "dp", scatter_dimension=0, tiled=True),
        lax.psum_scatter(weight_grads[1], "dp", scatter_dimension=0, tiled=True),
        lax.psum_scatter(weight_grads[2], "dp", scatter_dimension=0, tiled=True),
        lax.psum_scatter(weight_grads[3], "dp", scatter_dimension=0, tiled=True),
        lax.psum_scatter(weight_grads[4], "dp", scatter_dimension=0, tiled=True),
        lax.psum_scatter(weight_grads[5], "dp", scatter_dimension=0, tiled=True),
        lax.psum_scatter(weight_grads[6], "dp", scatter_dimension=0, tiled=True),
        lax.psum_scatter(weight_grads[7], "dp", scatter_dimension=0, tiled=True),
    )
    shares = lax.psum(
        (shares[0], shares[1], shares[2], shares[3], shares[4], shares[5], shares[6], shares[7]),
        "seq",
    )
    return (
        block_out.astype(jnp.bfloat16),
        input_grad.astype(jnp.bfloat16),
        shares[0],
        shares[1],
        shares[2],
        shares[3],
        shares[4],
        shares[5],
        shares[6],
        shares[7],
        grad_expert_in,
        grad_hidden_bias,
        grad_expert_out,
        grad_output_bias,
    )


def solution(mesh):
    return jax.shard_map(
        body,
        mesh=mesh,
        in_specs=(
            P("dp", "seq", None),
            P("dp", None),
            P("dp"),
            P("dp"),
            P("dp"),
            P("dp", None),
            P("dp", None),
            P("dp"),
            P("dp"),
            P("dp"),
            P("dp", None),
            P(("dp", "seq"), None, None),
            P(("dp", "seq"), None),
            P(("dp", "seq"), None, None),
            P(("dp", "seq"), None),
            P("dp", "seq", None),
        ),
        out_specs=(
            P("dp", "seq", None),
            P("dp", "seq", None),
            P("dp"),
            P("dp"),
            P("dp", None),
            P("dp", None),
            P("dp"),
            P("dp"),
            P("dp"),
            P("dp", None),
            P(("dp", "seq"), None, None),
            P(("dp", "seq"), None),
            P(("dp", "seq"), None, None),
            P(("dp", "seq"), None),
        ),
        check_vma=False,
    )
```

profile of v0, /device:TPU:1, one launch (start us, length us, event | category | flops | bytes accessed | tf_op | source)
XLA Modules:
  0.0 599.3 jit_solution(9825696099636021225)
XLA Ops:
  14.1 31.4 %all-reduce.13 = (bf16[768]{0:T(1024)(128)(2,1)S(1)}, bf16[768]{0:T(1024)(128)(2,1)S(1)}, bf16[768]{0:T(1024)(128)(2,1)S(1)}, bf16[768]{0:T(1024)(128)(2,1)}, bf16[768]{0:T(1024)(128)(2,1)S(1)}) all-reduce(bf16[768]{0:T(1024)(128)(2,1)S(1)} %dynamic-update-slice.1, ...), channel_id=1, replica_groups=mesh['dp'=8,'seq'=4] {'dp'}, use_global_device_ids=true, to_apply=%add.1 | all-reduce | flops 3840 | bytes 15360
  49.8 27.2 %all-gather.8.cloned.1.call-done = bf16[768,2304]{1,0:T(8,128)(2,1)} async-done(((bf16[96,2304]{1,0:T(8,128)(2,1)}), bf16[768,2304]{1,0:T(8,128)(2,1)}) %all-gather.8.cloned.1.call-update) | async-done | bytes 3538960 | tf_op jit(solution)/shard_map/all_gather | solution.py:89
  83.1 5.2 all-to-all-start
  89.8 17.7 %all-to-all-done = bf16[4,64,3,4,192]{4,1,2,0,3:T(8,128)(2,1)S(1)} async-done(((bf16[4,64,3,4,192]{4,1,2,0,3:T(8,128)(2,1)}), bf16[4,64,3,4,192]{4,1,2,0,3:T(8,128)(2,1)S(1)}, u32[]{:S(2)}, u32[]{:S(2)}) %all-to-all-start) | async-done | bytes 1179680 | tf_op jit(solution)/shard_map/all_to_all | solution.py:112
  122.2 5.0 all-to-all-start.1
  127.9 24.3 %all-gather.2 = bf16[8,96,32]{1,2,0:T(8,128)(2,1)S(1)} all-gather(bf16[1,96,32]{1,2,0:T(8,128)(2,1)} %bitcast.208), channel_id=1, replica_groups=mesh['dp'=8,'seq'=4] {'dp'}, dimensions={0}, use_global_device_ids=true | all-gather | bytes 55296 | tf_op jit(solution)/shard_map/all_gather | solution.py:94
  166.6 11.4 %all-gather.4 = f32[4,4,32]{2,1,0:T(4,128)S(1)} all-gather(f32[1,4,32]{2,1,0:T(4,128)S(1)} %bitcast.209), channel_id=3, replica_groups=mesh['dp'=8,'seq'=4] {'seq'}, dimensions={0}, use_global_device_ids=true | all-gather | bytes 2560 | tf_op jit(solution)/shard_map/all_gather | solution.py:16
  178.6 5.3 all-gather.3
  196.5 7.9 %all-to-all-done.4 = f32[4,32,768]{2,0,1:T(4,128)} async-done(((f32[4,32,768]{2,0,1:T(4,128)}), f32[4,32,768]{2,0,1:T(4,128)}, u32[]{:S(2)}, u32[]{:S(2)}) %all-to-all-start.4) | async-done | bytes 393248 | tf_op jit(solution)/shard_map/all_to_all | solution.py:60
  204.4 4.2 all-to-all-start.2
  213.7 7.3 %all-to-all-done.2 = f32[4,32,768]{2,0,1:T(4,128)} async-done(((f32[4,32,768]{2,0,1:T(4,128)}), f32[4,32,768]{2,0,1:T(4,128)}, u32[]{:S(2)}, u32[]{:S(2)}) %all-to-all-start.2) | async-done | bytes 393248 | tf_op jit(solution)/shard_map/all_to_all | solution.py:60
  228.3 4.4 convert_reduce_fusion.1
  233.4 4.5 fusion.39
  245.3 4.0 fusion.36
  263.5 5.9 psum.63
  294.3 12.9 %all_to_all.140 = bf16[4,2,24576]{2,1,0:T(2,128)(2,1)} all-to-all(bf16[4,2,24576]{2,1,0:T(2,128)(2,1)} %reshape.325), channel_id=1, replica_groups=mesh['dp'=8,'seq'=4] {'seq'}, dimensions={0} | all-to-all | bytes 786432 | tf_op jit(solution)/shard_map/all_to_all | solution.py:309
  329.6 22.6 %all_to_all.141 = bf16[4,256,3,1,192]{4,0,3,2,1:T(4,128)(2,1)S(1)} all-to-all(bf16[4,256,3,1,192]{4,0,3,2,1:T(4,128)(2,1)S(1)} %pad_maximum_fusion), channel_id=1, replica_groups=mesh['dp'=8,'seq'=4] {'seq'}, dimensions={1} | all-to-all | bytes 2359296 | tf_op jit(solution)/shard_map/all_to_all | solution.py:338
  355.9 5.3 fusion.105
  362.8 5.2 convolution_bitcast_fusion.1
  368.0 5.2 convolution_bitcast_fusion
  382.2 25.1 %reduce-scatter.8.cloned.1.call-done = f32[96,768]{1,0:T(8,128)} async-done(((f32[768,768]{1,0:T(8,128)}), f32[96,768]{1,0:T(8,128)}) %reduce-scatter.8.cloned.1.call-update) | async-done | bytes 294928 | tf_op jit(solution)/shard_map/reduce_scatter | solution.py:366
  407.3 132.1 %reduce-scatter.6.cloned.1.call-done = f32[96,2304]{1,0:T(8,128)} async-done(((f32[768,2304]{1,0:T(8,128)}), f32[96,2304]{1,0:T(8,128)}) %reduce-scatter.6.cloned.1.call-update) | async-done | bytes 884752 | tf_op jit(solution)/shard_map/reduce_scatter | solution.py:365
  539.5 29.1 %all-reduce.10 = (f32[768]{0:T(1024)S(1)}, f32[768]{0:T(1024)S(1)}, f32[768]{0:T(1024)S(1)}, f32[768]{0:T(1024)S(1)}, f32[768]{0:T(1024)S(1)}) all-reduce(f32[768]{0:T(1024)S(1)} %get-tuple-element.163, f32[768]{0:T(1024)S(1)} %get-tuple-element.168, f32[768]{0:T(1024)S(1)} %copy-done.37, ...), channel_id=4, replica_groups=mesh['dp'=8,'seq'=4] {'dp'}, use_global_device_ids=true, to_apply=%region_23.24.clone | all-reduce | flops 3840 | bytes 30720
  569.0 18.1 %all-reduce.11 = (f32[96]{0:T(128)}, f32[96]{0:T(128)}, f32[96]{0:T(128)}, f32[96]{0:T(128)}, f32[96]{0:T(128)}, /*index=5*/f32[96,32]{0,1:T(8,128)}) all-reduce(f32[96]{0:T(128)S(1)} %dynamic-slice.6, f32[96]{0:T(128)S(1)} %dynamic-slice.8, f32[96]{0:T(128)S(1)} %dynamic-slice.10, ...), channel_id=1, replica_groups=mesh['dp'=8,'seq'=4] {'seq'}, use_global_device_ids=true, to_apply=%region_24.25 | all-reduce | flops 3552 | bytes 28416 | tf_op jit(solution)/shard_map/psum | solution.py:372
  (215 shorter events, 162.8 us)
Async XLA Ops:
  7.2 69.8 %all-gather.8.cloned.1.call-start = ((), (), s32[]{:S(2)}) async-start(), calls=%async_computation.11 | async-start | bytes 3981312 | tf_op jit(solution)/shard_map/all_gather | solution.py:89
  49.8 27.2 %copy-start.14 = (bf16[4,64,768]{2,1,0:T(8,128)(2,1)}, bf16[4,64,768]{2,1,0:T(8,128)(2,1)S(1)}, u32[]{:S(2)}) copy-start(bf16[4,64,768]{2,1,0:T(8,128)(2,1)S(1)} %fusion.54) | copy-start | bytes 1179652
  81.7 8.0 %copy-start.39 = (s32[4,256]{1,0:T(4,128)S(1)}, s32[4,256]{1,0:T(4,128)}, u32[]{:S(2)}) copy-start(s32[4,256]{1,0:T(4,128)} %param.19) | copy-start | bytes 12292
  83.1 24.4 %all-to-all-start = ((bf16[4,64,3,4,192]{4,1,2,0,3:T(8,128)(2,1)}), bf16[4,64,3,4,192]{4,1,2,0,3:T(8,128)(2,1)S(1)}, u32[]{:S(2)}, u32[]{:S(2)}) async-start(bf16[4,64,3,4,192]{4,1,2,0,3:T(8,128)(2,1)} %copy.137), calls=%async_computation | async-start | bytes 3145728 | tf_op jit(solution)/shard_map/all_to_all | solution.py:112
  88.3 71.4 %all-gather.10.cloned.1.call-start = ((), (), s32[]{:S(2)}) async-start(), calls=%async_computation.12 | async-start | bytes 1327104 | tf_op jit(solution)/shard_map/all_gather | solution.py:90
  89.8 27.0 %copy-start.31 = (pred[4,256]{1,0:T(4,128)(4,1)}, pred[4,256]{1,0:T(4,128)(4,1)S(1)}, u32[]{:S(2)}) copy-start(pred[4,256]{1,0:T(4,128)(4,1)S(1)} %get-tuple-element.205) | copy-start | bytes 3076
  120.0 39.6 %copy-start.5 = (bf16[4,64,768]{2,1,0:T(8,128)(2,1)S(1)}, bf16[4,64,768]{2,1,0:T(8,128)(2,1)}, u32[]{:S(2)}) copy-start(bf16[4,64,768]{2,1,0:T(8,128)(2,1)} %param.18) | copy-start | bytes 1179652
  122.2 32.9 %all-to-all-start.1 = ((bf16[4,256,192]{2,0,1:T(4,128)(2,1)}), bf16[4,256,192]{2,0,1:T(4,128)(2,1)}, u32[]{:S(2)}, u32[]{:S(2)}) async-start(bf16[4,256,192]{2,0,1:T(4,128)(2,1)} %copy.143), calls=%async_computation.1 | async-start | bytes 1048576 | tf_op jit(solution)/shard_map/all_to_all | solution.py:132
  188.6 15.8 %all-to-all-start.4 = ((f32[4,32,768]{2,0,1:T(4,128)}), f32[4,32,768]{2,0,1:T(4,128)}, u32[]{:S(2)}, u32[]{:S(2)}) async-start(f32[4,32,768]{2,0,1:T(4,128)} %copy.151), calls=%async_computation.4 | async-start | bytes 786432 | tf_op jit(solution)/shard_map/all_to_all | solution.py:60
  204.4 16.7 %all-to-all-start.2 = ((f32[4,32,768]{2,0,1:T(4,128)}), f32[4,32,768]{2,0,1:T(4,128)}, u32[]{:S(2)}, u32[]{:S(2)}) async-start(f32[4,32,768]{2,0,1:T(4,128)} %copy.147), calls=%async_computation.2 | async-start | bytes 786432 | tf_op jit(solution)/shard_map/all_to_all | solution.py:60
  240.8 13.3 %all-to-all-start.5 = ((bf16[32,4,1,768]{3,1,2,0:T(4,128)(2,1)}), bf16[32,4,1,768]{3,1,2,0:T(4,128)(2,1)}, u32[]{:S(2)}, u32[]{:S(2)}) async-start(bf16[32,4,1,768]{3,1,2,0:T(4,128)(2,1)} %bitcast.202), calls=%async_computation.5 | async-start | bytes 393216 | tf_op jit(solution)/shard_map/all_to_all | solution.py:73
  255.6 13.8 %all-to-all-start.3 = ((bf16[32,4,1,768]{3,1,2,0:T(4,128)(2,1)}), bf16[32,4,1,768]{3,1,2,0:T(4,128)(2,1)}, u32[]{:S(2)}, u32[]{:S(2)}) async-start(bf16[32,4,1,768]{3,1,2,0:T(4,128)(2,1)} %bitcast.201), calls=%async_computation.3 | async-start | bytes 393216 | tf_op jit(solution)/shard_map/all_to_all | solution.py:73
  258.6 116.7 %reduce-scatter.10.cloned.1.call-start = ((), (), s32[]{:S(2)}) async-start(), calls=%async_computation.15 | async-start | bytes 442368
  273.8 133.5 %reduce-scatter.8.cloned.1.call-start = ((), (), s32[]{:S(2)}) async-start(), calls=%async_computation.14 | async-start | bytes 2654208 | tf_op jit(solution)/shard_map/reduce_scatter | solution.py:366
  286.9 252.6 %reduce-scatter.6.cloned.1.call-start = ((), (), s32[]{:S(2)}) async-start(), calls=%async_computation.13 | async-start | bytes 7962624 | tf_op jit(solution)/shard_map/reduce_scatter | solution.py:365
  291.8 23.0 %copy-start.21 = (f32[4,3,256]{2,1,0:T(4,128)S(1)}, f32[4,3,256]{2,1,0:T(4,128)}, u32[]{:S(2)}) copy-start(f32[4,3,256]{2,1,0:T(4,128)} %copy-done.20) | copy-start | bytes 36868
  361.3 226.9 %all-reduce.16.cloned.1.call-start = ((), (), s32[]{:S(2)}) async-start(), calls=%async_computation.16 | async-start | bytes 2359296 | tf_op jit(solution)/shard_map/psum | solution.py:372
  368.0 5.2 copy-start.1
  368.0 5.2 copy-start.28
  368.0 5.2 copy-start.29
  378.4 161.1 %copy-start.35 = (f32[768]{0:T(1024)S(1)}, f32[768]{0:T(1024)}, u32[]{:S(2)}) copy-start(f32[768]{0:T(1024)} %get-tuple-element.161) | copy-start | bytes 9220
  378.4 161.1 %copy-start.36 = (f32[768]{0:T(1024)S(1)}, f32[768]{0:T(1024)}, u32[]{:S(2)}) copy-start(f32[768]{0:T(1024)} %get-tuple-element.167) | copy-start | bytes 9220
  378.4 161.1 %copy-start.37 = (f32[768]{0:T(1024)S(1)}, f32[768]{0:T(1024)}, u32[]{:S(2)}) copy-start(f32[768]{0:T(1024)} %get-tuple-element.201) | copy-start | bytes 9220
  378.4 208.7 %copy-start.4 = (f32[4,64,768]{2,1,0:T(8,128)S(1)}, f32[4,64,768]{2,1,0:T(8,128)}, u32[]{:S(2)}) copy-start(f32[4,64,768]{2,1,0:T(8,128)} %copy-done.3) | copy-start | bytes 2359300
  (28 other events, 65.6 us)
Sparse Core Ops, SparseCore 0:
  10.2 66.7 all-gather.7
  91.3 38.2 all-gather.9
  274.0 60.8 reduce-scatter.9
  338.2 69.0 reduce-scatter.7
  410.8 128.5 reduce-scatter.5
  542.0 37.3 all-reduce.15
where the time goes:
time: 611 us; the launch traced here: 599 us
  waiting for transfers between devices  222 us (36%)
  blocking collectives  161 us (26%)
  matrix products  78.8 us (13%)
  local copies, waits for them, and re-layouts  73.1 us (12%)
  starting transfers between devices  25.1 us (4%)
  other arithmetic  21.7 us (4%)
  between operations  17.1 us (3%)
    reduce_scatter x1, waiting for transfers between devices, body(): lax.psum_scatter(weight_grads[2], 'dp', scatter_dimension=0, tiled=True)  132 us
    unnamed x2, blocking collectives  60.5 us
    all_gather x1, waiting for transfers between devices, forward(): lax.all_gather(weights[2], 'dp', axis=0, tiled=True)  27.2 us
    unnamed x103, local copies, waits for them, and re-layouts  25.5 us
    reduce_scatter x1, waiting for transfers between devices, body(): lax.psum_scatter(weight_grads[3], 'dp', scatter_dimension=0, tiled=True)  25.1 us
    all_gather x1, blocking collectives, forward(): lax.all_gather(weights[7], 'dp', axis=0, tiled=True)  24.3 us
    all_to_all x1, blocking collectives, body(): lax.all_to_all(grad_project, 'seq', split_axis=1, concat_axis=3, tiled=True)  22.6 us
    psum x1, blocking collectives, body(): lax.psum((shares[0], shares[1], shares[2], shares[3], shares[4], shares[5...  18.1 us
  transfers between devices with their start and end apart: 12, of which 7 were waited for; matrix products, arithmetic and copies ran while one was open for 20% of the time, Pallas kernels for 0%

commit v1 on v0

v1 whole, which is shorter than its diff:
```python
import math

import jax
import jax.numpy as jnp
from jax import lax
from jax.experimental import pallas as pl
from jax.experimental.pallas import tpu as pltpu
from jax.sharding import PartitionSpec as P

HEADS = 12
HEAD_DIM = 64
EPS = 1e-06
NEG = -1000000000.0
BF16 = jnp.bfloat16
F32 = jnp.float32
ALL_VMEM = 62.6
FOLD = 112
ROWS = 208
NT = (((1,), (1,)), ((), ()))
TN = (((0,), (0,)), ((), ()))


def mm(a, b):
    return jnp.dot(a, b, preferred_element_type=F32)


def mm_nt(a, b):
    return lax.dot_general(a, b, NT, preferred_element_type=F32)


def mm_tn(a, b):
    return lax.dot_general(a, b, TN, preferred_element_type=F32)


def unit(values):
    center = values - jnp.mean(values, axis=-1, keepdims=True)
    spread = jnp.mean(center * center, axis=-1, keepdims=True)
    root = lax.rsqrt(spread + EPS)
    return center * root, root


def unit_back(scaled, rows, root):
    inner = jnp.mean(scaled * rows, axis=-1, keepdims=True)
    return root * (scaled - jnp.mean(scaled, axis=-1, keepdims=True) - rows * inner)


def lane_mask(index, width):
    lane = lax.broadcasted_iota(jnp.int32, (1, width), 1)
    return (lane >= index * HEAD_DIM) & (lane < (index + 1) * HEAD_DIM)


def image_length(mask_ref, counts_ref, image):
    which = lax.broadcasted_iota(jnp.int32, mask_ref.shape, 0)
    real = jnp.where(which == image, mask_ref[...], 0)
    total = jnp.sum(jnp.sum(real, axis=1, keepdims=True), axis=0, keepdims=True)
    return jnp.where(image < counts_ref[0], total, 0)


def kernel_call(
    kernel, ins, outs, scratch=(), limit=48, smem=(), hbm_in=(), hbm_out=(), aliases=None, flops=1
):
    kw = {
        "input_output_aliases": aliases or {},
        "cost_estimate": pl.CostEstimate(flops=int(flops), bytes_accessed=0, transcendentals=0),
    }
    n_in, n_out, n_own = len(ins), len(outs), len(scratch)
    n_staged = len(hbm_in) + len(hbm_out)

    def wrapped(*refs):
        in_refs = list(refs[:n_in])
        out_refs = list(refs[n_in : n_in + n_out])
        own = refs[n_in + n_out : n_in + n_out + n_own]
        stages = refs[n_in + n_out + n_own :]
        reads, writes = [], {}
        for j, i in enumerate(hbm_in):
            reads.append(pltpu.make_async_copy(in_refs[i], stages[j], stages[-1].at[j]))
            in_refs[i] = stages[j]
        for j, i in enumerate(hbm_out, len(hbm_in)):
            writes[i] = pltpu.make_async_copy(stages[j], out_refs[i], stages[-1].at[j])
            out_refs[i] = stages[j]
        for copy in reads:
            copy.start()
        for copy in reads:
            copy.wait()
        kernel(*in_refs, *out_refs, *own)
        for copy in writes.values():
            copy.start()
        for copy in writes.values():
            copy.wait()

    def spec(i, staged):
        if i in staged:
            return pl.BlockSpec(memory_space=pltpu.HBM)
        return pl.BlockSpec(memory_space=pltpu.VMEM)

    in_specs = [
        pl.BlockSpec(memory_space=pltpu.SMEM) if i in smem else spec(i, hbm_in)
        for i in range(n_in)
    ]
    scratch = list(scratch)
    scratch += [pltpu.VMEM(ins[i].shape, ins[i].dtype) for i in hbm_in]
    scratch += [pltpu.VMEM(*outs[i]) for i in hbm_out]
    if n_staged:
        scratch.append(pltpu.SemaphoreType.DMA((n_staged,)))
    call = pl.pallas_call(
        wrapped,
        in_specs=in_specs,
        out_specs=[spec(i, hbm_out) for i in range(n_out)],
        out_shape=[jax.ShapeDtypeStruct(shape, kind) for shape, kind in outs],
        scratch_shapes=scratch,
        compiler_params=pltpu.CompilerParams(vmem_limit_bytes=int(limit * 2**20)),
        **kw,
    )
    return list(call(*ins))


def place(full, refs, dp):
    if len(refs) == 1:
        full[...] = refs[0][...]
        return
    part = refs[0].shape[0]
    half = part // 2

    def put(ref, rows, step, lo):
        at = pl.multiple_of((dp ^ step) * part + lo, half)
        full[pl.ds(at, rows.stop - rows.start), :] = ref[rows, :]

    whole, rest = slice(0, part), slice(part, part + half)
    for ref, step in zip(refs, (0, 1, 2, 4, 5, 6)):
        put(ref, whole, step, 0)
    put(refs[4], rest, 3, 0)
    put(refs[5], rest, 3, half)
    put(refs[6], slice(0, half), 7, 0)
    put(refs[7], slice(0, half), 7, half)


def forward_blocks(beside, across, far, y_ref, z_ref):
    part = far.shape[0]
    half = part // 2
    y_ref[:part, :] = far[...]
    y_ref[part:, :] = across[:half, :]
    z_ref[:part, :] = far[...]
    z_ref[part:, :] = beside[half:, :]


def forward_last(y_ref, z_ref, first_ref, second_ref):
    half = first_ref.shape[0]
    first_ref[...] = z_ref[:half, :]
    second_ref[...] = y_ref[half : 2 * half, :]


def head_masks(width, heads_here):
    return [lane_mask(h, width) for h in range(heads_here)]


def pack_inputs(groups, here, half, misc_w, experts):
    def kernel(*refs):
        qkv_ref, router_ref = refs[:2]
        vectors = refs[2:7]
        mix_ref, cot_ref, piece_ref = refs[7:10]
        cot_refs = refs[10 : 10 + groups]
        turn = refs[-1]
        seq = lax.axis_index("seq")
        features = qkv_ref.shape[1] // 3
        part = qkv_ref.shape[0]
        for g in range(groups):

            @pl.when(seq == g)
            def _():
                for j in range(3):
                    lo = j * features + g * here
                    piece_ref[:, j * here : (j + 1) * here] = qkv_ref[:, lo : lo + here]

        turn[...] = jnp.zeros_like(turn)
        turn[:experts, :part] = router_ref[...].astype(F32)
        for j in range(5):
            turn[experts + j : experts + j + 1, :part] = vectors[j][...].astype(F32)
        lo = 3 * here + misc_w
        piece_ref[:, 3 * here : lo] = turn[...].T[:part].astype(BF16)
        piece_ref[:, lo:] = mix_ref[:, pl.ds(pl.multiple_of((seq & 1) * half, 128), half)]
        for r in range(groups):
            cot_refs[r][...] = cot_ref[pl.ds(seq ^ r, 1)][0]

    return kernel


def normalize_tokens(groups):
    def kernel(*refs):
        tok_refs = refs[:groups]
        normed_ref, unit_ref, mine_ref, tok = refs[groups:]
        seq = lax.axis_index("seq")
        images, shard, _ = tok_refs[0].shape
        for r in range(groups):
            rows = pl.ds(pl.multiple_of((seq ^ r) * shard, shard), shard)
            tok[:, rows, :] = tok_refs[r][...]
        mine_ref[...] = tok[pl.ds(seq, 1), :ROWS, :][0]
        for i in range(images):
            normed, _ = unit(tok[i, :ROWS, :].astype(F32))
            normed_ref[i] = normed
            unit_ref[i] = normed.astype(BF16)

    return kernel


def attend_forward(groups, pieces, here, wide, misc_w, experts):
    heads_here = HEADS // groups

    def kernel(*refs):
        normed_ref, mask_ref, counts_ref = refs[:3]
        w_refs = refs[3 : 3 + pieces]
        sent_refs = refs[3 + pieces : 3 + pieces + groups]
        rest = refs[3 + pieces + groups :]
        (half_ref, probs_ref, xa_ref, qkv_ref, wpad_ref, rows_ref, router_ref, dense, heads) = rest
        seq = lax.axis_index("seq")
        images, _, features = normed_ref.shape
        place(dense, w_refs, lax.axis_index("dp"))
        wpad_ref[...] = jnp.zeros_like(wpad_ref)
        for j in range(3):
            wpad_ref[:, j * wide : j * wide + here] = dense[:, j * here : (j + 1) * here]
        half_ref[...] = dense[:, 3 * here + misc_w :]
        misc = dense[:, 3 * here : 3 * here + misc_w]
        router_ref[...] = misc[:, :experts]
        rows_ref[...] = misc.astype(F32).T[experts : experts + 8]
        xa_ref[...] = (normed_ref[...] * rows_ref[0:1][None] + rows_ref[1:2][None]).astype(BF16)
        flat = xa_ref[...].reshape(images * ROWS, features)
        qkv_ref[:, :ROWS, :] = (
            mm(flat, wpad_ref[...]).astype(BF16).reshape(images, ROWS, 3 * wide)
        )
        keys = qkv_ref.shape[1]
        qkv_ref[:, ROWS:, :] = jnp.zeros((images, keys - ROWS, 3 * wide), BF16)
        place_of_key = lax.broadcasted_iota(jnp.int32, (1, keys), 1)
        for i in range(images):
            valid = place_of_key < image_length(mask_ref, counts_ref, i)
            q, k, v = head_stacks(qkv_ref, i, wide, heads_here)
            scores = mm_nt(q, k) * HEAD_DIM ** (-0.5)
            for h in range(heads_here):
                lanes = slice(h * keys, (h + 1) * keys)
                masked = jnp.where(valid, scores[:, lanes], NEG)
                top = jnp.exp(masked - jnp.max(masked, axis=-1, keepdims=True))
                total = jnp.sum(top, axis=-1, keepdims=True)
                probs_ref[i, :, lanes] = (top / total).astype(BF16)
            heads[i] = mm(probs_ref[i], v)[:, :here].astype(BF16)
        for r in range(groups):
            fold(sent_refs[r], heads[pl.ds(seq ^ r, 1)][0])

    return kernel


def head_stacks(qkv_ref, image, wide, heads_here):
    masks = head_masks(wide, heads_here)
    stacks = []
    for j in (1, 2):
        rows = qkv_ref[image, :, j * wide : (j + 1) * wide]
        stacks.append(jnp.concatenate([jnp.where(m, rows, jnp.zeros_like(rows)) for m in masks]))
    return qkv_ref[image, :ROWS, :wide], stacks[0], stacks[1]


def fold(ref, rows):
    top, width = ref.shape[0], rows.shape[1]
    ref[:, :width] = rows[:top]
    ref[: rows.shape[0] - top, width:] = rows[top:]


def unfold(ref, part, count):
    width = ref.shape[1] // 2
    if part == 0:
        return ref[:, :width]
    return ref[: count - ref.shape[0], width:]


def head_rows(seq, r, here):
    return pl.ds(pl.multiple_of((seq ^ r) * here, here), here)


def route_forward(groups, here, half):
    def kernel(*refs):
        sent_refs = refs[:groups]
        cot_refs = refs[groups : 2 * groups]
        mine_ref, rows_ref, router_ref, mask_ref, counts_ref = refs[2 * groups : 2 * groups + 5]
        half_refs = refs[2 * groups + 5 : -8]
        slots_ref, resid_ref, mixed_ref, logits_ref, mix_ref, grad_ref, heads_ref, cot = refs[-8:]
        seq = lax.axis_index("seq")
        for j in range(2):
            lanes = pl.ds(pl.multiple_of(((seq & 1) ^ j) * half, 128), half)
            mix_ref[:, lanes] = half_refs[j][...]
        for r in range(groups):
            heads_ref[r, :FOLD] = unfold(sent_refs[r], 0, ROWS)
            heads_ref[r, FOLD:] = unfold(sent_refs[r], 1, ROWS)
            shard = cot_refs[r].shape[0]
            cot[pl.ds(pl.multiple_of((seq ^ r) * shard, shard), shard), :] = cot_refs[r][...]
        resid = mine_ref[...].astype(F32) + rows_ref[2:3]
        for r in range(groups):
            resid = resid + mm(heads_ref[r], mix_ref[head_rows(seq, r, here), :])
        resid_ref[...] = resid
        normed, _ = unit(resid)
        mixed = (normed * rows_ref[3:4] + rows_ref[4:5]).astype(BF16)
        mixed_ref[...] = mixed
        logits = mm(mixed, router_ref[...])
        logits_ref[...] = logits
        length = image_length(mask_ref, counts_ref, seq)
        valid = lax.broadcasted_iota(jnp.int32, (ROWS, 1), 0) < length
        dispatch = token_softmax(logits, valid)
        combine = slot_softmax(logits)
        grad = cot[:ROWS, :]
        grad = jnp.where(valid, grad, jnp.zeros_like(grad))
        grad_ref[...] = grad
        slots_ref[:, 0, :] = mm_tn(dispatch.astype(BF16), mixed).astype(BF16)
        slots_ref[:, 1, :] = mm_tn(combine.astype(BF16), grad).astype(BF16)

    return kernel


def token_softmax(logits, valid):
    masked = jnp.where(valid, logits, NEG)
    top = jnp.exp(masked - jnp.max(masked, axis=0, keepdims=True))
    return top / jnp.sum(top, axis=0, keepdims=True)


def slot_softmax(logits):
    top = jnp.exp(logits - jnp.max(logits, axis=-1, keepdims=True))
    return top / jnp.sum(top, axis=-1, keepdims=True)


def expert_values(
    x_ref, win_ref, bias_ref, wout_ref, obias_ref, back_ref, hid_ref, pre_ref, hb_ref, ob_ref
):
    x = x_ref[:, 0, :]
    g = x_ref[:, 1, :]
    ob_ref[...] = jnp.sum(g.astype(F32), axis=0, keepdims=True)
    pre = mm(x, win_ref[0]) + bias_ref[...].astype(F32)
    phi = 0.5 * (1.0 + lax.erf(pre * 2.0 ** (-0.5)))
    hidden = (pre * phi).astype(BF16)
    hid_ref[...] = hidden
    back_ref[:, 0, :] = (mm(hidden, wout_ref[0]) + obias_ref[...].astype(F32)).astype(BF16)
    slope = phi + pre * jnp.exp(-0.5 * pre * pre) * (2.0 * math.pi) ** (-0.5)
    grad_pre = (mm_nt(g, wout_ref[0]) * slope).astype(BF16)
    pre_ref[...] = grad_pre
    hb_ref[...] = jnp.sum(grad_pre.astype(F32), axis=0, keepdims=True)
    back_ref[:, 1, :] = mm_nt(grad_pre, win_ref[0]).astype(BF16)


def expert_weights(x_ref, hid_ref, pre_ref, *refs):
    gin_ref, gout_ref = refs[-2:]
    gin_ref[0] = mm_tn(x_ref[:, 0, :], pre_ref[...])
    gout_ref[0] = mm_tn(hid_ref[...], x_ref[:, 1, :])


def route_backward(groups, here, misc_w, experts):
    def kernel(*refs):
        (back_ref, resid_ref, mixed_ref, logits_ref, grad_ref, mix_ref, router_ref, rows_ref) = (
            refs[:8]
        )
        mask_ref, counts_ref = refs[8:10]
        heads_ref = refs[10]
        rest = refs[11:]
        gheads_refs = rest[:groups]
        tok, keep_ref, send_ref, misc_ref, full, turn = rest[groups:]
        seq = lax.axis_index("seq")
        length = image_length(mask_ref, counts_ref, seq)
        valid = lax.broadcasted_iota(jnp.int32, (ROWS, 1), 0) < length
        logits = logits_ref[...]
        dispatch = token_softmax(logits, valid)
        combine = slot_softmax(logits)
        resid = resid_ref[...]
        mixed = mixed_ref[...]
        slot_out = back_ref[:, 0, :]
        grad_slot = back_ref[:, 1, :]
        grad = grad_ref[...]
        out = jnp.where(valid, resid + mm(combine.astype(BF16), slot_out), 0.0).astype(BF16)
        grad_combine = mm_nt(grad, slot_out)
        grad_dispatch = mm_nt(mixed, grad_slot)
        grad_logits = combine * (
            grad_combine - jnp.sum(combine * grad_combine, axis=-1, keepdims=True)
        ) + dispatch * (grad_dispatch - jnp.sum(dispatch * grad_dispatch, axis=0, keepdims=True))
        low = grad_logits.astype(BF16)
        grad_mixed = mm(dispatch.astype(BF16), grad_slot) + mm_nt(low, router_ref[...])
        normed, root = unit(resid)
        turn[...] = jnp.zeros_like(turn)
        turn[experts + 3 : experts + 4, :] = jnp.sum(grad_mixed * normed, axis=0, keepdims=True)
        turn[experts + 4 : experts + 5, :] = jnp.sum(grad_mixed, axis=0, keepdims=True)
        grad_resid = grad.astype(F32) + unit_back(grad_mixed * rows_ref[3:4], normed, root)
        turn[experts + 2 : experts + 3, :] = jnp.sum(grad_resid, axis=0, keepdims=True)
        turn[:experts, :] = mm_tn(low, mixed)
        misc_ref[...] = turn[...]
        gr = grad_resid.astype(BF16)
        tok[...] = jnp.zeros_like(tok)
        tok[0, :ROWS, :] = out
        tok[1, :ROWS, :] = gr
        for r in range(groups):
            fold(gheads_refs[r], mm_nt(gr, mix_ref[head_rows(seq, r, here), :]).astype(BF16))
            full[head_rows(seq, r, here), :] = mm_tn(heads_ref[r], gr).astype(BF16)
        for core in range(2):

            @pl.when((seq & 1) == core)
            def _():
                for j in range(groups // 2):
                    lanes = slice(j * here, (j + 1) * here)
                    lo = (2 * j + core) * here
                    keep_ref[:, lanes] = full[:, lo : lo + here]
                    lo = (2 * j + 1 - core) * here
                    send_ref[:, lanes] = full[:, lo : lo + here]

    return kernel


def add_shares(keep_ref, got_ref, mine_ref, send_ref):
    chip = lax.axis_index("seq") // 2
    size = mine_ref.shape[1]
    for j in range(2):

        @pl.when(chip == j)
        def _():
            own, other = (slice(to * size, (to + 1) * size) for to in (j, 1 - j))
            mine_ref[...] = (keep_ref[:, own].astype(F32) + got_ref[:, own].astype(F32)).astype(BF16)
            fold(
                send_ref,
                (keep_ref[:, other].astype(F32) + got_ref[:, other].astype(F32)).astype(BF16),
            )


def attend_backward(groups, here, wide, experts):
    heads_here = HEADS // groups

    def kernel(*refs):
        gheads_refs = refs[:groups]
        qkv_ref, probs_ref, unit_ref, wpad_ref, misc_ref, token_ref = refs[groups : groups + 6]
        gqkv, keep_ref, send_ref, turn, gh, gxs, gs = refs[groups + 6 :]
        images, _, features = unit_ref.shape
        seq = lax.axis_index("seq")
        masks = head_masks(wide, heads_here)
        keys = qkv_ref.shape[1]
        scaling = HEAD_DIM ** (-0.5)
        gh[...] = jnp.zeros_like(gh)
        for r in range(groups):
            gh[pl.ds(seq ^ r, 1), :FOLD, :here] = unfold(gheads_refs[r], 0, ROWS)[None]
            gh[pl.ds(seq ^ r, 1), FOLD:, :here] = unfold(gheads_refs[r], 1, ROWS)[None]

        def by_head(stacked):
            picked = stacked[(heads_here - 1) * keys : (heads_here - 1) * keys + ROWS]
            for h in range(heads_here - 1):
                picked = jnp.where(masks[h], stacked[h * keys : h * keys + ROWS], picked)
            return picked

        for i in range(images):
            q, k, v = head_stacks(qkv_ref, i, wide, heads_here)
            go = gh[i]
            gp = mm_nt(go, v)
            for h in range(heads_here):
                lanes = slice(h * keys, (h + 1) * keys)
                probs = probs_ref[i, :, lanes].astype(F32)
                inner = jnp.sum(probs * gp[:, lanes], axis=-1, keepdims=True)
                gs[:, lanes] = (probs * (gp[:, lanes] - inner)).astype(BF16)
            rows = slice(i * ROWS, (i + 1) * ROWS)
            gqkv[rows, :wide] = (mm(gs[...], k) * scaling).astype(BF16)
            gqkv[rows, wide : 2 * wide] = (by_head(mm_tn(gs[...], q)) * scaling).astype(BF16)
            gqkv[rows, 2 * wide :] = by_head(mm_tn(probs_ref[i], go)).astype(BF16)
        gx = mm_nt(gqkv[...], wpad_ref[...])
        shard = keep_ref.shape[2]
        gxs[:, :ROWS, :] = gx.astype(BF16).reshape(images, ROWS, features)
        gxs[:, ROWS:, :] = jnp.zeros((images, gxs.shape[1] - ROWS, features), BF16)
        for j in range(2):
            for to, ref in ((seq ^ (2 * j), keep_ref), (seq ^ (2 * j + 1), send_ref)):
                rows = pl.ds(pl.multiple_of(to * shard, shard), shard)
                ref[j, :images] = gxs[:, rows, :]
                ref[j, images:] = token_ref[:, rows, :]
        normed = unit_ref[...].reshape(images * ROWS, features).astype(F32)
        turn[...] = misc_ref[...]
        turn[experts : experts + 1, :] = jnp.sum(gx * normed, axis=0, keepdims=True)
        turn[experts + 1 : experts + 2, :] = jnp.sum(gx, axis=0, keepdims=True)

    return kernel


def project_backward(pieces, here, wide, misc_w):
    def kernel(*refs):
        gqkv_ref, xa_ref, misc_ref, gmix_ref, other_ref = refs[:5]
        out_refs = refs[5 : 5 + pieces]
        full = refs[5 + pieces]
        images, _, features = xa_ref.shape
        flat = xa_ref[...].reshape(images * ROWS, features)
        gw = mm_tn(flat, gqkv_ref[...]).astype(BF16)
        for j in range(3):
            full[:, j * here : (j + 1) * here] = gw[:, j * wide : j * wide + here]
        full[:, 3 * here : 3 * here + misc_w] = misc_ref[...].T.astype(BF16)
        middle = other_ref.shape[0]
        for part, rows in ((0, slice(0, middle)), (1, slice(middle, features))):
            other = unfold(other_ref, part, features)
            gmix = gmix_ref[rows, :].astype(F32) + other.astype(F32)
            full[rows, 3 * here + misc_w :] = gmix.astype(BF16)
        if pieces == 1:
            out_refs[0][...] = full[...]
        else:
            dp = lax.axis_index("dp")
            part = out_refs[0].shape[0]
            half = part // 2

            def block(step, lo, rows):
                at = pl.multiple_of((dp ^ step) * part + lo, half)
                return full[pl.ds(at, rows), :]

            for ref, step in zip(out_refs, (0, 1, 2, 4)):
                ref[...] = block(step, 0, part)
            for ref, step, lo in ((out_refs[4], 5, 0), (out_refs[5], 6, half)):
                ref[:part, :] = block(step, 0, part)
                ref[part:, :] = block(3, lo, half)
            out_refs[6][...] = block(7, 0, half)
            out_refs[7][...] = block(7, half, half)

    return kernel


def token_backward(keep_ref, core_ref, chip_ref, tok_ref, rows_ref, out_ref, grad_ref, resid):
    seq = lax.axis_index("seq")
    images, shard, features = tok_ref.shape
    total = keep_ref[0, :images].astype(F32) + core_ref[0, :images].astype(F32)
    total = (total + chip_ref[:images].astype(F32)).reshape(images * shard, features)
    for r, got in enumerate(
        (keep_ref.at[0, images:], core_ref.at[0, images:], chip_ref.at[images : images + 2],
         chip_ref.at[images + 2 :])
    ):
        out_ref[pl.ds(seq ^ r, 1)] = got[0:1]
        resid[pl.ds(seq ^ r, 1)] = got[1:2]
    normed, root = unit(tok_ref[...].astype(F32).reshape(images * shard, features))
    back = unit_back(total * rows_ref[0:1], normed, root).reshape(images, shard, features)
    grad_ref[...] = (resid[...].astype(F32) + back).astype(BF16)


def plus(a, b):
    return (a.astype(F32) + b.astype(F32)).astype(BF16)


def reduce_last(y_ref, z_ref, first_ref, second_ref, to_y, to_z):
    half = first_ref.shape[0]
    to_y[...] = y_ref[...]
    to_z[...] = z_ref[...]
    to_y[half : 2 * half, :] = plus(y_ref[half : 2 * half, :], second_ref[...])
    to_z[:half, :] = plus(z_ref[:half, :], first_ref[...])


def reduce_blocks(beside_ref, across_ref, far_ref, y_ref, z_ref, beside, across, far):
    part = far_ref.shape[0]
    half = part // 2
    total = far_ref[...].astype(F32) + y_ref[:part, :].astype(F32)
    far[...] = (total + z_ref[:part, :].astype(F32)).astype(BF16)
    across[:half, :] = plus(across_ref[:half, :], y_ref[part:, :])
    across[half:, :] = across_ref[half:, :]
    beside[:half, :] = beside_ref[:half, :]
    beside[half:, :] = plus(beside_ref[half:, :], z_ref[part:, :])


def add_second(keep_ref, got_ref, out_ref):
    images = keep_ref.shape[1] - 2
    out_ref[:images] = (
        keep_ref[1, :images].astype(F32) + got_ref[1, :images].astype(F32)
    ).astype(BF16)
    out_ref[images : images + 2] = keep_ref[1, images:]
    out_ref[images + 2 :] = got_ref[1, images:]


def sum_parts(*refs):
    total = refs[0][...].astype(F32)
    for ref in refs[1:-1]:
        total = total + ref[...].astype(F32)
    refs[-1][...] = total.astype(BF16)


def spread_parts(groups, here, misc_w, experts):
    def kernel(*refs):
        in_refs = refs[:groups]
        qkv_ref, mix_ref, router_ref = refs[groups : groups + 3]
        row_refs = refs[groups + 3 :]
        features = mix_ref.shape[1]
        seq = lax.axis_index("seq")
        for s in range(groups):

            @pl.when(seq == s)
            def _():
                for r in range(groups):
                    g = s ^ r
                    for j in range(3):
                        lo = j * features + g * here
                        part = in_refs[r][:, j * here : (j + 1) * here]
                        qkv_ref[:, lo : lo + here] = part.astype(F32)
                    part = in_refs[r][:, 3 * here + misc_w :]
                    mix_ref[:, g * here : (g + 1) * here] = part.astype(F32)

        misc = in_refs[0][:, 3 * here : 3 * here + misc_w].astype(F32)
        for r in range(1, groups):
            misc = misc + in_refs[r][:, 3 * here : 3 * here + misc_w].astype(F32)
        misc = misc.T
        router_ref[...] = misc[:experts]
        for j in range(5):
            row_refs[j][...] = misc[experts + j : experts + j + 1]

    return kernel


def body(
    tokens,
    pad_mask,
    counts,
    attn_gain,
    attn_shift,
    qkv_weight,
    mix_weight,
    mix_bias,
    moe_gain,
    moe_shift,
    router,
    expert_in,
    hidden_bias,
    expert_out,
    output_bias,
    cotangent,
):
    images, shard, features = tokens.shape
    groups = lax.axis_size("seq")
    lanes = lax.axis_size("dp")
    devices = groups * lanes
    part = mix_weight.shape[0]
    experts = router.shape[1]
    hidden = expert_in.shape[2]
    misc_w = -(-(experts + 8) // 64) * 64
    here = HEADS // groups * HEAD_DIM
    wide = -(-here // 128) * 128
    half = features // 2
    full = groups * shard
    direct = lanes == 8 and part % 32 == 0
    piece_w = 3 * here + misc_w + here

    def swap(a, axis, step):
        return lax.ppermute(a, axis, [(i, i ^ step) for i in range(lax.axis_size(axis))])

    def exchange(parts):
        moved = {r: swap(parts[r], "seq", r) for r in range(groups - 1, 0, -1)}
        return [parts[0]] + [moved[r] for r in range(1, groups)]

    packed_w = 3 * here + misc_w + half
    piece, *cots = kernel_call(
        pack_inputs(groups, here, half, misc_w, experts),
        [qkv_weight, router.T]
        + [v.reshape(1, part) for v in (attn_gain, attn_shift, mix_bias, moe_gain, moe_shift)]
        + [mix_weight, cotangent],
        [((part, packed_w), BF16)] + [((shard, features), BF16)] * groups,
        [pltpu.VMEM((misc_w, -(-part // 128) * 128), F32)],
        limit=ALL_VMEM,
        hbm_in=tuple(range(9)),
    )
    cots = exchange(cots)
    over = swap(tokens, "seq", 2)
    near = swap(tokens, "seq", 1)
    if direct:
        far, across, beside = (swap(piece, "dp", step) for step in (4, 2, 1))
        far, across, beside, over, cots[2] = lax.optimization_barrier(
            (far, across, beside, over, cots[2])
        )
        longer = ((part + part // 2, packed_w), BF16)
        to_y, to_z = kernel_call(forward_blocks, [beside, across, far], [longer] * 2, limit=4)
        by_y, by_z = swap(to_y, "dp", 1), swap(to_z, "dp", 2)
        by_y, by_z, near, cots[1], cots[3] = lax.optimization_barrier(
            (by_y, by_z, near, cots[1], cots[3])
        )
        a, b = kernel_call(forward_last, [by_y, by_z], [((part // 2, packed_w), BF16)] * 2, limit=4)
        piece_parts = [piece, beside, across, far, by_y, by_z, swap(a, "dp", 1), swap(b, "dp", 2)]
    else:
        piece_parts = [lax.all_gather(piece, "dp", axis=0, tiled=True)]
    normed, units, mine = kernel_call(
        normalize_tokens(groups),
        [tokens, near, over, swap(over, "seq", 1)],
        [
            ((images, ROWS, features), F32),
            ((images, ROWS, features), BF16),
            ((ROWS, features), BF16),
        ],
        [pltpu.VMEM((images, full, features), BF16)],
        limit=8,
        flops=1e8,
    )
    outs = kernel_call(
        attend_forward(groups, len(piece_parts), here, wide, misc_w, experts),
        [normed, pad_mask, counts] + piece_parts,
        [((FOLD, 2 * here), BF16)] * groups
        + [
            ((features, half), BF16),
            ((images, ROWS, HEADS // groups * full), BF16),
            ((images, ROWS, features), BF16),
            ((images, full, 3 * wide), BF16),
            ((features, 3 * wide), BF16),
            ((8, features), F32),
            ((features, experts), BF16),
        ],
        [
            pltpu.VMEM((features, packed_w), BF16),
            pltpu.VMEM((images, ROWS, here), BF16),
        ],
        smem=(2,),
        limit=16,
        flops=1e8,
    )
    sent = exchange(outs[:groups])
    mix_half, probs, xa, qkv, wpad, rows, router_full = outs[groups:]
    slots, resid, mixed, logits, mix_full, grad, heads = kernel_call(
        route_forward(groups, here, half),
        sent
        + cots
        + [mine, rows, router_full, pad_mask, counts, mix_half, swap(mix_half, "seq", 1)],
        [
            ((experts, 2, features), BF16),
            ((ROWS, features), F32),
            ((ROWS, features), BF16),
            ((ROWS, experts), F32),
            ((features, features), BF16),
            ((ROWS, features), BF16),
            ((groups, ROWS, here), BF16),
        ],
        [pltpu.VMEM((full, features), BF16)],
        smem=(2 * groups + 4,),
        limit=10,
        flops=5e9,
    )
    slots = lax.all_to_all(slots, ("dp", "seq"), split_axis=0, concat_axis=0, tiled=True)
    block = min(512, hidden)
    back, hid, grad_pre, grad_hidden_bias, grad_output_bias = kernel_call(
        expert_values,
        [slots, expert_in, hidden_bias, expert_out, output_bias],
        [
            ((devices, 2, features), BF16),
            ((devices, hidden), BF16),
            ((devices, hidden), BF16),
            ((1, hidden), F32),
            ((1, features), F32),
        ],
        limit=8,
        flops=5e9,
    )
    back = lax.all_to_all(back, ("dp", "seq"), split_axis=0, concat_axis=0, tiled=True)

    def expert_gradients(first, count, ins):
        lane_spec = pl.BlockSpec((devices, block), lambda i: (0, i + first))
        return pl.pallas_call(
            expert_weights,
            grid=(count,),
            in_specs=[pl.BlockSpec((devices, 2, features), lambda i: (0, 0, 0))]
            + [lane_spec] * 2
            + [pl.BlockSpec(memory_space=pl.ANY)] * (len(ins) - 3),
            out_specs=[
                pl.BlockSpec((1, features, block), lambda i: (0, 0, i + first)),
                pl.BlockSpec((1, block, features), lambda i: (0, i + first, 0)),
            ],
            out_shape=[
                jax.ShapeDtypeStruct((1, features, hidden), F32),
                jax.ShapeDtypeStruct((1, hidden, features), F32),
            ],
            input_output_aliases={i: i - 3 for i in range(3, len(ins))},
            compiler_params=pltpu.CompilerParams(vmem_limit_bytes=12 * 2**20),
            cost_estimate=pl.CostEstimate(
                flops=1 if first else 10**11, bytes_accessed=0, transcendentals=0
            ),
        )(*ins)

    steps = hidden // block
    early = steps // 3
    expert_grads = expert_gradients(0, early, [slots, hid, grad_pre])
    outs = kernel_call(
        route_backward(groups, here, misc_w, experts),
        [back, resid, mixed, logits, grad, mix_full, router_full, rows, pad_mask, counts, heads],
        [((FOLD, 2 * here), BF16)] * groups
        + [((2, full, features), BF16)]
        + [((features, groups // 2 * here), BF16)] * 2
        + [((misc_w, features), F32)],
        [pltpu.VMEM((features, features), BF16), pltpu.VMEM((misc_w, features), F32)],
        smem=(9,),
        limit=16,
        flops=5e9,
    )
    gheads = exchange(outs[:groups])
    token_rows, keep, send, misc = outs[groups:]
    gmix, gmix_send = kernel_call(
        add_shares,
        [keep, swap(send, "seq", 1)],
        [((features, here), BF16), ((features // 2, 2 * here), BF16)],
        limit=8,
    )
    gmix, gmix_send, own = lax.optimization_barrier((gmix, gmix_send, gheads[0]))
    gmix_other = swap(gmix_send, "seq", 2)
    gqkv, gx, gx_send, misc = kernel_call(
        attend_backward(groups, here, wide, experts),
        [own] + gheads[1:] + [qkv, probs, units, wpad, misc, token_rows],
        [
            ((images * ROWS, 3 * wide), BF16),
            ((2, images + 2, shard, features), BF16),
            ((2, images + 2, shard, features), BF16),
            ((misc_w, features), F32),
        ],
        [
            pltpu.VMEM((images, ROWS, wide), BF16),
            pltpu.VMEM((images, full, features), BF16),
            pltpu.VMEM((ROWS, HEADS // groups * full), BF16),
        ],
        limit=16,
        flops=1e10,
    )
    gx_core = swap(gx_send, "seq", 1)
    whole = ((part, piece_w), BF16)
    longer = ((part + part // 2, piece_w), BF16)
    shorter = ((part // 2, piece_w), BF16)
    out_parts = [whole] * 4 + [longer] * 2 + [shorter] * 2
    if not direct:
        out_parts = [((features, piece_w), BF16)]
    outs = kernel_call(
        project_backward(len(out_parts), here, wide, misc_w),
        [gqkv, xa, misc, gmix, gmix_other],
        out_parts,
        [pltpu.VMEM((features, piece_w), BF16)],
        limit=16,
        flops=2e10,
    )
    gx_core, _ = lax.optimization_barrier((gx_core, outs[0]))
    if direct:
        own, beside, across, far, to_y, to_z, first, second = outs
        first, second = swap(first, "dp", 1), swap(second, "dp", 2)
        first, second, *expert_grads = lax.optimization_barrier([first, second] + list(expert_grads))
        expert_grads = expert_gradients(early, steps - early, [slots, hid, grad_pre, *expert_grads])
        to_y, to_z = kernel_call(
            reduce_last, [to_y, to_z, first, second], [longer] * 2, limit=4
        )
        by_y, by_z = swap(to_y, "dp", 1), swap(to_z, "dp", 2)
        by_y, by_z, *expert_grads = lax.optimization_barrier([by_y, by_z] + list(expert_grads))
        beside, across, far = kernel_call(
            reduce_blocks, [beside, across, far, by_y, by_z], [whole] * 3, limit=4
        )
        sums = [swap(far, "dp", 4), swap(across, "dp", 2), swap(beside, "dp", 1), own]
    else:
        expert_grads = expert_gradients(early, steps - early, [slots, hid, grad_pre, *expert_grads])
        arrived = lax.all_to_all(outs[0], "dp", split_axis=0, concat_axis=0, tiled=True)
        sums = [arrived[r * part : (r + 1) * part] for r in range(lanes)]
    (gx_sum,) = kernel_call(
        add_second, [gx, gx_core], [((images + 4, shard, features), BF16)], limit=4
    )
    gx_chip = swap(gx_sum, "seq", 2)
    (share,) = kernel_call(sum_parts, sums, [whole], limit=4)
    share, gx_chip = lax.optimization_barrier((share, gx_chip))
    block_out, input_grad = kernel_call(
        token_backward,
        [gx, gx_core, gx_chip, tokens, rows],
        [((images, shard, features), BF16), ((images, shard, features), BF16)],
        [pltpu.VMEM((images, shard, features), BF16)],
        limit=8,
        flops=2e9,
    )
    share_over = swap(share, "seq", 2)
    shares = [share, swap(share, "seq", 1), share_over, swap(share_over, "seq", 1)]
    grad_qkv, grad_mix, grad_router, *vector_rows = kernel_call(
        spread_parts(groups, here, misc_w, experts),
        shares,
        [((part, 3 * features), F32), ((part, features), F32), ((experts, part), F32)]
        + [((1, part), F32)] * 5,
        limit=8,
    )
    vector_rows = [v.reshape(part) for v in vector_rows]
    return (
        block_out,
        input_grad,
        vector_rows[0],
        vector_rows[1],
        grad_qkv,
        grad_mix,
        vector_rows[2],
        vector_rows[3],
        vector_rows[4],
        grad_router.T,
        expert_grads[0],
        grad_hidden_bias,
        expert_grads[1],
        grad_output_bias,
    )


def solution(mesh):
    return jax.shard_map(
        body,
        mesh=mesh,
        in_specs=(
            P("dp", "seq", None),
            P("dp", None),
            P("dp"),
            P("dp"),
            P("dp"),
            P("dp", None),
            P("dp", None),
            P("dp"),
            P("dp"),
            P("dp"),
            P("dp", None),
            P(("dp", "seq"), None, None),
            P(("dp", "seq"), None),
            P(("dp", "seq"), None, None),
            P(("dp", "seq"), None),
            P("dp", "seq", None),
        ),
        out_specs=(
            P("dp", "seq", None),
            P("dp", "seq", None),
            P("dp"),
            P("dp"),
            P("dp", None),
            P("dp", None),
            P("dp"),
            P("dp"),
            P("dp"),
            P("dp", None),
            P(("dp", "seq"), None, None),
            P(("dp", "seq"), None),
            P(("dp", "seq"), None, None),
            P(("dp", "seq"), None),
        ),
        check_vma=False,
    )
```

time: 611 us -> 122 us (0.20); the launches traced: 599 us -> 122 us
  waiting for transfers between devices: 222 us -> 31.4 us
  blocking collectives: 161 us -> 21.9 us
  matrix products: 78.8 us -> 0 us
  local copies, waits for them, and re-layouts: 73.1 us -> 0.05 us
  Pallas kernels: 0 us -> 33.5 us
  other arithmetic: 21.7 us -> 0.01 us
  between operations: 17.1 us -> 1.58 us
  starting transfers between devices: 25.1 us -> 33.5 us
    reduce_scatter x2 -> x0, waiting for transfers between devices: 157 us -> none  [the longest x1 132 us: body(): lax.psum_scatter(weight_grads[2], 'dp', scatter_dimension=0, tiled=True)]
    dot_general x27 -> x0, matrix products: 78.8 us -> none  [the longest x1 5.32 us: body(): jnp.dot(normed_low.reshape(-1, features).T, token_side, preferred_element...]
    unnamed x2 -> x0, blocking collectives: 60.5 us -> none
    all_gather x3 -> x0, blocking collectives: 41.1 us -> none  [the longest x1 24.3 us: forward(): lax.all_gather(weights[7], 'dp', axis=0, tiled=True)]
    all_to_all x6 -> x0, waiting for transfers between devices: 36.3 us -> none  [the longest x1 17.7 us: forward(): lax.all_to_all(project, 'seq', split_axis=3, concat_axis=1, tiled=True)]
    pallas_call x0 -> x19, Pallas kernels: none -> 33.5 us  [the longest x17 24.9 us: kernel_call(): return list(call(*ins))]
    ppermute x0 -> x34, starting transfers between devices: none -> 33.5 us  [swap(): lax.ppermute(a, axis, [(i, i ^ step) for i in range(lax.axis_size(axis))])]
    ppermute x0 -> x34, waiting for transfers between devices: none -> 31.4 us  [swap(): lax.ppermute(a, axis, [(i, i ^ step) for i in range(lax.axis_size(axis))])]
  transfers between devices with their start and end apart: 12 -> 34, of which waited for: 7 -> 13; matrix products, arithmetic and copies ran while one was open for 20% -> 0% of each run, Pallas kernels for 0% -> 16%
where the time goes in v1:
time: 122 us
  starting transfers between devices  33.5 us (27%)
  Pallas kernels  33.5 us (27%)
  waiting for transfers between devices  31.4 us (26%)
  blocking collectives  21.9 us (18%)
  between operations  1.58 us (1%)
    ppermute x34, starting transfers between devices, swap(): lax.ppermute(a, axis, [(i, i ^ step) for i in range(lax.axis_size(axis))])  33.5 us
    ppermute x34, waiting for transfers between devices, swap(): lax.ppermute(a, axis, [(i, i ^ step) for i in range(lax.axis_size(axis))])  31.4 us
    pallas_call x17, Pallas kernels, kernel_call(): return list(call(*ins))  24.9 us
    all_to_all x1, blocking collectives, body(): lax.all_to_all(slots, ('dp', 'seq'), split_axis=0, concat_axis=0, tiled=T...  12.4 us
    all_to_all x1, blocking collectives, body(): lax.all_to_all(back, ('dp', 'seq'), split_axis=0, concat_axis=0, tiled=True)  9.48 us
    pallas_call x2, Pallas kernels, expert_gradients(): pl.pallas_call(expert_weights, grid=(count,), in_specs=[pl.BlockSpec((dev...  8.67 us
  transfers between devices with their start and end apart: 34, of which 13 were waited for; matrix products, arithmetic and copies ran while one was open for 0% of the time, Pallas kernels for 16%

profile of v1, /device:TPU:1, one launch (start us, length us, event | category | flops | bytes accessed | tf_op | source)
XLA Modules:
  0.0 121.9 jit_solution(12658657047589612415)
XLA Ops:
  0.7 2.1 %collective-permute-start.3 = (bf16[4,64,768]{2,1,0:T(8,128)(2,1)}, bf16[4,64,768]{2,1,0:T(8,128)(2,1)S(1)}, u32[]{:S(2)}, u32[]{:S(2)}) collective-permute-start(bf16[4,64,768]{2,1,0:T(8,128)(2,1)} %refs_3_.3), channel_id=1, source_target_pairs={{0,2},{1,3},{2,0},{3,1},{4,6},{5,7},{6,4},{7,5},{8,10},{9,11},{10,... | collective-permute-start | bytes 1179656 | tf_op jit(solution)/shard_map/ppermute | solution.py:632
  2.8 2.3 %shard_map.263 = (bf16[96,1024]{1,0:T(8,128)(2,1)}, bf16[64,768]{1,0:T(8,128)(2,1)}, bf16[64,768]{1,0:T(8,128)(2,1)}, bf16[64,768]{1,0:T(8,128)(2,1)}, bf16[64,768]{1,0:T(8,128)(2,1)}) custom-call(bf16[96,2304]{1,0:T(8,128)(2,1)} %refs_0_.2, bf16[32,96]{1,0:T(8,128)(2,1)} %bitcast.16, bf16[1,96]{1,0:T(2,128)(2,1)} %bitcast.17, bf16[1,96]{1,0:T(2,128)(2,1)} %bitcast.18, ...), custom_call_target="tpu_custom_call" | custom-call | flops 1 | tf_op jit(solution)/shard_map/pallas_call | solution.py:114
  5.1 2.4 %collective-permute-start = (bf16[96,1024]{1,0:T(8,128)(2,1)}, bf16[96,1024]{1,0:T(8,128)(2,1)S(1)}, u32[]{:S(2)}, u32[]{:S(2)}) collective-permute-start(bf16[96,1024]{1,0:T(8,128)(2,1)} %get-tuple-element.114.refs_3_), channel_id=1, source_target_pairs={{0,16},{4,20},{8,24},{12,28},{16,0},{20,4},{24,8},{28,12},{1,17},{... | collective-permute-start | bytes 589832 | tf_op jit(solution)/shard_map/ppermute | solution.py:632
  10.3 3.7 %collective-permute-done.4.refs_6_ = bf16[64,768]{1,0:T(8,128)(2,1)S(1)} collective-permute-done((bf16[64,768]{1,0:T(8,128)(2,1)}, bf16[64,768]{1,0:T(8,128)(2,1)S(1)}, u32[]{:S(2)}, u32[]{:S(2)}) %collective-permute-start.4) | collective-permute-done | bytes 98336 | tf_op jit(solution)/shard_map/ppermute | solution.py:632
  14.0 2.6 %collective-permute-start.7 = (bf16[4,64,768]{2,1,0:T(8,128)(2,1)}, bf16[4,64,768]{2,1,0:T(8,128)(2,1)S(1)}, u32[]{:S(2)}, u32[]{:S(2)}) collective-permute-start(bf16[4,64,768]{2,1,0:T(8,128)(2,1)} %refs_3_.3), channel_id=1, source_target_pairs={{0,1},{1,0},{2,3},{3,2},{4,5},{5,4},{6,7},{7,6},{8,9},{9,8},{10,11... | collective-permute-start | bytes 1179656 | tf_op jit(solution)/shard_map/ppermute | solution.py:632
  22.8 4.8 %collective-permute-done.9.refs_7_ = bf16[64,768]{1,0:T(8,128)(2,1)S(1)} collective-permute-done((bf16[64,768]{1,0:T(8,128)(2,1)}, bf16[64,768]{1,0:T(8,128)(2,1)S(1)}, u32[]{:S(2)}, u32[]{:S(2)}) %collective-permute-start.9) | collective-permute-done | bytes 98336 | tf_op jit(solution)/shard_map/ppermute | solution.py:632
  31.7 3.5 %shard_map.267 = (bf16[112,384]{1,0:T(8,128)(2,1)S(1)}, bf16[112,384]{1,0:T(8,128)(2,1)S(1)}, bf16[112,384]{1,0:T(8,128)(2,1)S(1)}, bf16[112,384]{1,0:T(8,128)(2...) custom-call(f32[4,208,768]{2,1,0:T(8,128)S(1)} %get-tuple-element.12, ...), custom_call_target="tpu_custom_call" | custom-call | flops 100000000 | tf_op jit(solution)/shard_map/pallas_call | solution.py:114
  35.1 2.5 %collective-permute-start.16 = (bf16[768,384]{1,0:T(8,128)(2,1)S(1)}, bf16[768,384]{1,0:T(8,128)(2,1)S(1)}, u32[]{:S(2)}, u32[]{:S(2)}) collective-permute-start(bf16[768,384]{1,0:T(8,128)(2,1)S(1)} %get-tuple-element.141.refs_13_), channel_id=1, source_target_pairs={{0,1},{1,0},{2,3},{3,2},{4,5},{5,4},{6,7},{7,6},{8,9},{9,8},{10,11... | collective-permute-start | bytes 1769480 | tf_op jit(solution)/shard_map/ppermute | solution.py:632
  37.9 1.9 %collective-permute-start.15 = (bf16[112,384]{1,0:T(8,128)(2,1)S(1)}, bf16[112,384]{1,0:T(8,128)(2,1)S(1)}, u32[]{:S(2)}, u32[]{:S(2)}) collective-permute-start(bf16[112,384]{1,0:T(8,128)(2,1)S(1)} %get-tuple-element.133), channel_id=1, source_target_pairs={{0,3},{1,2},{2,1},{3,0},{4,7},{5,6},{6,5},{7,4},{8,11},{9,10},{10,... | collective-permute-start | bytes 258056 | tf_op jit(solution)/shard_map/ppermute | solution.py:632
  41.4 2.4 %collective-permute-done.15.refs_3_ = bf16[112,384]{1,0:T(8,128)(2,1)S(1)} collective-permute-done((bf16[112,384]{1,0:T(8,128)(2,1)S(1)}, bf16[112,384]{1,0:T(8,128)(2,1)S(1)}, u32[]{:S(2)}, u32[]{:S(2)}) %collective-permute-start.15) | collective-permute-done | bytes 86048 | tf_op jit(solution)/shard_map/ppermute | solution.py:632
  43.9 1.7 %shard_map.268 = (bf16[32,2,768]{2,1,0:T(2,128)(2,1)S(1)}, f32[208,768]{1,0:T(8,128)S(1)}, bf16[208,768]{1,0:T(8,128)(2,1)S(1)}, f32[208,32]{1,0:T(8,128)S(1)}, ...) custom-call(bf16[112,384]{1,0:T(8,128)(2,1)S(1)} %get-tuple-element.130.refs_0_, ...), custom_call_target="tpu_custom_call" | custom-call | flops 5000000000 | tf_op jit(solution)/shard_map/pallas_call | solution.py:114
  45.5 12.4 %all_to_all.10.refs_0_.x_ref = bf16[32,2,768]{2,1,0:T(2,128)(2,1)S(1)} all-to-all(bf16[32,2,768]{2,1,0:T(2,128)(2,1)S(1)} %get-tuple-element.142), channel_id=1, replica_groups=mesh['dp'=8,'seq'=4] {'dp','seq'}, dimensions={0} | all-to-all | bytes 196608 | tf_op jit(solution)/shard_map/all_to_all | solution.py:721
  58.0 5.0 %shard_map.269 = (bf16[32,2,768]{2,1,0:T(2,128)(2,1)S(1)}, bf16[32,3072]{1,0:T(8,128)(2,1)S(1)}, bf16[32,3072]{1,0:T(8,128)(2,1)S(1)}, f32[1,3072]{1,0:T(1,128)}, f32[1,768]{1,0:T(1,128)}) custom-call(bf16[32,2,768]{2,1,0:T(2,128)(2,1)S(1)} %all_to_all.10.refs_0_.x_ref, bf16[1,768,3072]{2,1,0:T(8,128)(2,1)S(1)} %bitcast.13, bf16[1,3072]{1,0:T(2,128)(2,1)S(1)} %copy-done.4, ...), custom_call_target="tpu_custom_call" | custom-call | flops 5000000000 | tf_op jit(solution)/shard_map/pallas_call | solution.py:114
  63.0 9.5 %all_to_all.11.refs_0_ = bf16[32,2,768]{2,1,0:T(2,128)(2,1)S(1)} all-to-all(bf16[32,2,768]{2,1,0:T(2,128)(2,1)S(1)} %get-tuple-element.143), channel_id=1, replica_groups=mesh['dp'=8,'seq'=4] {'dp','seq'}, dimensions={0} | all-to-all | bytes 196608 | tf_op jit(solution)/shard_map/all_to_all | solution.py:736
  72.5 2.4 %shard_map.270 = (bf16[112,384]{1,0:T(8,128)(2,1)S(1)}, bf16[112,384]{1,0:T(8,128)(2,1)S(1)}, bf16[112,384]{1,0:T(8,128)(2,1)S(1)}, bf16[112,384]{1,0:T(8,128)(2...) custom-call(bf16[32,2,768]{2,1,0:T(2,128)(2,1)S(1)} %all_to_all.11.r, ...), custom_call_target="tpu_custom_call" | custom-call | flops 5000000000 | tf_op jit(solution)/shard_map/pallas_call | solution.py:114
  75.6 1.9 %collective-permute-start.20 = (bf16[112,384]{1,0:T(8,128)(2,1)S(1)}, bf16[112,384]{1,0:T(8,128)(2,1)S(1)}, u32[]{:S(2)}, u32[]{:S(2)}) collective-permute-start(bf16[112,384]{1,0:T(8,128)(2,1)S(1)} %get-tuple-element.158), channel_id=1, source_target_pairs={{0,3},{1,2},{2,1},{3,0},{4,7},{5,6},{6,5},{7,4},{8,11},{9,10},{10,... | collective-permute-start | bytes 258056 | tf_op jit(solution)/shard_map/ppermute | solution.py:632
  79.3 3.1 %collective-permute-done.20.refs_3_ = bf16[112,384]{1,0:T(8,128)(2,1)S(1)} collective-permute-done((bf16[112,384]{1,0:T(8,128)(2,1)S(1)}, bf16[112,384]{1,0:T(8,128)(2,1)S(1)}, u32[]{:S(2)}, u32[]{:S(2)}) %collective-permute-start.20) | collective-permute-done | bytes 86048 | tf_op jit(solution)/shard_map/ppermute | solution.py:632
  82.4 4.1 %shard_map.272 = (bf16[832,768]{1,0:T(8,128)(2,1)S(1)}, bf16[2,6,64,768]{3,2,1,0:T(8,128)(2,1)S(1)}, bf16[2,6,64,768]{3,2,1,0:T(8,128)(2,1)S(1)}, f32[64,768]{1,0:T(8,128)S(1)}) custom-call(bf16[112,384]{1,0:T(8,128)(2,1)S(1)} %get-tuple-element.155.refs_0_, bf16[112,384]{1,0:T(8,128)(2,1)S(1)} %collective-permute-done.18.refs_1_, ...), custom_call_target="tpu_custom_call" | custom-call | flops 10000000000 | tf_op jit(solution)/shard_map/pallas_call | solution.py:114
  90.9 3.3 %shard_map.274 = (f32[1,768,3072]{2,1,0:T(8,128)}, f32[1,3072,768]{2,1,0:T(8,128)}) custom-call(bf16[32,2,768]{2,1,0:T(2,128)(2,1)S(1)} %all_to_all.10.refs_0_.x_ref, bf16[32,3072]{1,0:T(8,128)(2,1)S(1)} %get-tuple-element.181.hid_ref, bf16[32,3072]{1,0:T(8,128)(2,1)S(1)} %get-tuple-element.182.pre_ref), custom_call_target="tpu_custom_call" | custom-call | flops 99999997952 | tf_op jit(solution)/shard_map/pallas_call | solution.py:740
  96.5 5.4 %shard_map.276 = (f32[1,768,3072]{2,1,0:T(8,128)}, f32[1,3072,768]{2,1,0:T(8,128)}) custom-call(bf16[32,2,768]{2,1,0:T(2,128)(2,1)S(1)} %all_to_all.10.refs_0_.x_ref, bf16[32,3072]{1,0:T(8,128)(2,1)S(1)} %get-tuple-element.181.hid_ref, bf16[32,3072]{1,0:T(8,128)(2,1)S(1)} %get-tuple-element.182.pre_ref, ...), custom_call_target="tpu_custom_call", output_to_operand_aliasing={{0}: (3, {}), {1}: (4, {})} | custom-call | flops 1 | tf_op jit(solution)/shard_map/pallas_call | solution.py:740
  103.6 8.6 %collective-permute-done.27.refs_0_ = bf16[96,832]{1,0:T(8,128)(2,1)S(1)} collective-permute-done((bf16[96,832]{1,0:T(8,128)(2,1)S(1)}, bf16[96,832]{1,0:T(8,128)(2,1)S(1)}, u32[]{:S(2)}, u32[]{:S(2)}) %collective-permute-start.27) | collective-permute-done | bytes 159776 | tf_op jit(solution)/shard_map/ppermute | solution.py:632
  112.5 2.0 %collective-permute-start.31 = (bf16[96,832]{1,0:T(8,128)(2,1)S(1)}, bf16[96,832]{1,0:T(8,128)(2,1)S(1)}, u32[]{:S(2)}, u32[]{:S(2)}) collective-permute-start(bf16[96,832]{1,0:T(8,128)(2,1)S(1)} %shard_map.278.refs_0_), channel_id=1, source_target_pairs={{0,1},{1,0},{2,3},{3,2},{4,5},{5,4},{6,7},{7,6},{8,9},{9,8},{10,11... | collective-permute-start | bytes 479240 | tf_op jit(solution)/shard_map/ppermute | solution.py:632
  114.4 2.7 %collective-permute-done.32.refs_2_ = bf16[96,832]{1,0:T(8,128)(2,1)S(1)} collective-permute-done((bf16[96,832]{1,0:T(8,128)(2,1)S(1)}, bf16[96,832]{1,0:T(8,128)(2,1)S(1)}, u32[]{:S(2)}, u32[]{:S(2)}) %collective-permute-start.32) | collective-permute-done | bytes 159776 | tf_op jit(solution)/shard_map/ppermute | solution.py:632
  117.1 2.1 %collective-permute-start.33 = (bf16[96,832]{1,0:T(8,128)(2,1)S(1)}, bf16[96,832]{1,0:T(8,128)(2,1)S(1)}, u32[]{:S(2)}, u32[]{:S(2)}) collective-permute-start(bf16[96,832]{1,0:T(8,128)(2,1)S(1)} %collective-permute-done.32.refs_2_), channel_id=1, source_target_pairs={{0,1},{1,0},{2,3},{3,2},{4,5},{5,4},{6,7},{7,6},{8,9},{9,8},{10,11... | collective-permute-start | bytes 479240 | tf_op jit(solution)/shard_map/ppermute | solution.py:632
  (87 shorter events, 28.1 us)
Async XLA Ops:
  0.7 16.0 %collective-permute-start.3 = (bf16[4,64,768]{2,1,0:T(8,128)(2,1)}, bf16[4,64,768]{2,1,0:T(8,128)(2,1)S(1)}, u32[]{:S(2)}, u32[]{:S(2)}) collective-permute-start(bf16[4,64,768]{2,1,0:T(8,128)(2,1)} %refs_3_.3), channel_id=1, source_target_pairs={{0,2},{1,3},{2,0},{3,1},{4,6},{5,7},{6,4},{7,5},{8,10},{9,11},{10,... | collective-permute-start | bytes 1179656 | tf_op jit(solution)/shard_map/ppermute | solution.py:632
  5.1 11.5 %collective-permute-start = (bf16[96,1024]{1,0:T(8,128)(2,1)}, bf16[96,1024]{1,0:T(8,128)(2,1)S(1)}, u32[]{:S(2)}, u32[]{:S(2)}) collective-permute-start(bf16[96,1024]{1,0:T(8,128)(2,1)} %get-tuple-element.114.refs_3_), channel_id=1, source_target_pairs={{0,16},{4,20},{8,24},{12,28},{16,0},{20,4},{24,8},{28,12},{1,17},{... | collective-permute-start | bytes 589832 | tf_op jit(solution)/shard_map/ppermute | solution.py:632
  7.5 9.2 %collective-permute-start.1 = (bf16[96,1024]{1,0:T(8,128)(2,1)}, bf16[96,1024]{1,0:T(8,128)(2,1)S(1)}, u32[]{:S(2)}, u32[]{:S(2)}) collective-permute-start(bf16[96,1024]{1,0:T(8,128)(2,1)} %get-tuple-element.114.refs_3_), channel_id=1, source_target_pairs={{0,8},{4,12},{8,0},{12,4},{16,24},{20,28},{24,16},{28,20},{1,9},{5... | collective-permute-start | bytes 589832 | tf_op jit(solution)/shard_map/ppermute | solution.py:632
  8.8 7.9 %collective-permute-start.2 = (bf16[96,1024]{1,0:T(8,128)(2,1)}, bf16[96,1024]{1,0:T(8,128)(2,1)S(1)}, u32[]{:S(2)}, u32[]{:S(2)}) collective-permute-start(bf16[96,1024]{1,0:T(8,128)(2,1)} %get-tuple-element.114.refs_3_), channel_id=1, source_target_pairs={{0,4},{4,0},{8,12},{12,8},{16,20},{20,16},{24,28},{28,24},{1,5},{5... | collective-permute-start | bytes 589832 | tf_op jit(solution)/shard_map/ppermute | solution.py:632
  10.0 4.0 %collective-permute-start.4 = (bf16[64,768]{1,0:T(8,128)(2,1)}, bf16[64,768]{1,0:T(8,128)(2,1)S(1)}, u32[]{:S(2)}, u32[]{:S(2)}) collective-permute-start(bf16[64,768]{1,0:T(8,128)(2,1)} %get-tuple-element.115), channel_id=1, source_target_pairs={{0,2},{1,3},{2,0},{3,1},{4,6},{5,7},{6,4},{7,5},{8,10},{9,11},{10,... | collective-permute-start | bytes 294920 | tf_op jit(solution)/shard_map/ppermute | solution.py:632
  14.0 13.6 %collective-permute-start.7 = (bf16[4,64,768]{2,1,0:T(8,128)(2,1)}, bf16[4,64,768]{2,1,0:T(8,128)(2,1)S(1)}, u32[]{:S(2)}, u32[]{:S(2)}) collective-permute-start(bf16[4,64,768]{2,1,0:T(8,128)(2,1)} %refs_3_.3), channel_id=1, source_target_pairs={{0,1},{1,0},{2,3},{3,2},{4,5},{5,4},{6,7},{7,6},{8,9},{9,8},{10,11... | collective-permute-start | bytes 1179656 | tf_op jit(solution)/shard_map/ppermute | solution.py:632
  16.6 13.3 %collective-permute-start.10 = (bf16[4,64,768]{2,1,0:T(8,128)(2,1)S(1)}, bf16[4,64,768]{2,1,0:T(8,128)(2,1)S(1)}, u32[]{:S(2)}, u32[]{:S(2)}) collective-permute-start(bf16[4,64,768]{2,1,0:T(8,128)(2,1)S(1)} %collective-permute-done.3.refs_2_), channel_id=1, source_target_pairs={{0,1},{1,0},{2,3},{3,2},{4,5},{5,4},{6,7},{7,6},{8,9},{9,8},{10,11... | collective-permute-start | bytes 1179656 | tf_op jit(solution)/shard_map/ppermute | solution.py:632
  18.1 9.5 %collective-permute-start.5 = (bf16[144,1024]{1,0:T(8,128)(2,1)S(1)}, bf16[144,1024]{1,0:T(8,128)(2,1)S(1)}, u32[]{:S(2)}, u32[]{:S(2)}) collective-permute-start(bf16[144,1024]{1,0:T(8,128)(2,1)S(1)} %get-tuple-element.119), channel_id=1, source_target_pairs={{0,4},{4,0},{8,12},{12,8},{16,20},{20,16},{24,28},{28,24},{1,5},{5... | collective-permute-start | bytes 884744 | tf_op jit(solution)/shard_map/ppermute | solution.py:632
  19.5 8.3 %collective-permute-start.6 = (bf16[144,1024]{1,0:T(8,128)(2,1)S(1)}, bf16[144,1024]{1,0:T(8,128)(2,1)S(1)}, u32[]{:S(2)}, u32[]{:S(2)}) collective-permute-start(bf16[144,1024]{1,0:T(8,128)(2,1)S(1)} %get-tuple-element.120), channel_id=1, source_target_pairs={{0,8},{4,12},{8,0},{12,4},{16,24},{20,28},{24,16},{28,20},{1,9},{5... | collective-permute-start | bytes 884744 | tf_op jit(solution)/shard_map/ppermute | solution.py:632
  22.3 5.3 %collective-permute-start.9 = (bf16[64,768]{1,0:T(8,128)(2,1)}, bf16[64,768]{1,0:T(8,128)(2,1)S(1)}, u32[]{:S(2)}, u32[]{:S(2)}) collective-permute-start(bf16[64,768]{1,0:T(8,128)(2,1)} %get-tuple-element.122), channel_id=1, source_target_pairs={{0,3},{1,2},{2,1},{3,0},{4,7},{5,6},{6,5},{7,4},{8,11},{9,10},{10,... | collective-permute-start | bytes 294920 | tf_op jit(solution)/shard_map/ppermute | solution.py:632
  35.1 8.7 %collective-permute-start.16 = (bf16[768,384]{1,0:T(8,128)(2,1)S(1)}, bf16[768,384]{1,0:T(8,128)(2,1)S(1)}, u32[]{:S(2)}, u32[]{:S(2)}) collective-permute-start(bf16[768,384]{1,0:T(8,128)(2,1)S(1)} %get-tuple-element.141.refs_13_), channel_id=1, source_target_pairs={{0,1},{1,0},{2,3},{3,2},{4,5},{5,4},{6,7},{7,6},{8,9},{9,8},{10,11... | collective-permute-start | bytes 1769480 | tf_op jit(solution)/shard_map/ppermute | solution.py:632
  37.9 5.9 %collective-permute-start.15 = (bf16[112,384]{1,0:T(8,128)(2,1)S(1)}, bf16[112,384]{1,0:T(8,128)(2,1)S(1)}, u32[]{:S(2)}, u32[]{:S(2)}) collective-permute-start(bf16[112,384]{1,0:T(8,128)(2,1)S(1)} %get-tuple-element.133), channel_id=1, source_target_pairs={{0,3},{1,2},{2,1},{3,0},{4,7},{5,6},{6,5},{7,4},{8,11},{9,10},{10,... | collective-permute-start | bytes 258056 | tf_op jit(solution)/shard_map/ppermute | solution.py:632
  75.6 6.8 %collective-permute-start.20 = (bf16[112,384]{1,0:T(8,128)(2,1)S(1)}, bf16[112,384]{1,0:T(8,128)(2,1)S(1)}, u32[]{:S(2)}, u32[]{:S(2)}) collective-permute-start(bf16[112,384]{1,0:T(8,128)(2,1)S(1)} %get-tuple-element.158), channel_id=1, source_target_pairs={{0,3},{1,2},{2,1},{3,0},{4,7},{5,6},{6,5},{7,4},{8,11},{9,10},{10,... | collective-permute-start | bytes 258056 | tf_op jit(solution)/shard_map/ppermute | solution.py:632
  77.8 9.6 %collective-permute-start.22 = (bf16[384,384]{1,0:T(8,128)(2,1)S(1)}, bf16[384,384]{1,0:T(8,128)(2,1)S(1)}, u32[]{:S(2)}, u32[]{:S(2)}) collective-permute-start(bf16[384,384]{1,0:T(8,128)(2,1)S(1)} %get-tuple-element.171), channel_id=1, source_target_pairs={{0,2},{1,3},{2,0},{3,1},{4,6},{5,7},{6,4},{7,5},{8,10},{9,11},{10,... | collective-permute-start | bytes 884744 | tf_op jit(solution)/shard_map/ppermute | solution.py:632
  89.0 5.1 %collective-permute-start.23 = (bf16[48,832]{1,0:T(8,128)(2,1)S(1)}, bf16[48,832]{1,0:T(8,128)(2,1)S(1)}, u32[]{:S(2)}, u32[]{:S(2)}) collective-permute-start(bf16[48,832]{1,0:T(8,128)(2,1)S(1)} %get-tuple-element.179), channel_id=1, source_target_pairs={{0,4},{4,0},{8,12},{12,8},{16,20},{20,16},{24,28},{28,24},{1,5},{5... | collective-permute-start | bytes 239624 | tf_op jit(solution)/shard_map/ppermute | solution.py:632
  89.4 4.8 %collective-permute-start.24 = (bf16[48,832]{1,0:T(8,128)(2,1)S(1)}, bf16[48,832]{1,0:T(8,128)(2,1)S(1)}, u32[]{:S(2)}, u32[]{:S(2)}) collective-permute-start(bf16[48,832]{1,0:T(8,128)(2,1)S(1)} %get-tuple-element.180), channel_id=1, source_target_pairs={{0,8},{4,12},{8,0},{12,4},{16,24},{20,28},{24,16},{28,20},{1,9},{5... | collective-permute-start | bytes 239624 | tf_op jit(solution)/shard_map/ppermute | solution.py:632
  89.8 22.5 %collective-permute-start.30 = (bf16[8,64,768]{2,1,0:T(8,128)(2,1)S(1)}, bf16[8,64,768]{2,1,0:T(8,128)(2,1)S(1)}, u32[]{:S(2)}, u32[]{:S(2)}) collective-permute-start(bf16[8,64,768]{2,1,0:T(8,128)(2,1)S(1)} %shard_map.279), channel_id=1, source_target_pairs={{0,2},{1,3},{2,0},{3,1},{4,6},{5,7},{6,4},{7,5},{8,10},{9,11},{10,... | collective-permute-start | bytes 2359304 | tf_op jit(solution)/shard_map/ppermute | solution.py:632
  94.2 7.7 %collective-permute-start.25 = (bf16[144,832]{1,0:T(8,128)(2,1)S(1)}, bf16[144,832]{1,0:T(8,128)(2,1)S(1)}, u32[]{:S(2)}, u32[]{:S(2)}) collective-permute-start(bf16[144,832]{1,0:T(8,128)(2,1)S(1)} %get-tuple-element.187), channel_id=1, source_target_pairs={{0,4},{4,0},{8,12},{12,8},{16,20},{20,16},{24,28},{28,24},{1,5},{5... | collective-permute-start | bytes 718856 | tf_op jit(solution)/shard_map/ppermute | solution.py:632
  95.4 6.5 %collective-permute-start.26 = (bf16[144,832]{1,0:T(8,128)(2,1)S(1)}, bf16[144,832]{1,0:T(8,128)(2,1)S(1)}, u32[]{:S(2)}, u32[]{:S(2)}) collective-permute-start(bf16[144,832]{1,0:T(8,128)(2,1)S(1)} %get-tuple-element.188), channel_id=1, source_target_pairs={{0,8},{4,12},{8,0},{12,4},{16,24},{20,28},{24,16},{28,20},{1,9},{5... | collective-permute-start | bytes 718856 | tf_op jit(solution)/shard_map/ppermute | solution.py:632
  102.0 10.2 %collective-permute-start.27 = (bf16[96,832]{1,0:T(8,128)(2,1)S(1)}, bf16[96,832]{1,0:T(8,128)(2,1)S(1)}, u32[]{:S(2)}, u32[]{:S(2)}) collective-permute-start(bf16[96,832]{1,0:T(8,128)(2,1)S(1)} %get-tuple-element.195), channel_id=1, source_target_pairs={{0,16},{4,20},{8,24},{12,28},{16,0},{20,4},{24,8},{28,12},{1,17},{... | collective-permute-start | bytes 479240 | tf_op jit(solution)/shard_map/ppermute | solution.py:632
  102.5 9.7 %collective-permute-start.28 = (bf16[96,832]{1,0:T(8,128)(2,1)S(1)}, bf16[96,832]{1,0:T(8,128)(2,1)S(1)}, u32[]{:S(2)}, u32[]{:S(2)}) collective-permute-start(bf16[96,832]{1,0:T(8,128)(2,1)S(1)} %get-tuple-element.196), channel_id=1, source_target_pairs={{0,8},{4,12},{8,0},{12,4},{16,24},{20,28},{24,16},{28,20},{1,9},{5... | collective-permute-start | bytes 479240 | tf_op jit(solution)/shard_map/ppermute | solution.py:632
  103.3 8.9 %collective-permute-start.29 = (bf16[96,832]{1,0:T(8,128)(2,1)S(1)}, bf16[96,832]{1,0:T(8,128)(2,1)S(1)}, u32[]{:S(2)}, u32[]{:S(2)}) collective-permute-start(bf16[96,832]{1,0:T(8,128)(2,1)S(1)} %get-tuple-element.197), channel_id=1, source_target_pairs={{0,4},{4,0},{8,12},{12,8},{16,20},{20,16},{24,28},{28,24},{1,5},{5... | collective-permute-start | bytes 479240 | tf_op jit(solution)/shard_map/ppermute | solution.py:632
  112.4 4.7 %collective-permute-start.32 = (bf16[96,832]{1,0:T(8,128)(2,1)S(1)}, bf16[96,832]{1,0:T(8,128)(2,1)S(1)}, u32[]{:S(2)}, u32[]{:S(2)}) collective-permute-start(bf16[96,832]{1,0:T(8,128)(2,1)S(1)} %shard_map.278.refs_0_), channel_id=1, source_target_pairs={{0,2},{1,3},{2,0},{3,1},{4,6},{5,7},{6,4},{7,5},{8,10},{9,11},{10,... | collective-permute-start | bytes 479240 | tf_op jit(solution)/shard_map/ppermute | solution.py:632
  112.5 8.3 %collective-permute-start.31 = (bf16[96,832]{1,0:T(8,128)(2,1)S(1)}, bf16[96,832]{1,0:T(8,128)(2,1)S(1)}, u32[]{:S(2)}, u32[]{:S(2)}) collective-permute-start(bf16[96,832]{1,0:T(8,128)(2,1)S(1)} %shard_map.278.refs_0_), channel_id=1, source_target_pairs={{0,1},{1,0},{2,3},{3,2},{4,5},{5,4},{6,7},{7,6},{8,9},{9,8},{10,11... | collective-permute-start | bytes 479240 | tf_op jit(solution)/shard_map/ppermute | solution.py:632
  (20 other events, 225.9 us)

commit v2 on v1

--- a/solution.py
+++ b/solution.py
@@ -157,9 +157,7 @@
     def kernel(*refs):
         qkv_ref, router_ref = refs[:2]
         vectors = refs[2:7]
-        mix_ref, cot_ref, piece_ref = refs[7:10]
-        cot_refs = refs[10 : 10 + groups]
-        turn = refs[-1]
+        mix_ref, piece_ref, turn = refs[7:]
         seq = lax.axis_index("seq")
         features = qkv_ref.shape[1] // 3
         part = qkv_ref.shape[0]
@@ -178,10 +176,14 @@
         lo = 3 * here + misc_w
         piece_ref[:, 3 * here : lo] = turn[...].T[:part].astype(BF16)
         piece_ref[:, lo:] = mix_ref[:, pl.ds(pl.multiple_of((seq & 1) * half, 128), half)]
-        for r in range(groups):
-            cot_refs[r][...] = cot_ref[pl.ds(seq ^ r, 1)][0]
 
     return kernel
+
+
+def by_image_owner(cot_ref, *cot_refs):
+    seq = lax.axis_index("seq")
+    for r in range(len(cot_refs)):
+        cot_refs[r][...] = cot_ref[pl.ds(seq ^ r, 1)][0]
 
 
 def normalize_tokens(groups):
@@ -403,57 +405,96 @@
     return kernel
 
 
-def add_shares(keep_ref, got_ref, mine_ref, send_ref):
-    chip = lax.axis_index("seq") // 2
-    size = mine_ref.shape[1]
-    for j in range(2):
-
-        @pl.when(chip == j)
-        def _():
-            own, other = (slice(to * size, (to + 1) * size) for to in (j, 1 - j))
-            mine_ref[...] = (keep_ref[:, own].astype(F32) + got_ref[:, own].astype(F32)).astype(BF16)
-            fold(
-                send_ref,
-                (keep_ref[:, other].astype(F32) + got_ref[:, other].astype(F32)).astype(BF16),
-            )
-
-
-def attend_backward(groups, here, wide, experts):
+def add_shares(parts, size):
+    def kernel(keep_ref, got_ref, *refs):
+        mine_refs, send_refs = refs[: len(parts)], refs[len(parts) : -1]
+        total = refs[-1]
+        total[...] = (keep_ref[...].astype(F32) + got_ref[...].astype(F32)).astype(BF16)
+        chip = lax.axis_index("seq") // 2
+        dp = lax.axis_index("dp")
+        width = mine_refs[0].shape[1]
+
+        def block(step, lanes):
+            if size == total.shape[0]:
+                return total[:, lanes]
+            return total[pl.ds(pl.multiple_of((dp ^ step) * size, size), size), lanes]
+
+        for j in range(2):
+
+            @pl.when(chip == j)
+            def _():
+                own, other = (slice(to * width, (to + 1) * width) for to in (j, 1 - j))
+                for steps, mine, send in zip(parts, mine_refs, send_refs):
+                    for k, step in enumerate(steps):
+                        mine[k * size : (k + 1) * size, :] = block(step, own)
+                    fold(send, jnp.concatenate([block(step, other) for step in steps]))
+
+    return kernel
+
+
+def both_chips(mine_ref, other_ref):
+    count, half = mine_ref.shape[0], other_ref.shape[0]
+    return jnp.concatenate(
+        [
+            mine_ref[:half, :].astype(F32) + unfold(other_ref, 0, count).astype(F32),
+            mine_ref[half:, :].astype(F32) + unfold(other_ref, 1, count).astype(F32),
+        ]
+    )
+
+
+def image_backward(gheads_ref, image, qkv_ref, probs_ref, gqkv, gh, gs, heads_here):
+    keys = qkv_ref.shape[1]
+    wide = gh.shape[1]
+    here = gheads_ref.shape[1] // 2
+    masks = head_masks(wide, heads_here)
+    scaling = HEAD_DIM ** (-0.5)
+    gh[:FOLD, :here] = unfold(gheads_ref, 0, ROWS)
+    gh[FOLD:, :here] = unfold(gheads_ref, 1, ROWS)
+
+    def by_head(stacked):
+        picked = stacked[(heads_here - 1) * keys : (heads_here - 1) * keys + ROWS]
+        for h in range(heads_here - 1):
+            picked = jnp.where(masks[h], stacked[h * keys : h * keys + ROWS], picked)
+        return picked
+
+    q, k, v = head_stacks(qkv_ref, image, wide, heads_here)
+    go = gh[...]
+    gp = mm_nt(go, v)
+    for h in range(heads_here):
+        lanes = slice(h * keys, (h + 1) * keys)
+        probs = probs_ref[image, :, lanes].astype(F32)
+        inner = jnp.sum(probs * gp[:, lanes], axis=-1, keepdims=True)
+        gs[:, lanes] = (probs * (gp[:, lanes] - inner)).astype(BF16)
+    rows = pl.ds(pl.multiple_of(image * ROWS, ROWS), ROWS)
+    gqkv[rows, :wide] = (mm(gs[...], k) * scaling).astype(BF16)
+    gqkv[rows, wide : 2 * wide] = (by_head(mm_tn(gs[...], q)) * scaling).astype(BF16)
+    gqkv[rows, 2 * wide :] = by_head(mm_tn(probs_ref[image], go)).astype(BF16)
+
+
+def attend_backward_near(heads_here):
+    def kernel(own_ref, near_ref, qkv_ref, probs_ref, gqkv, gh, gs):
+        seq = lax.axis_index("seq")
+        gh[...] = jnp.zeros_like(gh)
+        for r, ref in enumerate((own_ref, near_ref)):
+            image_backward(ref, seq ^ r, qkv_ref, probs_ref, gqkv, gh, gs, heads_here)
+
+    return kernel
+
+
+def attend_backward_far(groups, here, wide, misc_w, experts):
     heads_here = HEADS // groups
 
     def kernel(*refs):
-        gheads_refs = refs[:groups]
-        qkv_ref, probs_ref, unit_ref, wpad_ref, misc_ref, token_ref = refs[groups : groups + 6]
-        gqkv, keep_ref, send_ref, turn, gh, gxs, gs = refs[groups + 6 :]
+        gheads_refs = refs[: groups - 2]
+        qkv_ref, probs_ref, xa_ref, unit_ref, wpad_ref, misc_ref, token_ref = refs[
+            groups - 2 : groups + 5
+        ]
+        gqkv, keep_ref, send_ref, gw_ref, gh, gs, gxs, turn = refs[groups + 6 :]
         images, _, features = unit_ref.shape
         seq = lax.axis_index("seq")
-        masks = head_masks(wide, heads_here)
-        keys = qkv_ref.shape[1]
-        scaling = HEAD_DIM ** (-0.5)
         gh[...] = jnp.zeros_like(gh)
-        for r in range(groups):
-            gh[pl.ds(seq ^ r, 1), :FOLD, :here] = unfold(gheads_refs[r], 0, ROWS)[None]
-            gh[pl.ds(seq ^ r, 1), FOLD:, :here] = unfold(gheads_refs[r], 1, ROWS)[None]
-
-        def by_head(stacked):
-            picked = stacked[(heads_here - 1) * keys : (heads_here - 1) * keys + ROWS]
-            for h in range(heads_here - 1):
-                picked = jnp.where(masks[h], stacked[h * keys : h * keys + ROWS], picked)
-            return picked
-
-        for i in range(images):
-            q, k, v = head_stacks(qkv_ref, i, wide, heads_here)
-            go = gh[i]
-            gp = mm_nt(go, v)
-            for h in range(heads_here):
-                lanes = slice(h * keys, (h + 1) * keys)
-                probs = probs_ref[i, :, lanes].astype(F32)
-                inner = jnp.sum(probs * gp[:, lanes], axis=-1, keepdims=True)
-                gs[:, lanes] = (probs * (gp[:, lanes] - inner)).astype(BF16)
-            rows = slice(i * ROWS, (i + 1) * ROWS)
-            gqkv[rows, :wide] = (mm(gs[...], k) * scaling).astype(BF16)
-            gqkv[rows, wide : 2 * wide] = (by_head(mm_tn(gs[...], q)) * scaling).astype(BF16)
-            gqkv[rows, 2 * wide :] = by_head(mm_tn(probs_ref[i], go)).astype(BF16)
+        for j, ref in enumerate(gheads_refs):
+            image_backward(ref, seq ^ (j + 2), qkv_ref, probs_ref, gqkv, gh, gs, heads_here)
         gx = mm_nt(gqkv[...], wpad_ref[...])
         shard = keep_ref.shape[2]
         gxs[:, :ROWS, :] = gx.astype(BF16).reshape(images, ROWS, features)
@@ -467,46 +508,39 @@
         turn[...] = misc_ref[...]
         turn[experts : experts + 1, :] = jnp.sum(gx * normed, axis=0, keepdims=True)
         turn[experts + 1 : experts + 2, :] = jnp.sum(gx, axis=0, keepdims=True)
+        gw_ref[:, 3 * here :] = turn[...].T.astype(BF16)
+        gw = mm_tn(xa_ref[...].reshape(images * ROWS, features), gqkv[...]).astype(BF16)
+        for j in range(3):
+            gw_ref[:, j * here : (j + 1) * here] = gw[:, j * wide : j * wide + here]
 
     return kernel
 
 
-def project_backward(pieces, here, wide, misc_w):
-    def kernel(*refs):
-        gqkv_ref, xa_ref, misc_ref, gmix_ref, other_ref = refs[:5]
-        out_refs = refs[5 : 5 + pieces]
-        full = refs[5 + pieces]
-        images, _, features = xa_ref.shape
-        flat = xa_ref[...].reshape(images * ROWS, features)
-        gw = mm_tn(flat, gqkv_ref[...]).astype(BF16)
-        for j in range(3):
-            full[:, j * here : (j + 1) * here] = gw[:, j * wide : j * wide + here]
-        full[:, 3 * here : 3 * here + misc_w] = misc_ref[...].T.astype(BF16)
-        middle = other_ref.shape[0]
-        for part, rows in ((0, slice(0, middle)), (1, slice(middle, features))):
-            other = unfold(other_ref, part, features)
-            gmix = gmix_ref[rows, :].astype(F32) + other.astype(F32)
-            full[rows, 3 * here + misc_w :] = gmix.astype(BF16)
-        if pieces == 1:
-            out_refs[0][...] = full[...]
-        else:
-            dp = lax.axis_index("dp")
-            part = out_refs[0].shape[0]
-            half = part // 2
-
-            def block(step, lo, rows):
-                at = pl.multiple_of((dp ^ step) * part + lo, half)
-                return full[pl.ds(at, rows), :]
-
-            for ref, step in zip(out_refs, (0, 1, 2, 4)):
-                ref[...] = block(step, 0, part)
-            for ref, step, lo in ((out_refs[4], 5, 0), (out_refs[5], 6, half)):
-                ref[:part, :] = block(step, 0, part)
-                ref[part:, :] = block(3, lo, half)
-            out_refs[6][...] = block(7, 0, half)
-            out_refs[7][...] = block(7, half, half)
-
-    return kernel
+def cut_gradients(gw_ref, mine_ref, other_ref, *out_refs):
+    width = gw_ref.shape[1]
+    gmix = both_chips(mine_ref, other_ref).astype(BF16)
+    if len(out_refs) == 1:
+        out_refs[0][:, :width] = gw_ref[...]
+        out_refs[0][:, width:] = gmix
+        return
+    dp = lax.axis_index("dp")
+    part = out_refs[0].shape[0]
+    half = part // 2
+
+    def put(ref, at, step, k, lo, rows):
+        source = pl.multiple_of((dp ^ step) * part + lo, half)
+        ref[at : at + rows, :width] = gw_ref[pl.ds(source, rows), :]
+        if k is not None:
+            ref[at : at + rows, width:] = gmix[k * part + lo : k * part + lo + rows]
+
+    for ref, step in zip(out_refs, (0, 1, 2, 4)):
+        put(ref, 0, step, None, 0, part)
+    put(out_refs[4], 0, 5, 1, 0, part)
+    put(out_refs[4], part, 3, 3, 0, half)
+    put(out_refs[5], 0, 6, 2, 0, part)
+    put(out_refs[5], part, 3, 3, half, half)
+    put(out_refs[6], 0, 7, 0, 0, half)
+    put(out_refs[7], 0, 7, 0, half, half)
 
 
 def token_backward(keep_ref, core_ref, chip_ref, tok_ref, rows_ref, out_ref, grad_ref, resid):
@@ -537,15 +571,30 @@
     to_z[:half, :] = plus(z_ref[:half, :], first_ref[...])
 
 
-def reduce_blocks(beside_ref, across_ref, far_ref, y_ref, z_ref, beside, across, far):
+def reduce_blocks(
+    own_ref, beside_ref, across_ref, far_ref, y_ref, z_ref, mine_ref, other_ref,
+    own, beside, across, far,
+):
     part = far_ref.shape[0]
     half = part // 2
-    total = far_ref[...].astype(F32) + y_ref[:part, :].astype(F32)
-    far[...] = (total + z_ref[:part, :].astype(F32)).astype(BF16)
-    across[:half, :] = plus(across_ref[:half, :], y_ref[part:, :])
-    across[half:, :] = across_ref[half:, :]
-    beside[:half, :] = beside_ref[:half, :]
-    beside[half:, :] = plus(beside_ref[half:, :], z_ref[part:, :])
+    gmix = both_chips(mine_ref, other_ref)
+    width = far_ref.shape[1] - gmix.shape[1]
+
+    def block(ref, k):
+        return jnp.concatenate(
+            [ref[:, :width].astype(F32), gmix[k * part : (k + 1) * part]], axis=1
+        )
+
+    beside_sum, across_sum, far_sum, own_sum = (
+        block(ref, k) for k, ref in enumerate((beside_ref, across_ref, far_ref, own_ref))
+    )
+    own[...] = own_sum.astype(BF16)
+    far_sum = far_sum + y_ref[:part, :].astype(F32) + z_ref[:part, :].astype(F32)
+    far[...] = far_sum.astype(BF16)
+    across[:half, :] = (across_sum[:half] + y_ref[part:, :].astype(F32)).astype(BF16)
+    across[half:, :] = across_sum[half:].astype(BF16)
+    beside[:half, :] = beside_sum[:half].astype(BF16)
+    beside[half:, :] = (beside_sum[half:] + z_ref[part:, :].astype(F32)).astype(BF16)
 
 
 def add_second(keep_ref, got_ref, out_ref):
@@ -636,17 +685,19 @@
         return [parts[0]] + [moved[r] for r in range(1, groups)]
 
     packed_w = 3 * here + misc_w + half
-    piece, *cots = kernel_call(
+    (piece,) = kernel_call(
         pack_inputs(groups, here, half, misc_w, experts),
         [qkv_weight, router.T]
         + [v.reshape(1, part) for v in (attn_gain, attn_shift, mix_bias, moe_gain, moe_shift)]
-        + [mix_weight, cotangent],
-        [((part, packed_w), BF16)] + [((shard, features), BF16)] * groups,
+        + [mix_weight],
+        [((part, packed_w), BF16)],
         [pltpu.VMEM((misc_w, -(-part // 128) * 128), F32)],
         limit=ALL_VMEM,
-        hbm_in=tuple(range(9)),
-    )
-    cots = exchange(cots)
+        hbm_in=tuple(range(8)),
+    )
+    cots = exchange(
+        kernel_call(by_image_owner, [cotangent], [((shard, features), BF16)] * groups, limit=4)
+    )
     over = swap(tokens, "seq", 2)
     near = swap(tokens, "seq", 1)
     if direct:
@@ -775,29 +826,49 @@
     )
     gheads = exchange(outs[:groups])
     token_rows, keep, send, misc = outs[groups:]
-    gmix, gmix_send = kernel_call(
-        add_shares,
+    mix_parts = ((7, 5, 6, 3), (1, 2, 4, 0)) if direct else ((0,),)
+    size = part if direct else features
+    count = size * len(mix_parts[0])
+    outs_mix = kernel_call(
+        add_shares(mix_parts, size),
         [keep, swap(send, "seq", 1)],
-        [((features, here), BF16), ((features // 2, 2 * here), BF16)],
+        [((count, here), BF16)] * len(mix_parts)
+        + [((count // 2, 2 * here), BF16)] * len(mix_parts),
+        [pltpu.VMEM((features, groups // 2 * here), BF16)],
         limit=8,
     )
-    gmix, gmix_send, own = lax.optimization_barrier((gmix, gmix_send, gheads[0]))
-    gmix_other = swap(gmix_send, "seq", 2)
-    gqkv, gx, gx_send, misc = kernel_call(
-        attend_backward(groups, here, wide, experts),
-        [own] + gheads[1:] + [qkv, probs, units, wpad, misc, token_rows],
+    *outs_mix, own = lax.optimization_barrier(outs_mix + [gheads[0]])
+    gmix, gmix_send = outs_mix[: len(mix_parts)], outs_mix[len(mix_parts) :]
+    gmix_other = [swap(gmix_send[0], "seq", 2)]
+    gqkv_spec = ((images * ROWS, 3 * wide), BF16)
+    image_scratch = [
+        pltpu.VMEM((ROWS, wide), BF16),
+        pltpu.VMEM((ROWS, HEADS // groups * full), BF16),
+    ]
+    (gqkv,) = kernel_call(
+        attend_backward_near(HEADS // groups),
+        [own, gheads[1], qkv, probs],
+        [gqkv_spec],
+        image_scratch,
+        limit=8,
+        flops=1e10,
+    )
+    gqkv, gx, gx_send, gw = kernel_call(
+        attend_backward_far(groups, here, wide, misc_w, experts),
+        gheads[2:] + [qkv, probs, xa, units, wpad, misc, token_rows, gqkv],
         [
-            ((images * ROWS, 3 * wide), BF16),
+            gqkv_spec,
             ((2, images + 2, shard, features), BF16),
             ((2, images + 2, shard, features), BF16),
-            ((misc_w, features), F32),
+            ((features, 3 * here + misc_w), BF16),
         ],
-        [
-            pltpu.VMEM((images, ROWS, wide), BF16),
+        image_scratch
+        + [
             pltpu.VMEM((images, full, features), BF16),
-            pltpu.VMEM((ROWS, HEADS // groups * full), BF16),
+            pltpu.VMEM((misc_w, features), F32),
         ],
-        limit=16,
+        limit=20,
+        aliases={groups + 5: 0},
         flops=1e10,
     )
     gx_core = swap(gx_send, "seq", 1)
@@ -808,26 +879,31 @@
     if not direct:
         out_parts = [((features, piece_w), BF16)]
     outs = kernel_call(
-        project_backward(len(out_parts), here, wide, misc_w),
-        [gqkv, xa, misc, gmix, gmix_other],
+        cut_gradients,
+        [gw, gmix[0], gmix_other[0]],
         out_parts,
-        [pltpu.VMEM((features, piece_w), BF16)],
-        limit=16,
+        limit=8,
         flops=2e10,
     )
     gx_core, _ = lax.optimization_barrier((gx_core, outs[0]))
     if direct:
         own, beside, across, far, to_y, to_z, first, second = outs
         first, second = swap(first, "dp", 1), swap(second, "dp", 2)
-        first, second, *expert_grads = lax.optimization_barrier([first, second] + list(expert_grads))
+        late, _ = lax.optimization_barrier((gmix_send[1], gmix_other[0]))
+        first, second, late, *expert_grads = lax.optimization_barrier(
+            [first, second, swap(late, "seq", 2)] + list(expert_grads)
+        )
         expert_grads = expert_gradients(early, steps - early, [slots, hid, grad_pre, *expert_grads])
         to_y, to_z = kernel_call(
             reduce_last, [to_y, to_z, first, second], [longer] * 2, limit=4
         )
         by_y, by_z = swap(to_y, "dp", 1), swap(to_z, "dp", 2)
         by_y, by_z, *expert_grads = lax.optimization_barrier([by_y, by_z] + list(expert_grads))
-        beside, across, far = kernel_call(
-            reduce_blocks, [beside, across, far, by_y, by_z], [whole] * 3, limit=4
+        own, beside, across, far = kernel_call(
+            reduce_blocks,
+            [own, beside, across, far, by_y, by_z, gmix[1], late],
+            [whole] * 4,
+            limit=8,
         )
         sums = [swap(far, "dp", 4), swap(across, "dp", 2), swap(beside, "dp", 1), own]
     else:

time: 122 us -> 121 us (level)
  waiting for transfers between devices: 31.4 us -> 27.5 us
    ppermute x34 -> x35, waiting for transfers between devices: 31.4 us -> 27.5 us  [swap(): lax.ppermute(a, axis, [(i, i ^ step) for i in range(lax.axis_size(axis))])]
    ppermute x34 -> x35, starting transfers between devices: 33.5 us -> 34.6 us  [swap(): lax.ppermute(a, axis, [(i, i ^ step) for i in range(lax.axis_size(axis))])]
    pallas_call x17 -> x19, Pallas kernels: 24.9 us -> 24.9 us  [kernel_call(): return list(call(*ins))]
  transfers between devices with their start and end apart: 34 -> 35, of which waited for: 13 -> 13; matrix products, arithmetic and copies ran while one was open for 0% -> 0% of each run, Pallas kernels for 16% -> 17%
where the time goes in v2:
time: 121 us; the launch traced here: 120 us
  starting transfers between devices  34.6 us (29%)
  Pallas kernels  33.6 us (28%)
  waiting for transfers between devices  27.5 us (23%)
  blocking collectives  21.9 us (18%)
  between operations  1.59 us (1%)
    ppermute x35, starting transfers between devices, swap(): lax.ppermute(a, axis, [(i, i ^ step) for i in range(lax.axis_size(axis))])  34.6 us
    ppermute x35, waiting for transfers between devices, swap(): lax.ppermute(a, axis, [(i, i ^ step) for i in range(lax.axis_size(axis))])  27.5 us
    pallas_call x19, Pallas kernels, kernel_call(): return list(call(*ins))  24.9 us
    all_to_all x1, blocking collectives, body(): lax.all_to_all(slots, ('dp', 'seq'), split_axis=0, concat_axis=0, tiled=T...  12.4 us
    all_to_all x1, blocking collectives, body(): lax.all_to_all(back, ('dp', 'seq'), split_axis=0, concat_axis=0, tiled=True)  9.48 us
    pallas_call x2, Pallas kernels, expert_gradients(): pl.pallas_call(expert_weights, grid=(count,), in_specs=[pl.BlockSpec((dev...  8.71 us
  transfers between devices with their start and end apart: 35, of which 13 were waited for; matrix products, arithmetic and copies ran while one was open for 0% of the time, Pallas kernels for 17%

profile of v2, /device:TPU:1, one launch (start us, length us, event | category | flops | bytes accessed | tf_op | source)
XLA Modules:
  0.0 120.3 jit_solution(6249462925166033367)
XLA Ops:
  0.7 2.1 %collective-permute-start.3 = (bf16[4,64,768]{2,1,0:T(8,128)(2,1)}, bf16[4,64,768]{2,1,0:T(8,128)(2,1)S(1)}, u32[]{:S(2)}, u32[]{:S(2)}) collective-permute-start(bf16[4,64,768]{2,1,0:T(8,128)(2,1)} %refs_3_.3), channel_id=1, source_target_pairs={{0,2},{1,3},{2,0},{3,1},{4,6},{5,7},{6,4},{7,5},{8,10},{9,11},{10,... | collective-permute-start | bytes 1179656 | tf_op jit(solution)/shard_map/ppermute | solution.py:681
  2.8 2.1 %shard_map.263.refs_3_ = bf16[96,1024]{1,0:T(8,128)(2,1)} custom-call(bf16[96,2304]{1,0:T(8,128)(2,1)} %refs_0_.3, bf16[32,96]{1,0:T(8,128)(2,1)} %bitcast.16, bf16[1,96]{1,0:T(2,128)(2,1)} %bitcast.17, bf16[1,96]{1,0:T(2,128)(2,1)} %bitcast.18, bf16[1,96]{1,0:T(2,128)(2,1)} %bitcast.19, bf16[1,96]{1,0:T(2,128)(2,1)} %bitcast.20, bf16[1,96]{1,0:T(2,128)(2,1)} %bitcast.21, ...), custom_call_target="tpu_custom_call" | custom-call | flops 1 | tf_op jit(solution)/shard_map/pallas_call | solution.py:114
  4.9 2.4 %collective-permute-start = (bf16[96,1024]{1,0:T(8,128)(2,1)}, bf16[96,1024]{1,0:T(8,128)(2,1)S(1)}, u32[]{:S(2)}, u32[]{:S(2)}) collective-permute-start(bf16[96,1024]{1,0:T(8,128)(2,1)} %shard_map.263.refs_3_), channel_id=1, source_target_pairs={{0,16},{4,20},{8,24},{12,28},{16,0},{20,4},{24,8},{28,12},{1,17},{... | collective-permute-start | bytes 589832 | tf_op jit(solution)/shard_map/ppermute | solution.py:681
  11.2 3.5 %collective-permute-done.4.refs_6_ = bf16[64,768]{1,0:T(8,128)(2,1)S(1)} collective-permute-done((bf16[64,768]{1,0:T(8,128)(2,1)S(1)}, bf16[64,768]{1,0:T(8,128)(2,1)S(1)}, u32[]{:S(2)}, u32[]{:S(2)}) %collective-permute-start.4) | collective-permute-done | bytes 98336 | tf_op jit(solution)/shard_map/ppermute | solution.py:681
  14.7 2.6 %collective-permute-start.7 = (bf16[4,64,768]{2,1,0:T(8,128)(2,1)}, bf16[4,64,768]{2,1,0:T(8,128)(2,1)S(1)}, u32[]{:S(2)}, u32[]{:S(2)}) collective-permute-start(bf16[4,64,768]{2,1,0:T(8,128)(2,1)} %refs_3_.3), channel_id=1, source_target_pairs={{0,1},{1,0},{2,3},{3,2},{4,5},{5,4},{6,7},{7,6},{8,9},{9,8},{10,11... | collective-permute-start | bytes 1179656 | tf_op jit(solution)/shard_map/ppermute | solution.py:681
  22.5 4.6 %collective-permute-done.9.refs_7_ = bf16[64,768]{1,0:T(8,128)(2,1)S(1)} collective-permute-done((bf16[64,768]{1,0:T(8,128)(2,1)S(1)}, bf16[64,768]{1,0:T(8,128)(2,1)S(1)}, u32[]{:S(2)}, u32[]{:S(2)}) %collective-permute-start.9) | collective-permute-done | bytes 98336 | tf_op jit(solution)/shard_map/ppermute | solution.py:681
  31.5 3.5 %shard_map.268 = (bf16[112,384]{1,0:T(8,128)(2,1)S(1)}, bf16[112,384]{1,0:T(8,128)(2,1)S(1)}, bf16[112,384]{1,0:T(8,128)(2,1)S(1)}, bf16[112,384]{1,0:T(8,128)(2...) custom-call(f32[4,208,768]{2,1,0:T(8,128)S(1)} %get-tuple-element.12, ...), custom_call_target="tpu_custom_call" | custom-call | flops 100000000 | tf_op jit(solution)/shard_map/pallas_call | solution.py:114
  35.0 2.5 %collective-permute-start.16 = (bf16[768,384]{1,0:T(8,128)(2,1)S(1)}, bf16[768,384]{1,0:T(8,128)(2,1)S(1)}, u32[]{:S(2)}, u32[]{:S(2)}) collective-permute-start(bf16[768,384]{1,0:T(8,128)(2,1)S(1)} %get-tuple-element.145.refs_13_), channel_id=1, source_target_pairs={{0,1},{1,0},{2,3},{3,2},{4,5},{5,4},{6,7},{7,6},{8,9},{9,8},{10,11... | collective-permute-start | bytes 1769480 | tf_op jit(solution)/shard_map/ppermute | solution.py:681
  37.8 1.9 %collective-permute-start.15 = (bf16[112,384]{1,0:T(8,128)(2,1)S(1)}, bf16[112,384]{1,0:T(8,128)(2,1)S(1)}, u32[]{:S(2)}, u32[]{:S(2)}) collective-permute-start(bf16[112,384]{1,0:T(8,128)(2,1)S(1)} %get-tuple-element.137), channel_id=1, source_target_pairs={{0,3},{1,2},{2,1},{3,0},{4,7},{5,6},{6,5},{7,4},{8,11},{9,10},{10,... | collective-permute-start | bytes 258056 | tf_op jit(solution)/shard_map/ppermute | solution.py:681
  41.3 2.4 %collective-permute-done.15.refs_3_ = bf16[112,384]{1,0:T(8,128)(2,1)S(1)} collective-permute-done((bf16[112,384]{1,0:T(8,128)(2,1)S(1)}, bf16[112,384]{1,0:T(8,128)(2,1)S(1)}, u32[]{:S(2)}, u32[]{:S(2)}) %collective-permute-start.15) | collective-permute-done | bytes 86048 | tf_op jit(solution)/shard_map/ppermute | solution.py:681
  43.7 1.6 %shard_map.269 = (bf16[32,2,768]{2,1,0:T(2,128)(2,1)S(1)}, f32[208,768]{1,0:T(8,128)S(1)}, bf16[208,768]{1,0:T(8,128)(2,1)S(1)}, f32[208,32]{1,0:T(8,128)S(1)}, ...) custom-call(bf16[112,384]{1,0:T(8,128)(2,1)S(1)} %get-tuple-element.134.refs_0_, ...), custom_call_target="tpu_custom_call" | custom-call | flops 5000000000 | tf_op jit(solution)/shard_map/pallas_call | solution.py:114
  45.4 12.4 %all_to_all.10.refs_0_.x_ref = bf16[32,2,768]{2,1,0:T(2,128)(2,1)S(1)} all-to-all(bf16[32,2,768]{2,1,0:T(2,128)(2,1)S(1)} %get-tuple-element.146), channel_id=1, replica_groups=mesh['dp'=8,'seq'=4] {'dp','seq'}, dimensions={0} | all-to-all | bytes 196608 | tf_op jit(solution)/shard_map/all_to_all | solution.py:772
  57.8 5.0 %shard_map.270 = (bf16[32,2,768]{2,1,0:T(2,128)(2,1)S(1)}, bf16[32,3072]{1,0:T(8,128)(2,1)S(1)}, bf16[32,3072]{1,0:T(8,128)(2,1)S(1)}, f32[1,3072]{1,0:T(1,128)}, f32[1,768]{1,0:T(1,128)}) custom-call(bf16[32,2,768]{2,1,0:T(2,128)(2,1)S(1)} %all_to_all.10.refs_0_.x_ref, bf16[1,768,3072]{2,1,0:T(8,128)(2,1)S(1)} %bitcast.13, bf16[1,3072]{1,0:T(2,128)(2,1)S(1)} %copy-done.6, ...), custom_call_target="tpu_custom_call" | custom-call | flops 5000000000 | tf_op jit(solution)/shard_map/pallas_call | solution.py:114
  62.9 9.5 %all_to_all.11.refs_0_ = bf16[32,2,768]{2,1,0:T(2,128)(2,1)S(1)} all-to-all(bf16[32,2,768]{2,1,0:T(2,128)(2,1)S(1)} %get-tuple-element.147), channel_id=1, replica_groups=mesh['dp'=8,'seq'=4] {'dp','seq'}, dimensions={0} | all-to-all | bytes 196608 | tf_op jit(solution)/shard_map/all_to_all | solution.py:787
  72.4 2.4 %shard_map.271 = (bf16[112,384]{1,0:T(8,128)(2,1)S(1)}, bf16[112,384]{1,0:T(8,128)(2,1)S(1)}, bf16[112,384]{1,0:T(8,128)(2,1)S(1)}, bf16[112,384]{1,0:T(8,128)(2...) custom-call(bf16[32,2,768]{2,1,0:T(2,128)(2,1)S(1)} %all_to_all.11.r, ...), custom_call_target="tpu_custom_call" | custom-call | flops 5000000000 | tf_op jit(solution)/shard_map/pallas_call | solution.py:114
  75.5 1.9 %collective-permute-start.18 = (bf16[112,384]{1,0:T(8,128)(2,1)S(1)}, bf16[112,384]{1,0:T(8,128)(2,1)S(1)}, u32[]{:S(2)}, u32[]{:S(2)}) collective-permute-start(bf16[112,384]{1,0:T(8,128)(2,1)S(1)} %get-tuple-element.155), channel_id=1, source_target_pairs={{0,3},{1,2},{2,1},{3,0},{4,7},{5,6},{6,5},{7,4},{8,11},{9,10},{10,... | collective-permute-start | bytes 258056 | tf_op jit(solution)/shard_map/ppermute | solution.py:681
  79.4 2.9 %collective-permute-done.18.refs_1_ = bf16[112,384]{1,0:T(8,128)(2,1)S(1)} collective-permute-done((bf16[112,384]{1,0:T(8,128)(2,1)S(1)}, bf16[112,384]{1,0:T(8,128)(2,1)S(1)}, u32[]{:S(2)}, u32[]{:S(2)}) %collective-permute-start.18) | collective-permute-done | bytes 86048 | tf_op jit(solution)/shard_map/ppermute | solution.py:681
  82.2 4.2 %shard_map.274 = (bf16[832,768]{1,0:T(8,128)(2,1)S(1)}, bf16[2,6,64,768]{3,2,1,0:T(8,128)(2,1)S(1)}, bf16[2,6,64,768]{3,2,1,0:T(8,128)(2,1)S(1)}, bf16[768,640]{1,0:T(8,128)(2,1)S(1)}) custom-call(bf16[112,384]{1,0:T(8,128)(2,1)S(1)} %collective-permute-done.17.refs_0_, ...), custom_call_target="tpu_custom_call", output_to_operand_aliasing={{0}: (9, {})} | custom-call | flops 10000000000 | tf_op jit(solution)/shard_map/pallas_call | solution.py:114
  87.4 1.9 %collective-permute-done.21.refs_1_ = bf16[2,6,64,768]{3,2,1,0:T(8,128)(2,1)S(1)} collective-permute-done((bf16[2,6,64,768]{3,2,1,0:T(8,128)(2,1)S(1)}, bf16[2,6,64,768]{3,2,1,0:T(8,128)(2,1)S(1)}, u32[]{:S(2)}, u32[]{:S(2)}) %collective-permute-start.21) | collective-permute-done | bytes 1179680 | tf_op jit(solution)/shard_map/ppermute | solution.py:681
  89.5 3.3 %shard_map.276 = (f32[1,768,3072]{2,1,0:T(8,128)}, f32[1,3072,768]{2,1,0:T(8,128)}) custom-call(bf16[32,2,768]{2,1,0:T(2,128)(2,1)S(1)} %all_to_all.10.refs_0_.x_ref, bf16[32,3072]{1,0:T(8,128)(2,1)S(1)} %get-tuple-element.188.hid_ref, bf16[32,3072]{1,0:T(8,128)(2,1)S(1)} %get-tuple-element.189.pre_ref), custom_call_target="tpu_custom_call" | custom-call | flops 99999997952 | tf_op jit(solution)/shard_map/pallas_call | solution.py:791
  94.7 5.4 %shard_map.278 = (f32[1,768,3072]{2,1,0:T(8,128)}, f32[1,3072,768]{2,1,0:T(8,128)}) custom-call(bf16[32,2,768]{2,1,0:T(2,128)(2,1)S(1)} %all_to_all.10.refs_0_.x_ref, bf16[32,3072]{1,0:T(8,128)(2,1)S(1)} %get-tuple-element.188.hid_ref, bf16[32,3072]{1,0:T(8,128)(2,1)S(1)} %get-tuple-element.189.pre_ref, ...), custom_call_target="tpu_custom_call", output_to_operand_aliasing={{0}: (3, {}), {1}: (4, {})} | custom-call | flops 1 | tf_op jit(solution)/shard_map/pallas_call | solution.py:791
  102.0 5.3 %collective-permute-done.28.refs_0_ = bf16[96,832]{1,0:T(8,128)(2,1)S(1)} collective-permute-done((bf16[96,832]{1,0:T(8,128)(2,1)S(1)}, bf16[96,832]{1,0:T(8,128)(2,1)S(1)}, u32[]{:S(2)}, u32[]{:S(2)}) %collective-permute-start.28) | collective-permute-done | bytes 159776 | tf_op jit(solution)/shard_map/ppermute | solution.py:681
  109.0 2.9 %collective-permute-start.33 = (bf16[96,832]{1,0:T(8,128)(2,1)S(1)}, bf16[96,832]{1,0:T(8,128)(2,1)S(1)}, u32[]{:S(2)}, u32[]{:S(2)}) collective-permute-start(bf16[96,832]{1,0:T(8,128)(2,1)S(1)} %shard_map.280.refs_0_), channel_id=1, source_target_pairs={{0,2},{1,3},{2,0},{3,1},{4,6},{5,7},{6,4},{7,5},{8,10},{9,11},{10,... | collective-permute-start | bytes 479240 | tf_op jit(solution)/shard_map/ppermute | solution.py:681
  114.8 2.8 %collective-permute-start.34 = (bf16[96,832]{1,0:T(8,128)(2,1)S(1)}, bf16[96,832]{1,0:T(8,128)(2,1)S(1)}, u32[]{:S(2)}, u32[]{:S(2)}) collective-permute-start(bf16[96,832]{1,0:T(8,128)(2,1)S(1)} %collective-permute-done.33.refs_2_), channel_id=1, source_target_pairs={{0,1},{1,0},{2,3},{3,2},{4,5},{5,4},{6,7},{7,6},{8,9},{9,8},{10,11... | collective-permute-start | bytes 479240 | tf_op jit(solution)/shard_map/ppermute | solution.py:681
  (95 shorter events, 29.4 us)
Async XLA Ops:
  0.7 16.7 %collective-permute-start.3 = (bf16[4,64,768]{2,1,0:T(8,128)(2,1)}, bf16[4,64,768]{2,1,0:T(8,128)(2,1)S(1)}, u32[]{:S(2)}, u32[]{:S(2)}) collective-permute-start(bf16[4,64,768]{2,1,0:T(8,128)(2,1)} %refs_3_.3), channel_id=1, source_target_pairs={{0,2},{1,3},{2,0},{3,1},{4,6},{5,7},{6,4},{7,5},{8,10},{9,11},{10,... | collective-permute-start | bytes 1179656 | tf_op jit(solution)/shard_map/ppermute | solution.py:681
  4.9 12.4 %collective-permute-start = (bf16[96,1024]{1,0:T(8,128)(2,1)}, bf16[96,1024]{1,0:T(8,128)(2,1)S(1)}, u32[]{:S(2)}, u32[]{:S(2)}) collective-permute-start(bf16[96,1024]{1,0:T(8,128)(2,1)} %shard_map.263.refs_3_), channel_id=1, source_target_pairs={{0,16},{4,20},{8,24},{12,28},{16,0},{20,4},{24,8},{28,12},{1,17},{... | collective-permute-start | bytes 589832 | tf_op jit(solution)/shard_map/ppermute | solution.py:681
  7.3 10.1 %collective-permute-start.1 = (bf16[96,1024]{1,0:T(8,128)(2,1)}, bf16[96,1024]{1,0:T(8,128)(2,1)S(1)}, u32[]{:S(2)}, u32[]{:S(2)}) collective-permute-start(bf16[96,1024]{1,0:T(8,128)(2,1)} %shard_map.263.refs_3_), channel_id=1, source_target_pairs={{0,8},{4,12},{8,0},{12,4},{16,24},{20,28},{24,16},{28,20},{1,9},{5... | collective-permute-start | bytes 589832 | tf_op jit(solution)/shard_map/ppermute | solution.py:681
  8.6 8.8 %collective-permute-start.2 = (bf16[96,1024]{1,0:T(8,128)(2,1)}, bf16[96,1024]{1,0:T(8,128)(2,1)S(1)}, u32[]{:S(2)}, u32[]{:S(2)}) collective-permute-start(bf16[96,1024]{1,0:T(8,128)(2,1)} %shard_map.263.refs_3_), channel_id=1, source_target_pairs={{0,4},{4,0},{8,12},{12,8},{16,20},{20,16},{24,28},{28,24},{1,5},{5... | collective-permute-start | bytes 589832 | tf_op jit(solution)/shard_map/ppermute | solution.py:681
  14.7 12.3 %collective-permute-start.7 = (bf16[4,64,768]{2,1,0:T(8,128)(2,1)}, bf16[4,64,768]{2,1,0:T(8,128)(2,1)S(1)}, u32[]{:S(2)}, u32[]{:S(2)}) collective-permute-start(bf16[4,64,768]{2,1,0:T(8,128)(2,1)} %refs_3_.3), channel_id=1, source_target_pairs={{0,1},{1,0},{2,3},{3,2},{4,5},{5,4},{6,7},{7,6},{8,9},{9,8},{10,11... | collective-permute-start | bytes 1179656 | tf_op jit(solution)/shard_map/ppermute | solution.py:681
  17.4 12.4 %collective-permute-start.10 = (bf16[4,64,768]{2,1,0:T(8,128)(2,1)S(1)}, bf16[4,64,768]{2,1,0:T(8,128)(2,1)S(1)}, u32[]{:S(2)}, u32[]{:S(2)}) collective-permute-start(bf16[4,64,768]{2,1,0:T(8,128)(2,1)S(1)} %collective-permute-done.3.refs_2_), channel_id=1, source_target_pairs={{0,1},{1,0},{2,3},{3,2},{4,5},{5,4},{6,7},{7,6},{8,9},{9,8},{10,11... | collective-permute-start | bytes 1179656 | tf_op jit(solution)/shard_map/ppermute | solution.py:681
  18.0 9.0 %collective-permute-start.5 = (bf16[144,1024]{1,0:T(8,128)(2,1)S(1)}, bf16[144,1024]{1,0:T(8,128)(2,1)S(1)}, u32[]{:S(2)}, u32[]{:S(2)}) collective-permute-start(bf16[144,1024]{1,0:T(8,128)(2,1)S(1)} %get-tuple-element.123), channel_id=1, source_target_pairs={{0,4},{4,0},{8,12},{12,8},{16,20},{20,16},{24,28},{28,24},{1,5},{5... | collective-permute-start | bytes 884744 | tf_op jit(solution)/shard_map/ppermute | solution.py:681
  19.3 8.3 %collective-permute-start.6 = (bf16[144,1024]{1,0:T(8,128)(2,1)S(1)}, bf16[144,1024]{1,0:T(8,128)(2,1)S(1)}, u32[]{:S(2)}, u32[]{:S(2)}) collective-permute-start(bf16[144,1024]{1,0:T(8,128)(2,1)S(1)} %get-tuple-element.124), channel_id=1, source_target_pairs={{0,8},{4,12},{8,0},{12,4},{16,24},{20,28},{24,16},{28,20},{1,9},{5... | collective-permute-start | bytes 884744 | tf_op jit(solution)/shard_map/ppermute | solution.py:681
  22.0 5.1 %collective-permute-start.9 = (bf16[64,768]{1,0:T(8,128)(2,1)S(1)}, bf16[64,768]{1,0:T(8,128)(2,1)S(1)}, u32[]{:S(2)}, u32[]{:S(2)}) collective-permute-start(bf16[64,768]{1,0:T(8,128)(2,1)S(1)} %get-tuple-element.126), channel_id=1, source_target_pairs={{0,3},{1,2},{2,1},{3,0},{4,7},{5,6},{6,5},{7,4},{8,11},{9,10},{10,... | collective-permute-start | bytes 294920 | tf_op jit(solution)/shard_map/ppermute | solution.py:681
  35.0 8.7 %collective-permute-start.16 = (bf16[768,384]{1,0:T(8,128)(2,1)S(1)}, bf16[768,384]{1,0:T(8,128)(2,1)S(1)}, u32[]{:S(2)}, u32[]{:S(2)}) collective-permute-start(bf16[768,384]{1,0:T(8,128)(2,1)S(1)} %get-tuple-element.145.refs_13_), channel_id=1, source_target_pairs={{0,1},{1,0},{2,3},{3,2},{4,5},{5,4},{6,7},{7,6},{8,9},{9,8},{10,11... | collective-permute-start | bytes 1769480 | tf_op jit(solution)/shard_map/ppermute | solution.py:681
  37.8 5.9 %collective-permute-start.15 = (bf16[112,384]{1,0:T(8,128)(2,1)S(1)}, bf16[112,384]{1,0:T(8,128)(2,1)S(1)}, u32[]{:S(2)}, u32[]{:S(2)}) collective-permute-start(bf16[112,384]{1,0:T(8,128)(2,1)S(1)} %get-tuple-element.137), channel_id=1, source_target_pairs={{0,3},{1,2},{2,1},{3,0},{4,7},{5,6},{6,5},{7,4},{8,11},{9,10},{10,... | collective-permute-start | bytes 258056 | tf_op jit(solution)/shard_map/ppermute | solution.py:681
  75.5 6.8 %collective-permute-start.18 = (bf16[112,384]{1,0:T(8,128)(2,1)S(1)}, bf16[112,384]{1,0:T(8,128)(2,1)S(1)}, u32[]{:S(2)}, u32[]{:S(2)}) collective-permute-start(bf16[112,384]{1,0:T(8,128)(2,1)S(1)} %get-tuple-element.155), channel_id=1, source_target_pairs={{0,3},{1,2},{2,1},{3,0},{4,7},{5,6},{6,5},{7,4},{8,11},{9,10},{10,... | collective-permute-start | bytes 258056 | tf_op jit(solution)/shard_map/ppermute | solution.py:681
  77.6 8.9 %collective-permute-start.22 = (bf16[192,384]{1,0:T(8,128)(2,1)S(1)}, bf16[192,384]{1,0:T(8,128)(2,1)S(1)}, u32[]{:S(2)}, u32[]{:S(2)}) collective-permute-start(bf16[192,384]{1,0:T(8,128)(2,1)S(1)} %get-tuple-element.176), channel_id=1, source_target_pairs={{0,2},{1,3},{2,0},{3,1},{4,6},{5,7},{6,4},{7,5},{8,10},{9,11},{10,... | collective-permute-start | bytes 442376 | tf_op jit(solution)/shard_map/ppermute | solution.py:681
  86.6 6.2 %collective-permute-start.23 = (bf16[48,832]{1,0:T(8,128)(2,1)S(1)}, bf16[48,832]{1,0:T(8,128)(2,1)S(1)}, u32[]{:S(2)}, u32[]{:S(2)}) collective-permute-start(bf16[48,832]{1,0:T(8,128)(2,1)S(1)} %get-tuple-element.184), channel_id=1, source_target_pairs={{0,4},{4,0},{8,12},{12,8},{16,20},{20,16},{24,28},{28,24},{1,5},{5... | collective-permute-start | bytes 239624 | tf_op jit(solution)/shard_map/ppermute | solution.py:681
  87.0 5.8 %collective-permute-start.24 = (bf16[48,832]{1,0:T(8,128)(2,1)S(1)}, bf16[48,832]{1,0:T(8,128)(2,1)S(1)}, u32[]{:S(2)}, u32[]{:S(2)}) collective-permute-start(bf16[48,832]{1,0:T(8,128)(2,1)S(1)} %get-tuple-element.185), channel_id=1, source_target_pairs={{0,8},{4,12},{8,0},{12,4},{16,24},{20,28},{24,16},{28,20},{1,9},{5... | collective-permute-start | bytes 239624 | tf_op jit(solution)/shard_map/ppermute | solution.py:681
  87.3 5.5 %collective-permute-start.25 = (bf16[192,384]{1,0:T(8,128)(2,1)S(1)}, bf16[192,384]{1,0:T(8,128)(2,1)S(1)}, u32[]{:S(2)}, u32[]{:S(2)}) collective-permute-start(bf16[192,384]{1,0:T(8,128)(2,1)S(1)} %get-tuple-element.187), channel_id=1, source_target_pairs={{0,2},{1,3},{2,0},{3,1},{4,6},{5,7},{6,4},{7,5},{8,10},{9,11},{10,... | collective-permute-start | bytes 442376 | tf_op jit(solution)/shard_map/ppermute | solution.py:681
  89.4 19.6 %collective-permute-start.31 = (bf16[8,64,768]{2,1,0:T(8,128)(2,1)S(1)}, bf16[8,64,768]{2,1,0:T(8,128)(2,1)S(1)}, u32[]{:S(2)}, u32[]{:S(2)}) collective-permute-start(bf16[8,64,768]{2,1,0:T(8,128)(2,1)S(1)} %shard_map.281), channel_id=1, source_target_pairs={{0,2},{1,3},{2,0},{3,1},{4,6},{5,7},{6,4},{7,5},{8,10},{9,11},{10,... | collective-permute-start | bytes 2359304 | tf_op jit(solution)/shard_map/ppermute | solution.py:681
  92.9 7.2 %collective-permute-start.26 = (bf16[144,832]{1,0:T(8,128)(2,1)S(1)}, bf16[144,832]{1,0:T(8,128)(2,1)S(1)}, u32[]{:S(2)}, u32[]{:S(2)}) collective-permute-start(bf16[144,832]{1,0:T(8,128)(2,1)S(1)} %get-tuple-element.194), channel_id=1, source_target_pairs={{0,4},{4,0},{8,12},{12,8},{16,20},{20,16},{24,28},{28,24},{1,5},{5... | collective-permute-start | bytes 718856 | tf_op jit(solution)/shard_map/ppermute | solution.py:681
  93.6 6.5 %collective-permute-start.27 = (bf16[144,832]{1,0:T(8,128)(2,1)S(1)}, bf16[144,832]{1,0:T(8,128)(2,1)S(1)}, u32[]{:S(2)}, u32[]{:S(2)}) collective-permute-start(bf16[144,832]{1,0:T(8,128)(2,1)S(1)} %get-tuple-element.195), channel_id=1, source_target_pairs={{0,8},{4,12},{8,0},{12,4},{16,24},{20,28},{24,16},{28,20},{1,9},{5... | collective-permute-start | bytes 718856 | tf_op jit(solution)/shard_map/ppermute | solution.py:681
  100.3 7.1 %collective-permute-start.28 = (bf16[96,832]{1,0:T(8,128)(2,1)S(1)}, bf16[96,832]{1,0:T(8,128)(2,1)S(1)}, u32[]{:S(2)}, u32[]{:S(2)}) collective-permute-start(bf16[96,832]{1,0:T(8,128)(2,1)S(1)} %get-tuple-element.204), channel_id=1, source_target_pairs={{0,16},{4,20},{8,24},{12,28},{16,0},{20,4},{24,8},{28,12},{1,17},{... | collective-permute-start | bytes 479240 | tf_op jit(solution)/shard_map/ppermute | solution.py:681
  100.8 6.5 %collective-permute-start.29 = (bf16[96,832]{1,0:T(8,128)(2,1)S(1)}, bf16[96,832]{1,0:T(8,128)(2,1)S(1)}, u32[]{:S(2)}, u32[]{:S(2)}) collective-permute-start(bf16[96,832]{1,0:T(8,128)(2,1)S(1)} %get-tuple-element.205), channel_id=1, source_target_pairs={{0,8},{4,12},{8,0},{12,4},{16,24},{20,28},{24,16},{28,20},{1,9},{5... | collective-permute-start | bytes 479240 | tf_op jit(solution)/shard_map/ppermute | solution.py:681
  101.5 5.9 %collective-permute-start.30 = (bf16[96,832]{1,0:T(8,128)(2,1)S(1)}, bf16[96,832]{1,0:T(8,128)(2,1)S(1)}, u32[]{:S(2)}, u32[]{:S(2)}) collective-permute-start(bf16[96,832]{1,0:T(8,128)(2,1)S(1)} %get-tuple-element.206), channel_id=1, source_target_pairs={{0,4},{4,0},{8,12},{12,8},{16,20},{20,16},{24,28},{28,24},{1,5},{5... | collective-permute-start | bytes 479240 | tf_op jit(solution)/shard_map/ppermute | solution.py:681
  109.0 5.7 %collective-permute-start.33 = (bf16[96,832]{1,0:T(8,128)(2,1)S(1)}, bf16[96,832]{1,0:T(8,128)(2,1)S(1)}, u32[]{:S(2)}, u32[]{:S(2)}) collective-permute-start(bf16[96,832]{1,0:T(8,128)(2,1)S(1)} %shard_map.280.refs_0_), channel_id=1, source_target_pairs={{0,2},{1,3},{2,0},{3,1},{4,6},{5,7},{6,4},{7,5},{8,10},{9,11},{10,... | collective-permute-start | bytes 479240 | tf_op jit(solution)/shard_map/ppermute | solution.py:681
  112.0 7.1 %collective-permute-start.32 = (bf16[96,832]{1,0:T(8,128)(2,1)S(1)}, bf16[96,832]{1,0:T(8,128)(2,1)S(1)}, u32[]{:S(2)}, u32[]{:S(2)}) collective-permute-start(bf16[96,832]{1,0:T(8,128)(2,1)S(1)} %shard_map.280.refs_0_), channel_id=1, source_target_pairs={{0,1},{1,0},{2,3},{3,2},{4,5},{5,4},{6,7},{7,6},{8,9},{9,8},{10,11... | collective-permute-start | bytes 479240 | tf_op jit(solution)/shard_map/ppermute | solution.py:681
  (23 other events, 270.0 us)

commit v3 on v2

--- a/solution.py
+++ b/solution.py
@@ -276,7 +276,7 @@
 
 def route_forward(groups, here, half):
     def kernel(*refs):
-        sent_refs = refs[:groups]
+        sent_refs = [refs[0], *refs[groups - 1 : 0 : -1]]
         cot_refs = refs[groups : 2 * groups]
         mine_ref, rows_ref, router_ref, mask_ref, counts_ref = refs[2 * groups : 2 * groups + 5]
         half_refs = refs[2 * groups + 5 : -8]
@@ -485,7 +485,7 @@
     heads_here = HEADS // groups
 
     def kernel(*refs):
-        gheads_refs = refs[: groups - 2]
+        gheads_refs = refs[groups - 3 :: -1]
         qkv_ref, probs_ref, xa_ref, unit_ref, wpad_ref, misc_ref, token_ref = refs[
             groups - 2 : groups + 5
         ]
@@ -752,7 +752,7 @@
     mix_half, probs, xa, qkv, wpad, rows, router_full = outs[groups:]
     slots, resid, mixed, logits, mix_full, grad, heads = kernel_call(
         route_forward(groups, here, half),
-        sent
+        [sent[0], *sent[:0:-1]]
         + cots
         + [mine, rows, router_full, pad_mask, counts, mix_half, swap(mix_half, "seq", 1)],
         [
@@ -855,7 +855,7 @@
     )
     gqkv, gx, gx_send, gw = kernel_call(
         attend_backward_far(groups, here, wide, misc_w, experts),
-        gheads[2:] + [qkv, probs, xa, units, wpad, misc, token_rows, gqkv],
+        gheads[:1:-1] + [qkv, probs, xa, units, wpad, misc, token_rows, gqkv],
         [
             gqkv_spec,
             ((2, images + 2, shard, features), BF16),

time: 121 us -> 121 us (level)
  waiting for transfers between devices: 27.5 us -> 25.6 us
  starting transfers between devices: 34.6 us -> 36.4 us
    ppermute x35, waiting for transfers between devices: 27.5 us -> 25.6 us  [swap(): lax.ppermute(a, axis, [(i, i ^ step) for i in range(lax.axis_size(axis))])]
    ppermute x35, starting transfers between devices: 34.6 us -> 36.4 us  [swap(): lax.ppermute(a, axis, [(i, i ^ step) for i in range(lax.axis_size(axis))])]
  transfers between devices with their start and end apart: 35 -> 35, of which waited for: 13 -> 14; matrix products, arithmetic and copies ran while one was open for 0% -> 0% of each run, Pallas kernels for 17% -> 16%
where the time goes in v3:
time: 121 us; the launch traced here: 120 us
  starting transfers between devices  36.4 us (30%)
  Pallas kernels  33.6 us (28%)
  waiting for transfers between devices  25.6 us (21%)
  blocking collectives  22.3 us (18%)
  between operations  1.57 us (1%)
    ppermute x35, starting transfers between devices, swap(): lax.ppermute(a, axis, [(i, i ^ step) for i in range(lax.axis_size(axis))])  36.4 us
    ppermute x35, waiting for transfers between devices, swap(): lax.ppermute(a, axis, [(i, i ^ step) for i in range(lax.axis_size(axis))])  25.6 us
    pallas_call x19, Pallas kernels, kernel_call(): return list(call(*ins))  24.9 us
    all_to_all x1, blocking collectives, body(): lax.all_to_all(slots, ('dp', 'seq'), split_axis=0, concat_axis=0, tiled=T...  12.8 us
    all_to_all x1, blocking collectives, body(): lax.all_to_all(back, ('dp', 'seq'), split_axis=0, concat_axis=0, tiled=True)  9.49 us
    pallas_call x2, Pallas kernels, expert_gradients(): pl.pallas_call(expert_weights, grid=(count,), in_specs=[pl.BlockSpec((dev...  8.69 us
  transfers between devices with their start and end apart: 35, of which 14 were waited for; matrix products, arithmetic and copies ran while one was open for 0% of the time, Pallas kernels for 16%

profile of v3, /device:TPU:1, one launch (start us, length us, event | category | flops | bytes accessed | tf_op | source)
XLA Modules:
  0.0 120.5 jit_solution(13919435310084566076)
XLA Ops:
  0.7 2.1 %collective-permute-start.3 = (bf16[4,64,768]{2,1,0:T(8,128)(2,1)}, bf16[4,64,768]{2,1,0:T(8,128)(2,1)S(1)}, u32[]{:S(2)}, u32[]{:S(2)}) collective-permute-start(bf16[4,64,768]{2,1,0:T(8,128)(2,1)} %refs_3_.3), channel_id=1, source_target_pairs={{0,2},{1,3},{2,0},{3,1},{4,6},{5,7},{6,4},{7,5},{8,10},{9,11},{10,... | collective-permute-start | bytes 1179656 | tf_op jit(solution)/shard_map/ppermute | solution.py:681
  2.8 2.1 %shard_map.263.refs_3_ = bf16[96,1024]{1,0:T(8,128)(2,1)} custom-call(bf16[96,2304]{1,0:T(8,128)(2,1)} %refs_0_.3, bf16[32,96]{1,0:T(8,128)(2,1)} %bitcast.16, bf16[1,96]{1,0:T(2,128)(2,1)} %bitcast.17, bf16[1,96]{1,0:T(2,128)(2,1)} %bitcast.18, bf16[1,96]{1,0:T(2,128)(2,1)} %bitcast.19, bf16[1,96]{1,0:T(2,128)(2,1)} %bitcast.20, bf16[1,96]{1,0:T(2,128)(2,1)} %bitcast.21, ...), custom_call_target="tpu_custom_call" | custom-call | flops 1 | tf_op jit(solution)/shard_map/pallas_call | solution.py:114
  4.9 2.4 %collective-permute-start = (bf16[96,1024]{1,0:T(8,128)(2,1)}, bf16[96,1024]{1,0:T(8,128)(2,1)S(1)}, u32[]{:S(2)}, u32[]{:S(2)}) collective-permute-start(bf16[96,1024]{1,0:T(8,128)(2,1)} %shard_map.263.refs_3_), channel_id=1, source_target_pairs={{0,16},{4,20},{8,24},{12,28},{16,0},{20,4},{24,8},{28,12},{1,17},{... | collective-permute-start | bytes 589832 | tf_op jit(solution)/shard_map/ppermute | solution.py:681
  11.2 3.5 %collective-permute-done.4.refs_6_ = bf16[64,768]{1,0:T(8,128)(2,1)S(1)} collective-permute-done((bf16[64,768]{1,0:T(8,128)(2,1)S(1)}, bf16[64,768]{1,0:T(8,128)(2,1)S(1)}, u32[]{:S(2)}, u32[]{:S(2)}) %collective-permute-start.4) | collective-permute-done | bytes 98336 | tf_op jit(solution)/shard_map/ppermute | solution.py:681
  14.7 2.6 %collective-permute-start.7 = (bf16[4,64,768]{2,1,0:T(8,128)(2,1)}, bf16[4,64,768]{2,1,0:T(8,128)(2,1)S(1)}, u32[]{:S(2)}, u32[]{:S(2)}) collective-permute-start(bf16[4,64,768]{2,1,0:T(8,128)(2,1)} %refs_3_.3), channel_id=1, source_target_pairs={{0,1},{1,0},{2,3},{3,2},{4,5},{5,4},{6,7},{7,6},{8,9},{9,8},{10,11... | collective-permute-start | bytes 1179656 | tf_op jit(solution)/shard_map/ppermute | solution.py:681
  22.5 4.6 %collective-permute-done.9.refs_7_ = bf16[64,768]{1,0:T(8,128)(2,1)S(1)} collective-permute-done((bf16[64,768]{1,0:T(8,128)(2,1)S(1)}, bf16[64,768]{1,0:T(8,128)(2,1)S(1)}, u32[]{:S(2)}, u32[]{:S(2)}) %collective-permute-start.9) | collective-permute-done | bytes 98336 | tf_op jit(solution)/shard_map/ppermute | solution.py:681
  31.5 3.5 %shard_map.268 = (bf16[112,384]{1,0:T(8,128)(2,1)S(1)}, bf16[112,384]{1,0:T(8,128)(2,1)S(1)}, bf16[112,384]{1,0:T(8,128)(2,1)S(1)}, bf16[112,384]{1,0:T(8,128)(2...) custom-call(f32[4,208,768]{2,1,0:T(8,128)S(1)} %get-tuple-element.12, ...), custom_call_target="tpu_custom_call" | custom-call | flops 100000000 | tf_op jit(solution)/shard_map/pallas_call | solution.py:114
  35.0 2.5 %collective-permute-start.16 = (bf16[768,384]{1,0:T(8,128)(2,1)S(1)}, bf16[768,384]{1,0:T(8,128)(2,1)S(1)}, u32[]{:S(2)}, u32[]{:S(2)}) collective-permute-start(bf16[768,384]{1,0:T(8,128)(2,1)S(1)} %get-tuple-element.145.refs_13_), channel_id=1, source_target_pairs={{0,1},{1,0},{2,3},{3,2},{4,5},{5,4},{6,7},{7,6},{8,9},{9,8},{10,11... | collective-permute-start | bytes 1769480 | tf_op jit(solution)/shard_map/ppermute | solution.py:681
  39.7 2.6 %collective-permute-done.13.refs_1_ = bf16[112,384]{1,0:T(8,128)(2,1)S(1)} collective-permute-done((bf16[112,384]{1,0:T(8,128)(2,1)S(1)}, bf16[112,384]{1,0:T(8,128)(2,1)S(1)}, u32[]{:S(2)}, u32[]{:S(2)}) %collective-permute-start.13) | collective-permute-done | bytes 86048 | tf_op jit(solution)/shard_map/ppermute | solution.py:681
  43.3 1.6 %shard_map.269 = (bf16[32,2,768]{2,1,0:T(2,128)(2,1)S(1)}, f32[208,768]{1,0:T(8,128)S(1)}, bf16[208,768]{1,0:T(8,128)(2,1)S(1)}, f32[208,32]{1,0:T(8,128)S(1)}, ...) custom-call(bf16[112,384]{1,0:T(8,128)(2,1)S(1)} %get-tuple-element.134.refs_0_, ...), custom_call_target="tpu_custom_call" | custom-call | flops 5000000000 | tf_op jit(solution)/shard_map/pallas_call | solution.py:114
  45.0 12.8 %all_to_all.10.refs_0_.x_ref = bf16[32,2,768]{2,1,0:T(2,128)(2,1)S(1)} all-to-all(bf16[32,2,768]{2,1,0:T(2,128)(2,1)S(1)} %get-tuple-element.146), channel_id=1, replica_groups=mesh['dp'=8,'seq'=4] {'dp','seq'}, dimensions={0} | all-to-all | bytes 196608 | tf_op jit(solution)/shard_map/all_to_all | solution.py:772
  57.8 5.0 %shard_map.270 = (bf16[32,2,768]{2,1,0:T(2,128)(2,1)S(1)}, bf16[32,3072]{1,0:T(8,128)(2,1)S(1)}, bf16[32,3072]{1,0:T(8,128)(2,1)S(1)}, f32[1,3072]{1,0:T(1,128)}, f32[1,768]{1,0:T(1,128)}) custom-call(bf16[32,2,768]{2,1,0:T(2,128)(2,1)S(1)} %all_to_all.10.refs_0_.x_ref, bf16[1,768,3072]{2,1,0:T(8,128)(2,1)S(1)} %bitcast.13, bf16[1,3072]{1,0:T(2,128)(2,1)S(1)} %copy-done.6, ...), custom_call_target="tpu_custom_call" | custom-call | flops 5000000000 | tf_op jit(solution)/shard_map/pallas_call | solution.py:114
  62.8 9.5 %all_to_all.11.refs_0_ = bf16[32,2,768]{2,1,0:T(2,128)(2,1)S(1)} all-to-all(bf16[32,2,768]{2,1,0:T(2,128)(2,1)S(1)} %get-tuple-element.147), channel_id=1, replica_groups=mesh['dp'=8,'seq'=4] {'dp','seq'}, dimensions={0} | all-to-all | bytes 196608 | tf_op jit(solution)/shard_map/all_to_all | solution.py:787
  72.3 2.4 %shard_map.271 = (bf16[112,384]{1,0:T(8,128)(2,1)S(1)}, bf16[112,384]{1,0:T(8,128)(2,1)S(1)}, bf16[112,384]{1,0:T(8,128)(2,1)S(1)}, bf16[112,384]{1,0:T(8,128)(2...) custom-call(bf16[32,2,768]{2,1,0:T(2,128)(2,1)S(1)} %all_to_all.11.r, ...), custom_call_target="tpu_custom_call" | custom-call | flops 5000000000 | tf_op jit(solution)/shard_map/pallas_call | solution.py:114
  75.6 1.4 %collective-permute-start.18 = (bf16[112,384]{1,0:T(8,128)(2,1)S(1)}, bf16[112,384]{1,0:T(8,128)(2,1)S(1)}, u32[]{:S(2)}, u32[]{:S(2)}) collective-permute-start(bf16[112,384]{1,0:T(8,128)(2,1)S(1)} %get-tuple-element.155), channel_id=1, source_target_pairs={{0,2},{1,3},{2,0},{3,1},{4,6},{5,7},{6,4},{7,5},{8,10},{9,11},{10,... | collective-permute-start | bytes 258056 | tf_op jit(solution)/shard_map/ppermute | solution.py:681
  77.5 1.5 %shard_map.273.refs_9_ = bf16[832,768]{1,0:T(8,128)(2,1)S(1)} custom-call(bf16[112,384]{1,0:T(8,128)(2,1)S(1)} %get-tuple-element.170.refs_0_, bf16[112,384]{1,0:T(8,128)(2,1)S(1)} %collective-permute-done.20.refs_1_, bf16[4,256,768]{2,1,0:T(8,128)(2,1)S(1)} %get-tuple-element.156.refs_2_, bf16[4,208,768]{2,1,0:T(8,128)(2,1)S(1)} %get-tuple-element.157.refs_3_), custom_call_target="tpu_custom_call" | custom-call | flops 10000000000 | tf_op jit(solution)/shard_map/pallas_call | solution.py:114
  80.2 1.5 %collective-permute-done.18.refs_1_ = bf16[112,384]{1,0:T(8,128)(2,1)S(1)} collective-permute-done((bf16[112,384]{1,0:T(8,128)(2,1)S(1)}, bf16[112,384]{1,0:T(8,128)(2,1)S(1)}, u32[]{:S(2)}, u32[]{:S(2)}) %collective-permute-start.18) | collective-permute-done | bytes 86048 | tf_op jit(solution)/shard_map/ppermute | solution.py:681
  81.6 4.2 %shard_map.274 = (bf16[832,768]{1,0:T(8,128)(2,1)S(1)}, bf16[2,6,64,768]{3,2,1,0:T(8,128)(2,1)S(1)}, bf16[2,6,64,768]{3,2,1,0:T(8,128)(2,1)S(1)}, bf16[768,640]{1,0:T(8,128)(2,1)S(1)}) custom-call(bf16[112,384]{1,0:T(8,128)(2,1)S(1)} %collective-permute-done.17.refs_0_, ...), custom_call_target="tpu_custom_call", output_to_operand_aliasing={{0}: (9, {})} | custom-call | flops 10000000000 | tf_op jit(solution)/shard_map/pallas_call | solution.py:114
  89.6 3.3 %shard_map.276 = (f32[1,768,3072]{2,1,0:T(8,128)}, f32[1,3072,768]{2,1,0:T(8,128)}) custom-call(bf16[32,2,768]{2,1,0:T(2,128)(2,1)S(1)} %all_to_all.10.refs_0_.x_ref, bf16[32,3072]{1,0:T(8,128)(2,1)S(1)} %get-tuple-element.188.hid_ref, bf16[32,3072]{1,0:T(8,128)(2,1)S(1)} %get-tuple-element.189.pre_ref), custom_call_target="tpu_custom_call" | custom-call | flops 99999997952 | tf_op jit(solution)/shard_map/pallas_call | solution.py:791
  95.1 5.4 %shard_map.278 = (f32[1,768,3072]{2,1,0:T(8,128)}, f32[1,3072,768]{2,1,0:T(8,128)}) custom-call(bf16[32,2,768]{2,1,0:T(2,128)(2,1)S(1)} %all_to_all.10.refs_0_.x_ref, bf16[32,3072]{1,0:T(8,128)(2,1)S(1)} %get-tuple-element.188.hid_ref, bf16[32,3072]{1,0:T(8,128)(2,1)S(1)} %get-tuple-element.189.pre_ref, ...), custom_call_target="tpu_custom_call", output_to_operand_aliasing={{0}: (3, {}), {1}: (4, {})} | custom-call | flops 1 | tf_op jit(solution)/shard_map/pallas_call | solution.py:791
  102.2 6.1 %collective-permute-done.28.refs_0_ = bf16[96,832]{1,0:T(8,128)(2,1)S(1)} collective-permute-done((bf16[96,832]{1,0:T(8,128)(2,1)S(1)}, bf16[96,832]{1,0:T(8,128)(2,1)S(1)}, u32[]{:S(2)}, u32[]{:S(2)}) %collective-permute-start.28) | collective-permute-done | bytes 159776 | tf_op jit(solution)/shard_map/ppermute | solution.py:681
  109.9 3.1 %collective-permute-start.32 = (bf16[96,832]{1,0:T(8,128)(2,1)S(1)}, bf16[96,832]{1,0:T(8,128)(2,1)S(1)}, u32[]{:S(2)}, u32[]{:S(2)}) collective-permute-start(bf16[96,832]{1,0:T(8,128)(2,1)S(1)} %shard_map.280.refs_0_), channel_id=1, source_target_pairs={{0,1},{1,0},{2,3},{3,2},{4,5},{5,4},{6,7},{7,6},{8,9},{9,8},{10,11... | collective-permute-start | bytes 479240 | tf_op jit(solution)/shard_map/ppermute | solution.py:681
  113.7 4.1 %collective-permute-start.34 = (bf16[96,832]{1,0:T(8,128)(2,1)S(1)}, bf16[96,832]{1,0:T(8,128)(2,1)S(1)}, u32[]{:S(2)}, u32[]{:S(2)}) collective-permute-start(bf16[96,832]{1,0:T(8,128)(2,1)S(1)} %collective-permute-done.33.refs_2_), channel_id=1, source_target_pairs={{0,1},{1,0},{2,3},{3,2},{4,5},{5,4},{6,7},{7,6},{8,9},{9,8},{10,11... | collective-permute-start | bytes 479240 | tf_op jit(solution)/shard_map/ppermute | solution.py:681
  117.8 1.5 %shard_map.282 = (bf16[4,64,768]{2,1,0:T(8,128)(2,1)}, bf16[4,64,768]{2,1,0:T(8,128)(2,1)}) custom-call(bf16[2,6,64,768]{3,2,1,0:T(8,128)(2,1)S(1)} %get-tuple-element.172.refs_0_, bf16[2,6,64,768]{3,2,1,0:T(8,128)(2,1)S(1)} %collective-permute-done.21.refs_1_, bf16[8,64,768]{2,1,0:T(8,128)(2,1)S(1)} %collective-permute-done.31.refs_2_, ...), custom_call_target="tpu_custom_call" | custom-call | flops 2000000000 | tf_op jit(solution)/shard_map/pallas_call | solution.py:114
  (95 shorter events, 29.6 us)
Async XLA Ops:
  0.7 16.7 %collective-permute-start.3 = (bf16[4,64,768]{2,1,0:T(8,128)(2,1)}, bf16[4,64,768]{2,1,0:T(8,128)(2,1)S(1)}, u32[]{:S(2)}, u32[]{:S(2)}) collective-permute-start(bf16[4,64,768]{2,1,0:T(8,128)(2,1)} %refs_3_.3), channel_id=1, source_target_pairs={{0,2},{1,3},{2,0},{3,1},{4,6},{5,7},{6,4},{7,5},{8,10},{9,11},{10,... | collective-permute-start | bytes 1179656 | tf_op jit(solution)/shard_map/ppermute | solution.py:681
  4.9 12.4 %collective-permute-start = (bf16[96,1024]{1,0:T(8,128)(2,1)}, bf16[96,1024]{1,0:T(8,128)(2,1)S(1)}, u32[]{:S(2)}, u32[]{:S(2)}) collective-permute-start(bf16[96,1024]{1,0:T(8,128)(2,1)} %shard_map.263.refs_3_), channel_id=1, source_target_pairs={{0,16},{4,20},{8,24},{12,28},{16,0},{20,4},{24,8},{28,12},{1,17},{... | collective-permute-start | bytes 589832 | tf_op jit(solution)/shard_map/ppermute | solution.py:681
  7.3 10.1 %collective-permute-start.1 = (bf16[96,1024]{1,0:T(8,128)(2,1)}, bf16[96,1024]{1,0:T(8,128)(2,1)S(1)}, u32[]{:S(2)}, u32[]{:S(2)}) collective-permute-start(bf16[96,1024]{1,0:T(8,128)(2,1)} %shard_map.263.refs_3_), channel_id=1, source_target_pairs={{0,8},{4,12},{8,0},{12,4},{16,24},{20,28},{24,16},{28,20},{1,9},{5... | collective-permute-start | bytes 589832 | tf_op jit(solution)/shard_map/ppermute | solution.py:681
  8.6 8.8 %collective-permute-start.2 = (bf16[96,1024]{1,0:T(8,128)(2,1)}, bf16[96,1024]{1,0:T(8,128)(2,1)S(1)}, u32[]{:S(2)}, u32[]{:S(2)}) collective-permute-start(bf16[96,1024]{1,0:T(8,128)(2,1)} %shard_map.263.refs_3_), channel_id=1, source_target_pairs={{0,4},{4,0},{8,12},{12,8},{16,20},{20,16},{24,28},{28,24},{1,5},{5... | collective-permute-start | bytes 589832 | tf_op jit(solution)/shard_map/ppermute | solution.py:681
  14.7 12.3 %collective-permute-start.7 = (bf16[4,64,768]{2,1,0:T(8,128)(2,1)}, bf16[4,64,768]{2,1,0:T(8,128)(2,1)S(1)}, u32[]{:S(2)}, u32[]{:S(2)}) collective-permute-start(bf16[4,64,768]{2,1,0:T(8,128)(2,1)} %refs_3_.3), channel_id=1, source_target_pairs={{0,1},{1,0},{2,3},{3,2},{4,5},{5,4},{6,7},{7,6},{8,9},{9,8},{10,11... | collective-permute-start | bytes 1179656 | tf_op jit(solution)/shard_map/ppermute | solution.py:681
  17.4 12.4 %collective-permute-start.10 = (bf16[4,64,768]{2,1,0:T(8,128)(2,1)S(1)}, bf16[4,64,768]{2,1,0:T(8,128)(2,1)S(1)}, u32[]{:S(2)}, u32[]{:S(2)}) collective-permute-start(bf16[4,64,768]{2,1,0:T(8,128)(2,1)S(1)} %collective-permute-done.3.refs_2_), channel_id=1, source_target_pairs={{0,1},{1,0},{2,3},{3,2},{4,5},{5,4},{6,7},{7,6},{8,9},{9,8},{10,11... | collective-permute-start | bytes 1179656 | tf_op jit(solution)/shard_map/ppermute | solution.py:681
  18.0 9.0 %collective-permute-start.5 = (bf16[144,1024]{1,0:T(8,128)(2,1)S(1)}, bf16[144,1024]{1,0:T(8,128)(2,1)S(1)}, u32[]{:S(2)}, u32[]{:S(2)}) collective-permute-start(bf16[144,1024]{1,0:T(8,128)(2,1)S(1)} %get-tuple-element.123), channel_id=1, source_target_pairs={{0,4},{4,0},{8,12},{12,8},{16,20},{20,16},{24,28},{28,24},{1,5},{5... | collective-permute-start | bytes 884744 | tf_op jit(solution)/shard_map/ppermute | solution.py:681
  19.3 8.3 %collective-permute-start.6 = (bf16[144,1024]{1,0:T(8,128)(2,1)S(1)}, bf16[144,1024]{1,0:T(8,128)(2,1)S(1)}, u32[]{:S(2)}, u32[]{:S(2)}) collective-permute-start(bf16[144,1024]{1,0:T(8,128)(2,1)S(1)} %get-tuple-element.124), channel_id=1, source_target_pairs={{0,8},{4,12},{8,0},{12,4},{16,24},{20,28},{24,16},{28,20},{1,9},{5... | collective-permute-start | bytes 884744 | tf_op jit(solution)/shard_map/ppermute | solution.py:681
  22.0 5.1 %collective-permute-start.9 = (bf16[64,768]{1,0:T(8,128)(2,1)S(1)}, bf16[64,768]{1,0:T(8,128)(2,1)S(1)}, u32[]{:S(2)}, u32[]{:S(2)}) collective-permute-start(bf16[64,768]{1,0:T(8,128)(2,1)S(1)} %get-tuple-element.126), channel_id=1, source_target_pairs={{0,3},{1,2},{2,1},{3,0},{4,7},{5,6},{6,5},{7,4},{8,11},{9,10},{10,... | collective-permute-start | bytes 294920 | tf_op jit(solution)/shard_map/ppermute | solution.py:681
  35.0 8.3 %collective-permute-start.16 = (bf16[768,384]{1,0:T(8,128)(2,1)S(1)}, bf16[768,384]{1,0:T(8,128)(2,1)S(1)}, u32[]{:S(2)}, u32[]{:S(2)}) collective-permute-start(bf16[768,384]{1,0:T(8,128)(2,1)S(1)} %get-tuple-element.145.refs_13_), channel_id=1, source_target_pairs={{0,1},{1,0},{2,3},{3,2},{4,5},{5,4},{6,7},{7,6},{8,9},{9,8},{10,11... | collective-permute-start | bytes 1769480 | tf_op jit(solution)/shard_map/ppermute | solution.py:681
  37.7 5.6 %collective-permute-start.14 = (bf16[112,384]{1,0:T(8,128)(2,1)S(1)}, bf16[112,384]{1,0:T(8,128)(2,1)S(1)}, u32[]{:S(2)}, u32[]{:S(2)}) collective-permute-start(bf16[112,384]{1,0:T(8,128)(2,1)S(1)} %get-tuple-element.136), channel_id=1, source_target_pairs={{0,2},{1,3},{2,0},{3,1},{4,6},{5,7},{6,4},{7,5},{8,10},{9,11},{10,... | collective-permute-start | bytes 258056 | tf_op jit(solution)/shard_map/ppermute | solution.py:681
  75.6 6.0 %collective-permute-start.18 = (bf16[112,384]{1,0:T(8,128)(2,1)S(1)}, bf16[112,384]{1,0:T(8,128)(2,1)S(1)}, u32[]{:S(2)}, u32[]{:S(2)}) collective-permute-start(bf16[112,384]{1,0:T(8,128)(2,1)S(1)} %get-tuple-element.155), channel_id=1, source_target_pairs={{0,2},{1,3},{2,0},{3,1},{4,6},{5,7},{6,4},{7,5},{8,10},{9,11},{10,... | collective-permute-start | bytes 258056 | tf_op jit(solution)/shard_map/ppermute | solution.py:681
  77.3 9.6 %collective-permute-start.22 = (bf16[192,384]{1,0:T(8,128)(2,1)S(1)}, bf16[192,384]{1,0:T(8,128)(2,1)S(1)}, u32[]{:S(2)}, u32[]{:S(2)}) collective-permute-start(bf16[192,384]{1,0:T(8,128)(2,1)S(1)} %get-tuple-element.176), channel_id=1, source_target_pairs={{0,2},{1,3},{2,0},{3,1},{4,6},{5,7},{6,4},{7,5},{8,10},{9,11},{10,... | collective-permute-start | bytes 442376 | tf_op jit(solution)/shard_map/ppermute | solution.py:681
  87.1 5.8 %collective-permute-start.23 = (bf16[48,832]{1,0:T(8,128)(2,1)S(1)}, bf16[48,832]{1,0:T(8,128)(2,1)S(1)}, u32[]{:S(2)}, u32[]{:S(2)}) collective-permute-start(bf16[48,832]{1,0:T(8,128)(2,1)S(1)} %get-tuple-element.184), channel_id=1, source_target_pairs={{0,4},{4,0},{8,12},{12,8},{16,20},{20,16},{24,28},{28,24},{1,5},{5... | collective-permute-start | bytes 239624 | tf_op jit(solution)/shard_map/ppermute | solution.py:681
  87.4 5.5 %collective-permute-start.24 = (bf16[48,832]{1,0:T(8,128)(2,1)S(1)}, bf16[48,832]{1,0:T(8,128)(2,1)S(1)}, u32[]{:S(2)}, u32[]{:S(2)}) collective-permute-start(bf16[48,832]{1,0:T(8,128)(2,1)S(1)} %get-tuple-element.185), channel_id=1, source_target_pairs={{0,8},{4,12},{8,0},{12,4},{16,24},{20,28},{24,16},{28,20},{1,9},{5... | collective-permute-start | bytes 239624 | tf_op jit(solution)/shard_map/ppermute | solution.py:681
  87.7 5.1 %collective-permute-start.25 = (bf16[192,384]{1,0:T(8,128)(2,1)S(1)}, bf16[192,384]{1,0:T(8,128)(2,1)S(1)}, u32[]{:S(2)}, u32[]{:S(2)}) collective-permute-start(bf16[192,384]{1,0:T(8,128)(2,1)S(1)} %get-tuple-element.187), channel_id=1, source_target_pairs={{0,2},{1,3},{2,0},{3,1},{4,6},{5,7},{6,4},{7,5},{8,10},{9,11},{10,... | collective-permute-start | bytes 442376 | tf_op jit(solution)/shard_map/ppermute | solution.py:681
  89.5 19.9 %collective-permute-start.31 = (bf16[8,64,768]{2,1,0:T(8,128)(2,1)S(1)}, bf16[8,64,768]{2,1,0:T(8,128)(2,1)S(1)}, u32[]{:S(2)}, u32[]{:S(2)}) collective-permute-start(bf16[8,64,768]{2,1,0:T(8,128)(2,1)S(1)} %shard_map.281), channel_id=1, source_target_pairs={{0,2},{1,3},{2,0},{3,1},{4,6},{5,7},{6,4},{7,5},{8,10},{9,11},{10,... | collective-permute-start | bytes 2359304 | tf_op jit(solution)/shard_map/ppermute | solution.py:681
  93.0 7.6 %collective-permute-start.26 = (bf16[144,832]{1,0:T(8,128)(2,1)S(1)}, bf16[144,832]{1,0:T(8,128)(2,1)S(1)}, u32[]{:S(2)}, u32[]{:S(2)}) collective-permute-start(bf16[144,832]{1,0:T(8,128)(2,1)S(1)} %get-tuple-element.194), channel_id=1, source_target_pairs={{0,4},{4,0},{8,12},{12,8},{16,20},{20,16},{24,28},{28,24},{1,5},{5... | collective-permute-start | bytes 718856 | tf_op jit(solution)/shard_map/ppermute | solution.py:681
  93.9 6.6 %collective-permute-start.27 = (bf16[144,832]{1,0:T(8,128)(2,1)S(1)}, bf16[144,832]{1,0:T(8,128)(2,1)S(1)}, u32[]{:S(2)}, u32[]{:S(2)}) collective-permute-start(bf16[144,832]{1,0:T(8,128)(2,1)S(1)} %get-tuple-element.195), channel_id=1, source_target_pairs={{0,8},{4,12},{8,0},{12,4},{16,24},{20,28},{24,16},{28,20},{1,9},{5... | collective-permute-start | bytes 718856 | tf_op jit(solution)/shard_map/ppermute | solution.py:681
  100.7 7.5 %collective-permute-start.28 = (bf16[96,832]{1,0:T(8,128)(2,1)S(1)}, bf16[96,832]{1,0:T(8,128)(2,1)S(1)}, u32[]{:S(2)}, u32[]{:S(2)}) collective-permute-start(bf16[96,832]{1,0:T(8,128)(2,1)S(1)} %get-tuple-element.204), channel_id=1, source_target_pairs={{0,16},{4,20},{8,24},{12,28},{16,0},{20,4},{24,8},{28,12},{1,17},{... | collective-permute-start | bytes 479240 | tf_op jit(solution)/shard_map/ppermute | solution.py:681
  101.2 7.1 %collective-permute-start.29 = (bf16[96,832]{1,0:T(8,128)(2,1)S(1)}, bf16[96,832]{1,0:T(8,128)(2,1)S(1)}, u32[]{:S(2)}, u32[]{:S(2)}) collective-permute-start(bf16[96,832]{1,0:T(8,128)(2,1)S(1)} %get-tuple-element.205), channel_id=1, source_target_pairs={{0,8},{4,12},{8,0},{12,4},{16,24},{20,28},{24,16},{28,20},{1,9},{5... | collective-permute-start | bytes 479240 | tf_op jit(solution)/shard_map/ppermute | solution.py:681
  101.8 6.5 %collective-permute-start.30 = (bf16[96,832]{1,0:T(8,128)(2,1)S(1)}, bf16[96,832]{1,0:T(8,128)(2,1)S(1)}, u32[]{:S(2)}, u32[]{:S(2)}) collective-permute-start(bf16[96,832]{1,0:T(8,128)(2,1)S(1)} %get-tuple-element.206), channel_id=1, source_target_pairs={{0,4},{4,0},{8,12},{12,8},{16,20},{20,16},{24,28},{28,24},{1,5},{5... | collective-permute-start | bytes 479240 | tf_op jit(solution)/shard_map/ppermute | solution.py:681
  109.9 9.4 %collective-permute-start.32 = (bf16[96,832]{1,0:T(8,128)(2,1)S(1)}, bf16[96,832]{1,0:T(8,128)(2,1)S(1)}, u32[]{:S(2)}, u32[]{:S(2)}) collective-permute-start(bf16[96,832]{1,0:T(8,128)(2,1)S(1)} %shard_map.280.refs_0_), channel_id=1, source_target_pairs={{0,1},{1,0},{2,3},{3,2},{4,5},{5,4},{6,7},{7,6},{8,9},{9,8},{10,11... | collective-permute-start | bytes 479240 | tf_op jit(solution)/shard_map/ppermute | solution.py:681
  113.7 5.6 %collective-permute-start.34 = (bf16[96,832]{1,0:T(8,128)(2,1)S(1)}, bf16[96,832]{1,0:T(8,128)(2,1)S(1)}, u32[]{:S(2)}, u32[]{:S(2)}) collective-permute-start(bf16[96,832]{1,0:T(8,128)(2,1)S(1)} %collective-permute-done.33.refs_2_), channel_id=1, source_target_pairs={{0,1},{1,0},{2,3},{3,2},{4,5},{5,4},{6,7},{7,6},{8,9},{9,8},{10,11... | collective-permute-start | bytes 479240 | tf_op jit(solution)/shard_map/ppermute | solution.py:681
  (23 other events, 275.3 us)

commit v4 on v2

--- a/solution.py
+++ b/solution.py
@@ -57,10 +57,9 @@
 
 
 def kernel_call(
-    kernel, ins, outs, scratch=(), limit=48, smem=(), hbm_in=(), hbm_out=(), aliases=None, flops=1
+    kernel, ins, outs, scratch=(), limit=48, smem=(), hbm_in=(), hbm_out=(), flops=1
 ):
     kw = {
-        "input_output_aliases": aliases or {},
         "cost_estimate": pl.CostEstimate(flops=int(flops), bytes_accessed=0, transcendentals=0),
     }
     n_in, n_out, n_own = len(ins), len(outs), len(scratch)
@@ -489,10 +488,13 @@
         qkv_ref, probs_ref, xa_ref, unit_ref, wpad_ref, misc_ref, token_ref = refs[
             groups - 2 : groups + 5
         ]
-        gqkv, keep_ref, send_ref, gw_ref, gh, gs, gxs, turn = refs[groups + 6 :]
+        done_ref, gqkv, keep_ref, send_ref, gw_ref, gh, gs, gxs, turn = refs[groups + 5 :]
         images, _, features = unit_ref.shape
         seq = lax.axis_index("seq")
         gh[...] = jnp.zeros_like(gh)
+        for r in range(2):
+            rows = pl.ds(pl.multiple_of((seq ^ r) * ROWS, ROWS), ROWS)
+            gqkv[rows, :] = done_ref[rows, :]
         for j, ref in enumerate(gheads_refs):
             image_backward(ref, seq ^ (j + 2), qkv_ref, probs_ref, gqkv, gh, gs, heads_here)
         gx = mm_nt(gqkv[...], wpad_ref[...])
@@ -868,7 +870,6 @@
             pltpu.VMEM((misc_w, features), F32),
         ],
         limit=20,
-        aliases={groups + 5: 0},
         flops=1e10,
     )
     gx_core = swap(gx_send, "seq", 1)

time: 121 us -> 121 us (level)
  no operation moved by 1% of the time
where the time goes in v4:
time: 121 us
  starting transfers between devices  34.6 us (29%)
  Pallas kernels  34.6 us (29%)
  waiting for transfers between devices  27.5 us (23%)
  blocking collectives  21.9 us (18%)
  between operations  1.57 us (1%)
    ppermute x35, starting transfers between devices, swap(): lax.ppermute(a, axis, [(i, i ^ step) for i in range(lax.axis_size(axis))])  34.6 us
    ppermute x35, waiting for transfers between devices, swap(): lax.ppermute(a, axis, [(i, i ^ step) for i in range(lax.axis_size(axis))])  27.5 us
    pallas_call x19, Pallas kernels, kernel_call(): return list(call(*ins))  25.9 us
    all_to_all x1, blocking collectives, body(): lax.all_to_all(slots, ('dp', 'seq'), split_axis=0, concat_axis=0, tiled=T...  12.4 us
    all_to_all x1, blocking collectives, body(): lax.all_to_all(back, ('dp', 'seq'), split_axis=0, concat_axis=0, tiled=True)  9.49 us
    pallas_call x2, Pallas kernels, expert_gradients(): pl.pallas_call(expert_weights, grid=(count,), in_specs=[pl.BlockSpec((dev...  8.7 us
  transfers between devices with their start and end apart: 35, of which 13 were waited for; matrix products, arithmetic and copies ran while one was open for 0% of the time, Pallas kernels for 17%

profile of v4, /device:TPU:1, one launch (start us, length us, event | category | flops | bytes accessed | tf_op | source)
XLA Modules:
  0.0 121.2 jit_solution(13073173080675074518)
XLA Ops:
  0.7 2.1 %collective-permute-start.3 = (bf16[4,64,768]{2,1,0:T(8,128)(2,1)}, bf16[4,64,768]{2,1,0:T(8,128)(2,1)S(1)}, u32[]{:S(2)}, u32[]{:S(2)}) collective-permute-start(bf16[4,64,768]{2,1,0:T(8,128)(2,1)} %refs_3_.3), channel_id=1, source_target_pairs={{0,2},{1,3},{2,0},{3,1},{4,6},{5,7},{6,4},{7,5},{8,10},{9,11},{10,... | collective-permute-start | bytes 1179656 | tf_op jit(solution)/shard_map/ppermute | solution.py:683
  2.8 2.1 %shard_map.263.refs_3_ = bf16[96,1024]{1,0:T(8,128)(2,1)} custom-call(bf16[96,2304]{1,0:T(8,128)(2,1)} %refs_0_.3, bf16[32,96]{1,0:T(8,128)(2,1)} %bitcast.16, bf16[1,96]{1,0:T(2,128)(2,1)} %bitcast.17, bf16[1,96]{1,0:T(2,128)(2,1)} %bitcast.18, bf16[1,96]{1,0:T(2,128)(2,1)} %bitcast.19, bf16[1,96]{1,0:T(2,128)(2,1)} %bitcast.20, bf16[1,96]{1,0:T(2,128)(2,1)} %bitcast.21, ...), custom_call_target="tpu_custom_call" | custom-call | flops 1 | tf_op jit(solution)/shard_map/pallas_call | solution.py:113
  4.9 2.4 %collective-permute-start = (bf16[96,1024]{1,0:T(8,128)(2,1)}, bf16[96,1024]{1,0:T(8,128)(2,1)S(1)}, u32[]{:S(2)}, u32[]{:S(2)}) collective-permute-start(bf16[96,1024]{1,0:T(8,128)(2,1)} %shard_map.263.refs_3_), channel_id=1, source_target_pairs={{0,16},{4,20},{8,24},{12,28},{16,0},{20,4},{24,8},{28,12},{1,17},{... | collective-permute-start | bytes 589832 | tf_op jit(solution)/shard_map/ppermute | solution.py:683
  11.2 3.5 %collective-permute-done.4.refs_6_ = bf16[64,768]{1,0:T(8,128)(2,1)S(1)} collective-permute-done((bf16[64,768]{1,0:T(8,128)(2,1)S(1)}, bf16[64,768]{1,0:T(8,128)(2,1)S(1)}, u32[]{:S(2)}, u32[]{:S(2)}) %collective-permute-start.4) | collective-permute-done | bytes 98336 | tf_op jit(solution)/shard_map/ppermute | solution.py:683
  14.7 2.6 %collective-permute-start.7 = (bf16[4,64,768]{2,1,0:T(8,128)(2,1)}, bf16[4,64,768]{2,1,0:T(8,128)(2,1)S(1)}, u32[]{:S(2)}, u32[]{:S(2)}) collective-permute-start(bf16[4,64,768]{2,1,0:T(8,128)(2,1)} %refs_3_.3), channel_id=1, source_target_pairs={{0,1},{1,0},{2,3},{3,2},{4,5},{5,4},{6,7},{7,6},{8,9},{9,8},{10,11... | collective-permute-start | bytes 1179656 | tf_op jit(solution)/shard_map/ppermute | solution.py:683
  22.5 4.6 %collective-permute-done.9.refs_7_ = bf16[64,768]{1,0:T(8,128)(2,1)S(1)} collective-permute-done((bf16[64,768]{1,0:T(8,128)(2,1)S(1)}, bf16[64,768]{1,0:T(8,128)(2,1)S(1)}, u32[]{:S(2)}, u32[]{:S(2)}) %collective-permute-start.9) | collective-permute-done | bytes 98336 | tf_op jit(solution)/shard_map/ppermute | solution.py:683
  31.5 3.5 %shard_map.268 = (bf16[112,384]{1,0:T(8,128)(2,1)S(1)}, bf16[112,384]{1,0:T(8,128)(2,1)S(1)}, bf16[112,384]{1,0:T(8,128)(2,1)S(1)}, bf16[112,384]{1,0:T(8,128)(2...) custom-call(f32[4,208,768]{2,1,0:T(8,128)S(1)} %get-tuple-element.12, ...), custom_call_target="tpu_custom_call" | custom-call | flops 100000000 | tf_op jit(solution)/shard_map/pallas_call | solution.py:113
  35.0 2.5 %collective-permute-start.16 = (bf16[768,384]{1,0:T(8,128)(2,1)S(1)}, bf16[768,384]{1,0:T(8,128)(2,1)S(1)}, u32[]{:S(2)}, u32[]{:S(2)}) collective-permute-start(bf16[768,384]{1,0:T(8,128)(2,1)S(1)} %get-tuple-element.145.refs_13_), channel_id=1, source_target_pairs={{0,1},{1,0},{2,3},{3,2},{4,5},{5,4},{6,7},{7,6},{8,9},{9,8},{10,11... | collective-permute-start | bytes 1769480 | tf_op jit(solution)/shard_map/ppermute | solution.py:683
  37.8 1.9 %collective-permute-start.15 = (bf16[112,384]{1,0:T(8,128)(2,1)S(1)}, bf16[112,384]{1,0:T(8,128)(2,1)S(1)}, u32[]{:S(2)}, u32[]{:S(2)}) collective-permute-start(bf16[112,384]{1,0:T(8,128)(2,1)S(1)} %get-tuple-element.137), channel_id=1, source_target_pairs={{0,3},{1,2},{2,1},{3,0},{4,7},{5,6},{6,5},{7,4},{8,11},{9,10},{10,... | collective-permute-start | bytes 258056 | tf_op jit(solution)/shard_map/ppermute | solution.py:683
  41.3 2.4 %collective-permute-done.15.refs_3_ = bf16[112,384]{1,0:T(8,128)(2,1)S(1)} collective-permute-done((bf16[112,384]{1,0:T(8,128)(2,1)S(1)}, bf16[112,384]{1,0:T(8,128)(2,1)S(1)}, u32[]{:S(2)}, u32[]{:S(2)}) %collective-permute-start.15) | collective-permute-done | bytes 86048 | tf_op jit(solution)/shard_map/ppermute | solution.py:683
  43.7 1.6 %shard_map.269 = (bf16[32,2,768]{2,1,0:T(2,128)(2,1)S(1)}, f32[208,768]{1,0:T(8,128)S(1)}, bf16[208,768]{1,0:T(8,128)(2,1)S(1)}, f32[208,32]{1,0:T(8,128)S(1)}, ...) custom-call(bf16[112,384]{1,0:T(8,128)(2,1)S(1)} %get-tuple-element.134.refs_0_, ...), custom_call_target="tpu_custom_call" | custom-call | flops 5000000000 | tf_op jit(solution)/shard_map/pallas_call | solution.py:113
  45.4 12.4 %all_to_all.10.refs_0_.x_ref = bf16[32,2,768]{2,1,0:T(2,128)(2,1)S(1)} all-to-all(bf16[32,2,768]{2,1,0:T(2,128)(2,1)S(1)} %get-tuple-element.146), channel_id=1, replica_groups=mesh['dp'=8,'seq'=4] {'dp','seq'}, dimensions={0} | all-to-all | bytes 196608 | tf_op jit(solution)/shard_map/all_to_all | solution.py:774
  57.8 5.0 %shard_map.270 = (bf16[32,2,768]{2,1,0:T(2,128)(2,1)S(1)}, bf16[32,3072]{1,0:T(8,128)(2,1)S(1)}, bf16[32,3072]{1,0:T(8,128)(2,1)S(1)}, f32[1,3072]{1,0:T(1,128)}, f32[1,768]{1,0:T(1,128)}) custom-call(bf16[32,2,768]{2,1,0:T(2,128)(2,1)S(1)} %all_to_all.10.refs_0_.x_ref, bf16[1,768,3072]{2,1,0:T(8,128)(2,1)S(1)} %bitcast.13, bf16[1,3072]{1,0:T(2,128)(2,1)S(1)} %copy-done.6, ...), custom_call_target="tpu_custom_call" | custom-call | flops 5000000000 | tf_op jit(solution)/shard_map/pallas_call | solution.py:113
  62.9 9.5 %all_to_all.11.refs_0_ = bf16[32,2,768]{2,1,0:T(2,128)(2,1)S(1)} all-to-all(bf16[32,2,768]{2,1,0:T(2,128)(2,1)S(1)} %get-tuple-element.147), channel_id=1, replica_groups=mesh['dp'=8,'seq'=4] {'dp','seq'}, dimensions={0} | all-to-all | bytes 196608 | tf_op jit(solution)/shard_map/all_to_all | solution.py:789
  72.3 2.4 %shard_map.271 = (bf16[112,384]{1,0:T(8,128)(2,1)S(1)}, bf16[112,384]{1,0:T(8,128)(2,1)S(1)}, bf16[112,384]{1,0:T(8,128)(2,1)S(1)}, bf16[112,384]{1,0:T(8,128)(2...) custom-call(bf16[32,2,768]{2,1,0:T(2,128)(2,1)S(1)} %all_to_all.11.r, ...), custom_call_target="tpu_custom_call" | custom-call | flops 5000000000 | tf_op jit(solution)/shard_map/pallas_call | solution.py:113
  75.5 1.9 %collective-permute-start.18 = (bf16[112,384]{1,0:T(8,128)(2,1)S(1)}, bf16[112,384]{1,0:T(8,128)(2,1)S(1)}, u32[]{:S(2)}, u32[]{:S(2)}) collective-permute-start(bf16[112,384]{1,0:T(8,128)(2,1)S(1)} %get-tuple-element.155), channel_id=1, source_target_pairs={{0,3},{1,2},{2,1},{3,0},{4,7},{5,6},{6,5},{7,4},{8,11},{9,10},{10,... | collective-permute-start | bytes 258056 | tf_op jit(solution)/shard_map/ppermute | solution.py:683
  79.4 2.9 %collective-permute-done.18.refs_1_ = bf16[112,384]{1,0:T(8,128)(2,1)S(1)} collective-permute-done((bf16[112,384]{1,0:T(8,128)(2,1)S(1)}, bf16[112,384]{1,0:T(8,128)(2,1)S(1)}, u32[]{:S(2)}, u32[]{:S(2)}) %collective-permute-start.18) | collective-permute-done | bytes 86048 | tf_op jit(solution)/shard_map/ppermute | solution.py:683
  82.2 5.1 %shard_map.274 = (bf16[832,768]{1,0:T(8,128)(2,1)}, bf16[2,6,64,768]{3,2,1,0:T(8,128)(2,1)S(1)}, bf16[2,6,64,768]{3,2,1,0:T(8,128)(2,1)S(1)}, bf16[768,640]{1,0:T(8,128)(2,1)S(1)}) custom-call(bf16[112,384]{1,0:T(8,128)(2,1)S(1)} %collective-permute-done.17.refs_0_, bf16[112,384]{1,0:T(8,128)(2,1)S(1)} %collective-permute-done.18.refs_1_, ...), custom_call_target="tpu_custom_call" | custom-call | flops 10000000000 | tf_op jit(solution)/shard_map/pallas_call | solution.py:113
  88.3 1.9 %collective-permute-done.21.refs_1_ = bf16[2,6,64,768]{3,2,1,0:T(8,128)(2,1)S(1)} collective-permute-done((bf16[2,6,64,768]{3,2,1,0:T(8,128)(2,1)S(1)}, bf16[2,6,64,768]{3,2,1,0:T(8,128)(2,1)S(1)}, u32[]{:S(2)}, u32[]{:S(2)}) %collective-permute-start.21) | collective-permute-done | bytes 1179680 | tf_op jit(solution)/shard_map/ppermute | solution.py:683
  90.4 3.3 %shard_map.276 = (f32[1,768,3072]{2,1,0:T(8,128)}, f32[1,3072,768]{2,1,0:T(8,128)}) custom-call(bf16[32,2,768]{2,1,0:T(2,128)(2,1)S(1)} %all_to_all.10.refs_0_.x_ref, bf16[32,3072]{1,0:T(8,128)(2,1)S(1)} %get-tuple-element.188.hid_ref, bf16[32,3072]{1,0:T(8,128)(2,1)S(1)} %get-tuple-element.189.pre_ref), custom_call_target="tpu_custom_call" | custom-call | flops 99999997952 | tf_op jit(solution)/shard_map/pallas_call | solution.py:793
  95.6 5.4 %shard_map.278 = (f32[1,768,3072]{2,1,0:T(8,128)}, f32[1,3072,768]{2,1,0:T(8,128)}) custom-call(bf16[32,2,768]{2,1,0:T(2,128)(2,1)S(1)} %all_to_all.10.refs_0_.x_ref, bf16[32,3072]{1,0:T(8,128)(2,1)S(1)} %get-tuple-element.188.hid_ref, bf16[32,3072]{1,0:T(8,128)(2,1)S(1)} %get-tuple-element.189.pre_ref, ...), custom_call_target="tpu_custom_call", output_to_operand_aliasing={{0}: (3, {}), {1}: (4, {})} | custom-call | flops 1 | tf_op jit(solution)/shard_map/pallas_call | solution.py:793
  102.9 5.3 %collective-permute-done.28.refs_0_ = bf16[96,832]{1,0:T(8,128)(2,1)S(1)} collective-permute-done((bf16[96,832]{1,0:T(8,128)(2,1)S(1)}, bf16[96,832]{1,0:T(8,128)(2,1)S(1)}, u32[]{:S(2)}, u32[]{:S(2)}) %collective-permute-start.28) | collective-permute-done | bytes 159776 | tf_op jit(solution)/shard_map/ppermute | solution.py:683
  109.9 3.0 %collective-permute-start.33 = (bf16[96,832]{1,0:T(8,128)(2,1)S(1)}, bf16[96,832]{1,0:T(8,128)(2,1)S(1)}, u32[]{:S(2)}, u32[]{:S(2)}) collective-permute-start(bf16[96,832]{1,0:T(8,128)(2,1)S(1)} %shard_map.280.refs_0_), channel_id=1, source_target_pairs={{0,2},{1,3},{2,0},{3,1},{4,6},{5,7},{6,4},{7,5},{8,10},{9,11},{10,... | collective-permute-start | bytes 479240 | tf_op jit(solution)/shard_map/ppermute | solution.py:683
  115.7 2.8 %collective-permute-start.34 = (bf16[96,832]{1,0:T(8,128)(2,1)S(1)}, bf16[96,832]{1,0:T(8,128)(2,1)S(1)}, u32[]{:S(2)}, u32[]{:S(2)}) collective-permute-start(bf16[96,832]{1,0:T(8,128)(2,1)S(1)} %collective-permute-done.33.refs_2_), channel_id=1, source_target_pairs={{0,1},{1,0},{2,3},{3,2},{4,5},{5,4},{6,7},{7,6},{8,9},{9,8},{10,11... | collective-permute-start | bytes 479240 | tf_op jit(solution)/shard_map/ppermute | solution.py:683
  (95 shorter events, 29.4 us)
Async XLA Ops:
  0.7 16.7 %collective-permute-start.3 = (bf16[4,64,768]{2,1,0:T(8,128)(2,1)}, bf16[4,64,768]{2,1,0:T(8,128)(2,1)S(1)}, u32[]{:S(2)}, u32[]{:S(2)}) collective-permute-start(bf16[4,64,768]{2,1,0:T(8,128)(2,1)} %refs_3_.3), channel_id=1, source_target_pairs={{0,2},{1,3},{2,0},{3,1},{4,6},{5,7},{6,4},{7,5},{8,10},{9,11},{10,... | collective-permute-start | bytes 1179656 | tf_op jit(solution)/shard_map/ppermute | solution.py:683
  4.9 12.4 %collective-permute-start = (bf16[96,1024]{1,0:T(8,128)(2,1)}, bf16[96,1024]{1,0:T(8,128)(2,1)S(1)}, u32[]{:S(2)}, u32[]{:S(2)}) collective-permute-start(bf16[96,1024]{1,0:T(8,128)(2,1)} %shard_map.263.refs_3_), channel_id=1, source_target_pairs={{0,16},{4,20},{8,24},{12,28},{16,0},{20,4},{24,8},{28,12},{1,17},{... | collective-permute-start | bytes 589832 | tf_op jit(solution)/shard_map/ppermute | solution.py:683
  7.3 10.1 %collective-permute-start.1 = (bf16[96,1024]{1,0:T(8,128)(2,1)}, bf16[96,1024]{1,0:T(8,128)(2,1)S(1)}, u32[]{:S(2)}, u32[]{:S(2)}) collective-permute-start(bf16[96,1024]{1,0:T(8,128)(2,1)} %shard_map.263.refs_3_), channel_id=1, source_target_pairs={{0,8},{4,12},{8,0},{12,4},{16,24},{20,28},{24,16},{28,20},{1,9},{5... | collective-permute-start | bytes 589832 | tf_op jit(solution)/shard_map/ppermute | solution.py:683
  8.6 8.8 %collective-permute-start.2 = (bf16[96,1024]{1,0:T(8,128)(2,1)}, bf16[96,1024]{1,0:T(8,128)(2,1)S(1)}, u32[]{:S(2)}, u32[]{:S(2)}) collective-permute-start(bf16[96,1024]{1,0:T(8,128)(2,1)} %shard_map.263.refs_3_), channel_id=1, source_target_pairs={{0,4},{4,0},{8,12},{12,8},{16,20},{20,16},{24,28},{28,24},{1,5},{5... | collective-permute-start | bytes 589832 | tf_op jit(solution)/shard_map/ppermute | solution.py:683
  14.7 12.3 %collective-permute-start.7 = (bf16[4,64,768]{2,1,0:T(8,128)(2,1)}, bf16[4,64,768]{2,1,0:T(8,128)(2,1)S(1)}, u32[]{:S(2)}, u32[]{:S(2)}) collective-permute-start(bf16[4,64,768]{2,1,0:T(8,128)(2,1)} %refs_3_.3), channel_id=1, source_target_pairs={{0,1},{1,0},{2,3},{3,2},{4,5},{5,4},{6,7},{7,6},{8,9},{9,8},{10,11... | collective-permute-start | bytes 1179656 | tf_op jit(solution)/shard_map/ppermute | solution.py:683
  17.4 12.4 %collective-permute-start.10 = (bf16[4,64,768]{2,1,0:T(8,128)(2,1)S(1)}, bf16[4,64,768]{2,1,0:T(8,128)(2,1)S(1)}, u32[]{:S(2)}, u32[]{:S(2)}) collective-permute-start(bf16[4,64,768]{2,1,0:T(8,128)(2,1)S(1)} %collective-permute-done.3.refs_2_), channel_id=1, source_target_pairs={{0,1},{1,0},{2,3},{3,2},{4,5},{5,4},{6,7},{7,6},{8,9},{9,8},{10,11... | collective-permute-start | bytes 1179656 | tf_op jit(solution)/shard_map/ppermute | solution.py:683
  18.0 9.0 %collective-permute-start.5 = (bf16[144,1024]{1,0:T(8,128)(2,1)S(1)}, bf16[144,1024]{1,0:T(8,128)(2,1)S(1)}, u32[]{:S(2)}, u32[]{:S(2)}) collective-permute-start(bf16[144,1024]{1,0:T(8,128)(2,1)S(1)} %get-tuple-element.123), channel_id=1, source_target_pairs={{0,4},{4,0},{8,12},{12,8},{16,20},{20,16},{24,28},{28,24},{1,5},{5... | collective-permute-start | bytes 884744 | tf_op jit(solution)/shard_map/ppermute | solution.py:683
  19.3 8.3 %collective-permute-start.6 = (bf16[144,1024]{1,0:T(8,128)(2,1)S(1)}, bf16[144,1024]{1,0:T(8,128)(2,1)S(1)}, u32[]{:S(2)}, u32[]{:S(2)}) collective-permute-start(bf16[144,1024]{1,0:T(8,128)(2,1)S(1)} %get-tuple-element.124), channel_id=1, source_target_pairs={{0,8},{4,12},{8,0},{12,4},{16,24},{20,28},{24,16},{28,20},{1,9},{5... | collective-permute-start | bytes 884744 | tf_op jit(solution)/shard_map/ppermute | solution.py:683
  22.0 5.1 %collective-permute-start.9 = (bf16[64,768]{1,0:T(8,128)(2,1)S(1)}, bf16[64,768]{1,0:T(8,128)(2,1)S(1)}, u32[]{:S(2)}, u32[]{:S(2)}) collective-permute-start(bf16[64,768]{1,0:T(8,128)(2,1)S(1)} %get-tuple-element.126), channel_id=1, source_target_pairs={{0,3},{1,2},{2,1},{3,0},{4,7},{5,6},{6,5},{7,4},{8,11},{9,10},{10,... | collective-permute-start | bytes 294920 | tf_op jit(solution)/shard_map/ppermute | solution.py:683
  35.0 8.7 %collective-permute-start.16 = (bf16[768,384]{1,0:T(8,128)(2,1)S(1)}, bf16[768,384]{1,0:T(8,128)(2,1)S(1)}, u32[]{:S(2)}, u32[]{:S(2)}) collective-permute-start(bf16[768,384]{1,0:T(8,128)(2,1)S(1)} %get-tuple-element.145.refs_13_), channel_id=1, source_target_pairs={{0,1},{1,0},{2,3},{3,2},{4,5},{5,4},{6,7},{7,6},{8,9},{9,8},{10,11... | collective-permute-start | bytes 1769480 | tf_op jit(solution)/shard_map/ppermute | solution.py:683
  37.8 5.9 %collective-permute-start.15 = (bf16[112,384]{1,0:T(8,128)(2,1)S(1)}, bf16[112,384]{1,0:T(8,128)(2,1)S(1)}, u32[]{:S(2)}, u32[]{:S(2)}) collective-permute-start(bf16[112,384]{1,0:T(8,128)(2,1)S(1)} %get-tuple-element.137), channel_id=1, source_target_pairs={{0,3},{1,2},{2,1},{3,0},{4,7},{5,6},{6,5},{7,4},{8,11},{9,10},{10,... | collective-permute-start | bytes 258056 | tf_op jit(solution)/shard_map/ppermute | solution.py:683
  75.5 6.8 %collective-permute-start.18 = (bf16[112,384]{1,0:T(8,128)(2,1)S(1)}, bf16[112,384]{1,0:T(8,128)(2,1)S(1)}, u32[]{:S(2)}, u32[]{:S(2)}) collective-permute-start(bf16[112,384]{1,0:T(8,128)(2,1)S(1)} %get-tuple-element.155), channel_id=1, source_target_pairs={{0,3},{1,2},{2,1},{3,0},{4,7},{5,6},{6,5},{7,4},{8,11},{9,10},{10,... | collective-permute-start | bytes 258056 | tf_op jit(solution)/shard_map/ppermute | solution.py:683
  77.6 9.8 %collective-permute-start.22 = (bf16[192,384]{1,0:T(8,128)(2,1)S(1)}, bf16[192,384]{1,0:T(8,128)(2,1)S(1)}, u32[]{:S(2)}, u32[]{:S(2)}) collective-permute-start(bf16[192,384]{1,0:T(8,128)(2,1)S(1)} %get-tuple-element.176), channel_id=1, source_target_pairs={{0,2},{1,3},{2,0},{3,1},{4,6},{5,7},{6,4},{7,5},{8,10},{9,11},{10,... | collective-permute-start | bytes 442376 | tf_op jit(solution)/shard_map/ppermute | solution.py:683
  87.5 6.2 %collective-permute-start.23 = (bf16[48,832]{1,0:T(8,128)(2,1)S(1)}, bf16[48,832]{1,0:T(8,128)(2,1)S(1)}, u32[]{:S(2)}, u32[]{:S(2)}) collective-permute-start(bf16[48,832]{1,0:T(8,128)(2,1)S(1)} %get-tuple-element.184), channel_id=1, source_target_pairs={{0,4},{4,0},{8,12},{12,8},{16,20},{20,16},{24,28},{28,24},{1,5},{5... | collective-permute-start | bytes 239624 | tf_op jit(solution)/shard_map/ppermute | solution.py:683
  87.8 5.8 %collective-permute-start.24 = (bf16[48,832]{1,0:T(8,128)(2,1)S(1)}, bf16[48,832]{1,0:T(8,128)(2,1)S(1)}, u32[]{:S(2)}, u32[]{:S(2)}) collective-permute-start(bf16[48,832]{1,0:T(8,128)(2,1)S(1)} %get-tuple-element.185), channel_id=1, source_target_pairs={{0,8},{4,12},{8,0},{12,4},{16,24},{20,28},{24,16},{28,20},{1,9},{5... | collective-permute-start | bytes 239624 | tf_op jit(solution)/shard_map/ppermute | solution.py:683
  88.2 5.5 %collective-permute-start.25 = (bf16[192,384]{1,0:T(8,128)(2,1)S(1)}, bf16[192,384]{1,0:T(8,128)(2,1)S(1)}, u32[]{:S(2)}, u32[]{:S(2)}) collective-permute-start(bf16[192,384]{1,0:T(8,128)(2,1)S(1)} %get-tuple-element.187), channel_id=1, source_target_pairs={{0,2},{1,3},{2,0},{3,1},{4,6},{5,7},{6,4},{7,5},{8,10},{9,11},{10,... | collective-permute-start | bytes 442376 | tf_op jit(solution)/shard_map/ppermute | solution.py:683
  90.3 19.6 %collective-permute-start.31 = (bf16[8,64,768]{2,1,0:T(8,128)(2,1)S(1)}, bf16[8,64,768]{2,1,0:T(8,128)(2,1)S(1)}, u32[]{:S(2)}, u32[]{:S(2)}) collective-permute-start(bf16[8,64,768]{2,1,0:T(8,128)(2,1)S(1)} %shard_map.281), channel_id=1, source_target_pairs={{0,2},{1,3},{2,0},{3,1},{4,6},{5,7},{6,4},{7,5},{8,10},{9,11},{10,... | collective-permute-start | bytes 2359304 | tf_op jit(solution)/shard_map/ppermute | solution.py:683
  93.8 7.2 %collective-permute-start.26 = (bf16[144,832]{1,0:T(8,128)(2,1)S(1)}, bf16[144,832]{1,0:T(8,128)(2,1)S(1)}, u32[]{:S(2)}, u32[]{:S(2)}) collective-permute-start(bf16[144,832]{1,0:T(8,128)(2,1)S(1)} %get-tuple-element.194), channel_id=1, source_target_pairs={{0,4},{4,0},{8,12},{12,8},{16,20},{20,16},{24,28},{28,24},{1,5},{5... | collective-permute-start | bytes 718856 | tf_op jit(solution)/shard_map/ppermute | solution.py:683
  94.4 6.5 %collective-permute-start.27 = (bf16[144,832]{1,0:T(8,128)(2,1)S(1)}, bf16[144,832]{1,0:T(8,128)(2,1)S(1)}, u32[]{:S(2)}, u32[]{:S(2)}) collective-permute-start(bf16[144,832]{1,0:T(8,128)(2,1)S(1)} %get-tuple-element.195), channel_id=1, source_target_pairs={{0,8},{4,12},{8,0},{12,4},{16,24},{20,28},{24,16},{28,20},{1,9},{5... | collective-permute-start | bytes 718856 | tf_op jit(solution)/shard_map/ppermute | solution.py:683
  101.2 7.1 %collective-permute-start.28 = (bf16[96,832]{1,0:T(8,128)(2,1)S(1)}, bf16[96,832]{1,0:T(8,128)(2,1)S(1)}, u32[]{:S(2)}, u32[]{:S(2)}) collective-permute-start(bf16[96,832]{1,0:T(8,128)(2,1)S(1)} %get-tuple-element.204), channel_id=1, source_target_pairs={{0,16},{4,20},{8,24},{12,28},{16,0},{20,4},{24,8},{28,12},{1,17},{... | collective-permute-start | bytes 479240 | tf_op jit(solution)/shard_map/ppermute | solution.py:683
  101.7 6.5 %collective-permute-start.29 = (bf16[96,832]{1,0:T(8,128)(2,1)S(1)}, bf16[96,832]{1,0:T(8,128)(2,1)S(1)}, u32[]{:S(2)}, u32[]{:S(2)}) collective-permute-start(bf16[96,832]{1,0:T(8,128)(2,1)S(1)} %get-tuple-element.205), channel_id=1, source_target_pairs={{0,8},{4,12},{8,0},{12,4},{16,24},{20,28},{24,16},{28,20},{1,9},{5... | collective-permute-start | bytes 479240 | tf_op jit(solution)/shard_map/ppermute | solution.py:683
  102.3 5.9 %collective-permute-start.30 = (bf16[96,832]{1,0:T(8,128)(2,1)S(1)}, bf16[96,832]{1,0:T(8,128)(2,1)S(1)}, u32[]{:S(2)}, u32[]{:S(2)}) collective-permute-start(bf16[96,832]{1,0:T(8,128)(2,1)S(1)} %get-tuple-element.206), channel_id=1, source_target_pairs={{0,4},{4,0},{8,12},{12,8},{16,20},{20,16},{24,28},{28,24},{1,5},{5... | collective-permute-start | bytes 479240 | tf_op jit(solution)/shard_map/ppermute | solution.py:683
  109.9 5.8 %collective-permute-start.33 = (bf16[96,832]{1,0:T(8,128)(2,1)S(1)}, bf16[96,832]{1,0:T(8,128)(2,1)S(1)}, u32[]{:S(2)}, u32[]{:S(2)}) collective-permute-start(bf16[96,832]{1,0:T(8,128)(2,1)S(1)} %shard_map.280.refs_0_), channel_id=1, source_target_pairs={{0,2},{1,3},{2,0},{3,1},{4,6},{5,7},{6,4},{7,5},{8,10},{9,11},{10,... | collective-permute-start | bytes 479240 | tf_op jit(solution)/shard_map/ppermute | solution.py:683
  112.9 7.1 %collective-permute-start.32 = (bf16[96,832]{1,0:T(8,128)(2,1)S(1)}, bf16[96,832]{1,0:T(8,128)(2,1)S(1)}, u32[]{:S(2)}, u32[]{:S(2)}) collective-permute-start(bf16[96,832]{1,0:T(8,128)(2,1)S(1)} %shard_map.280.refs_0_), channel_id=1, source_target_pairs={{0,1},{1,0},{2,3},{3,2},{4,5},{5,4},{6,7},{7,6},{8,9},{9,8},{10,11... | collective-permute-start | bytes 479240 | tf_op jit(solution)/shard_map/ppermute | solution.py:683
  (23 other events, 269.9 us)
